TPU v7x, 128 devices: a whole 4x4x4 slice. The times are simulated.
128 devices in a mesh: dp: 16 (over x_hi, y, core), mp: 8 (over x_lo, z).
Axes of the slice: x: 4 (x_hi: 2, x_lo: 2; x = x_hi * 2 + x_lo), y: 4, z: 4, core: 2. Of those that a mesh axis runs over, the one named last changes fastest.
Arguments:
- tokens: bfloat16 [16384, 8192], P('dp', 'mp'), may hold values from -6 to 6
- w_query: bfloat16 [8192, 8192], P(None, 'mp'), may hold values from -0.0625 to 0.0625
- w_value: bfloat16 [8192, 1024], P(None, 'mp'), may hold values from -0.0625 to 0.0625
- a_both: bfloat16 [80, 8192, 128], P('dp', 'mp'), may hold values from -0.0625 to 0.0625
- b_query: bfloat16 [80, 64, 8192], P('dp', None, 'mp'), may hold values from -0.75 to 0.75
- b_value: bfloat16 [80, 64, 1024], P('dp', None, 'mp'), may hold values from -0.75 to 0.75
- request_adapter: int32 [16, 2], P('dp'), may hold values from 0 to 79
- adapter_slot: int32 [80], replicated, may hold values from 0 to 79, each once
- block_request: int32 [16, 8], P('dp'), may hold values from 0 to 1, never falling along the last dimension, each value on 1 to 7 neighbouring positions
Outputs:
- query_out: bfloat16 [16384, 8192], P('dp', 'mp')
- value_out: bfloat16 [16384, 1024], P('dp', 'mp')
Inputs may be any that keep to these rules, and one draw needn't show every extreme that they name: `request_adapter`: adapter ids; several requests may name one adapter. `adapter_slot`: a permutation; the adapter stored at row s is owned by index s // 5 of dp. `block_request`: within a group never falling, every request has one block or more.
All inputs are finite; a program needn't handle non-finite values.
Results may differ from a plain program's by a relative error of at most 0.004.
Values may be sent and summed in bfloat16 or wider, within the bound.
No kernel may reach another device: no remote copies, remote signals or barrier semaphores. Data moves between devices by JAX's collectives and lax.ppermute only.
A program may use at most 192 MiB of HBM per device.

v0:
```python
import jax
import jax.numpy as jnp
from jax import lax
from jax.sharding import PartitionSpec as P

SEG = 128


def widened(mask, ndim):
    return mask.reshape(mask.shape + (1,) * ndim)


def on_device(
    tokens, w_query, w_value, a_both, b_query, b_value, request_adapter, adapter_slot, block_request
):
    rows = tokens.shape[0]
    wanted = request_adapter.shape[1]
    rank = b_query.shape[1]
    every = adapter_slot.shape[0]
    ids = request_adapter[0]
    slots = jnp.sum(
        jnp.where(
            ids[:, None] == jnp.arange(every, dtype=jnp.int32)[None, :], adapter_slot[None, :], 0
        ),
        axis=1,
    )
    row_request = jnp.repeat(block_request[0], SEG, total_repeat_length=rows)
    member = (row_request[:, None] == jnp.arange(wanted, dtype=jnp.int32)[None, :]).astype(
        jnp.float32
    )
    empty = (
        jnp.zeros((wanted,) + a_both.shape[1:], jnp.bfloat16),
        jnp.zeros((wanted,) + b_query.shape[1:], jnp.bfloat16),
        jnp.zeros((wanted,) + b_value.shape[1:], jnp.bfloat16),
    )
    piece = (
        lax.all_gather(a_both, "dp", axis=0, tiled=True),
        lax.all_gather(b_query, "dp", axis=0, tiled=True),
        lax.all_gather(b_value, "dp", axis=0, tiled=True),
    )
    start = jnp.int32(0)
    count = piece[0].shape[0]
    offset = jnp.clip(slots, 0, count - 1)
    inside = (slots >= start) & (slots < start + count)
    chosen_a, chosen_query, chosen_value = tuple(
        (
            jnp.where(widened(inside, held.ndim - 1), jnp.take(part, offset, axis=0), held)
            for held, part in zip(empty, piece)
        )
    )
    piece = lax.all_gather(tokens, "mp", axis=1, tiled=True)
    base_query = jnp.dot(piece, w_query, preferred_element_type=jnp.float32)
    base_value = jnp.dot(piece, w_value, preferred_element_type=jnp.float32)
    partial_shrink = jnp.zeros((rows, 2 * rank), jnp.float32)
    for request in range(wanted):
        partial_shrink = partial_shrink + member[:, request : request + 1] * jnp.dot(
            tokens, chosen_a[request], preferred_element_type=jnp.float32
        )
    shrink = lax.psum(partial_shrink, "mp").astype(jnp.bfloat16)
    for request in range(wanted):
        base_query = base_query + member[:, request : request + 1] * jnp.dot(
            shrink[:, :rank], chosen_query[request], preferred_element_type=jnp.float32
        )
        base_value = base_value + member[:, request : request + 1] * jnp.dot(
            shrink[:, rank:], chosen_value[request], preferred_element_type=jnp.float32
        )
    return (base_query.astype(jnp.bfloat16), base_value.astype(jnp.bfloat16))


def solution(mesh):
    placed = (
        P("dp", "mp"),
        P(None, "mp"),
        P(None, "mp"),
        P("dp", "mp", None),
        P("dp", None, "mp"),
        P("dp", None, "mp"),
        P("dp", None),
        P(),
        P("dp", None),
    )
    return jax.shard_map(
        on_device,
        mesh=mesh,
        in_specs=placed,
        out_specs=(P("dp", "mp"), P("dp", "mp")),
        check_vma=False,
    )
```

profile of v0, /device:TPU:0, one launch (start us, length us, event | category | flops | bytes accessed | tf_op | source)
XLA Modules:
  0.0 526.7 jit_solution(5419647573917939917)
XLA Ops:
  7.2 0.0 copy-start
  7.2 0.0 all-gather.11.cloned.1.call-start
  7.2 0.7 all-gather.11.cloned.1.call-update
  7.9 0.0 all-gather.9.cloned.1.call-start
  8.0 0.7 all-gather.9.cloned.1.call-update
  8.7 0.0 all-gather.5.cloned.1.call-start
  8.7 0.7 all-gather.5.cloned.1.call-update
  9.4 0.0 all-gather.7.cloned.1.call-start
  9.4 0.5 all-gather.7.cloned.1.call-update
  10.0 0.9 fusion.13
  10.9 1.6 fusion.16
  12.5 4.4 compare_select_fusion.1
  16.9 0.7 select_select_fusion.3
  17.6 40.7 %all-gather.11.cloned.1.call-done = bf16[80,64,128]{2,1,0:T(8,128)(2,1)} async-done(((bf16[5,64,128]{2,1,0:T(8,128)(2,1)}), bf16[80,64,128]{2,1,0:T(8,128)(2,1)}) %all-gather.11.cloned.1.call-update) | async-done | bytes 1310736 | tf_op jit(solution)/shard_map/all_gather | solution.py:39
  58.4 1.9 gather_fusion.2
  60.2 0.1 select_select_fusion.2
  60.3 81.1 %all-gather.9.cloned.1.call-done = bf16[80,64,1024]{2,1,0:T(8,128)(2,1)} async-done(((bf16[5,64,1024]{2,1,0:T(8,128)(2,1)}), bf16[80,64,1024]{2,1,0:T(8,128)(2,1)}) %all-gather.9.cloned.1.call-update) | async-done | bytes 10485776 | tf_op jit(solution)/shard_map/all_gather | solution.py:38
  141.4 4.5 gather_fusion.1
  146.0 0.1 select_select_fusion.1
  146.1 165.6 %all-gather.5.cloned.1.call-done = bf16[1024,8192]{1,0:T(8,128)(2,1)} async-done(((bf16[1024,1024]{1,0:T(8,128)(2,1)}), bf16[1024,8192]{1,0:T(8,128)(2,1)}) %all-gather.5.cloned.1.call-update) | async-done | bytes 16777232 | tf_op jit(solution)/shard_map/all_gather | solution.py:51
  311.7 8.1 %fusion.17 = f32[1024,128]{1,0:T(8,128)S(1)} fusion(bf16[1024,8192]{1,0:T(8,128)(2,1)} %all-gather.5.cloned.1.call-done, bf16[8192,128]{1,0:T(8,128)(2,1)S(1)} %copy-done), kind=kOutput, calls=%fused_computation.52 | convolution fusion | flops 2147483648 | bytes 19398656 | tf_op jit(solution)/shard_map/dot_general | solution.py:53
  319.8 121.2 %all-gather.7.cloned.1.call-done = bf16[80,1024,128]{2,1,0:T(8,128)(2,1)} async-done(((bf16[5,1024,128]{2,1,0:T(8,128)(2,1)}), bf16[80,1024,128]{2,1,0:T(8,128)(2,1)}) %all-gather.7.cloned.1.call-update) | async-done | bytes 20971536 | tf_op jit(solution)/shard_map/all_gather | solution.py:37
  441.0 7.6 %gather_fusion = bf16[2,1024,128]{2,1,0:T(8,128)(2,1)S(1)} fusion(bf16[80,1024,128]{2,1,0:T(8,128)(2,1)} %all-gather.7.cloned.1.call-done, s32[1024]{0:T(1024)S(1)} %pad_clamp_fusion), kind=kCustom, calls=%fused_computation | custom fusion | bytes 1048584 | tf_op jit(solution)/shard_map/jit(_take)/gather | solution.py:47
  448.6 0.1 select_select_fusion
  448.8 2.4 convolution_multiply_fusion.3
  451.2 0.8 fusion.1
  452.1 39.2 %all-reduce.1 = bf16[1024,128]{0,1:T(8,128)(2,1)S(1)} all-reduce(f32[1024,128]{0,1:T(8,128)S(1)} %fusion.1), channel_id=1, replica_groups=mesh['dp'=16,'mp'=8] {'mp'}, use_global_device_ids=true, to_apply=%region_1.2 | all-reduce | flops 131072 | bytes 786432 | tf_op jit(solution)/shard_map/psum | solution.py:59
  491.2 0.7 fusion.6
  492.0 0.7 fusion.5
  492.7 0.3 convolution_multiply_fusion
  493.0 1.0 fusion.4
  494.0 26.2 %add_convert_fusion = bf16[1024,1024]{1,0:T(8,128)(2,1)} fusion(f32[1024,1024]{1,0:T(8,128)S(1)} %fusion.5, f32[1024,1024]{1,0:T(8,128)S(1)} %fusion.6, bf16[1024,8192]{1,0:T(8,128)(2,1)} %all-gather.5.cloned.1.call-done, bf16[8192,1024]{1,0:T(8,128)(2,1)} %param.12, f32[1024]{0:T(1024)S(1)} %bitcast.54, f32[1024]{0:T(1024)S(1)} %bitcast.57), kind=kOutput, calls=%fused_computation.3 | convolution fusion | flops 17185112064 | bytes 44048384 | tf_op jit(solution)/shard_map/dot_general | solution.py:52
  (13 shorter events, 0.1 us)
Async XLA Ops:
  7.2 304.5 %copy-start = (bf16[8192,128]{1,0:T(8,128)(2,1)S(1)}, bf16[8192,128]{1,0:T(8,128)(2,1)}, u32[]{:S(2)}) copy-start(bf16[8192,128]{1,0:T(8,128)(2,1)} %param.13) | copy-start | bytes 6291460
  7.2 51.2 %all-gather.11.cloned.1.call-start = ((), (), s32[]{:S(2)}) async-start(), calls=%async_computation.3 | async-start | bytes 1392640 | tf_op jit(solution)/shard_map/all_gather | solution.py:39
  7.9 133.5 %all-gather.9.cloned.1.call-start = ((), (), s32[]{:S(2)}) async-start(), calls=%async_computation.2 | async-start | bytes 11141120 | tf_op jit(solution)/shard_map/all_gather | solution.py:38
  8.7 303.0 %all-gather.5.cloned.1.call-start = ((), (), s32[]{:S(2)}) async-start(), calls=%async_computation | async-start | bytes 18874368 | tf_op jit(solution)/shard_map/all_gather | solution.py:51
  9.4 431.6 %all-gather.7.cloned.1.call-start = ((), (), s32[]{:S(2)}) async-start(), calls=%async_computation.1 | async-start | bytes 22282240 | tf_op jit(solution)/shard_map/all_gather | solution.py:37
  319.8 131.4 %copy-start.2 = (bf16[1024,1024]{1,0:T(8,128)(2,1)S(1)}, bf16[1024,1024]{1,0:T(8,128)(2,1)}, u32[]{:S(2)}) copy-start(bf16[1024,1024]{1,0:T(8,128)(2,1)} %param.11) | copy-start | bytes 6291460
  494.0 26.2 %copy-start.1 = (bf16[8192,128]{1,0:T(8,128)(2,1)S(1)}, bf16[8192,128]{1,0:T(8,128)(2,1)}, u32[]{:S(2)}) copy-start(bf16[8192,128]{1,0:T(8,128)(2,1)} %param.13) | copy-start | bytes 6291460
Sparse Core Ops, SparseCore 0:
  10.5 47.8 all-gather.10
  60.8 80.5 all-gather.8
  143.1 168.5 all-gather.4
  314.0 126.9 all-gather.6
where the time goes:
time: 527 us
  waiting for transfers between devices  411 us (78%)
  matrix products  40.3 us (8%)
  blocking collectives  39.2 us (7%)
  local copies, waits for them, and re-layouts  15.7 us (3%)
  between operations  13.9 us (3%)
  other arithmetic  6.28 us (1%)
    all_gather x1, waiting for transfers between devices, on_device(): piece = lax.all_gather(tokens, 'mp', axis=1, tiled=True)  166 us
    all_gather x1, waiting for transfers between devices, on_device(): lax.all_gather(a_both, 'dp', axis=0, tiled=True)  121 us
    all_gather x1, waiting for transfers between devices, on_device(): lax.all_gather(b_query, 'dp', axis=0, tiled=True)  81.1 us
    all_gather x1, waiting for transfers between devices, on_device(): lax.all_gather(b_value, 'dp', axis=0, tiled=True)  40.7 us
    psum x1, blocking collectives, on_device(): shrink = lax.psum(partial_shrink, 'mp').astype(jnp.bfloat16)  39.2 us
    dot_general x1, matrix products, on_device(): base_query = jnp.dot(piece, w_query, preferred_element_type=jnp.float32)  26.2 us
    gather x3, local copies, waits for them, and re-layouts, on_device(): jnp.take(part, offset, axis=0)  14 us
  transfers between devices with their start and end apart: 4, of which 4 were waited for; matrix products, arithmetic and copies ran while one was open for 4% of the time, Pallas kernels for 0%

commit v1 on v0

v1 whole, which is shorter than its diff:
```python
import functools

import jax
import jax.numpy as jnp
from jax import lax
from jax.experimental import pallas as pl
from jax.experimental.pallas import tpu as pltpu
from jax.sharding import PartitionSpec as P

SEG = 128
NX, NZ = 2, 4
TILE = 256
EARLY = 384


def pairs(move):
    found = []
    for h in range(2):
        for y in range(4):
            for c in range(2):
                for x in range(NX):
                    for z in range(NZ):
                        th, ty, tc, tx, tz = move(h, y, c, x, z, 1 - 2 * c)
                        there = ((th * 4 + ty % 4) * 2 + tc) * NX * NZ + tx * NZ + tz % NZ
                        found.append((((h * 4 + y) * 2 + c) * NX * NZ + x * NZ + z, there))
    return found


def to_z(v, step):
    return lax.ppermute(
        v, ("dp", "mp"), pairs(lambda h, y, c, x, z, s: (h, y, c, x, z + s * step))
    )


def to_y(v, step):
    return lax.ppermute(
        v, ("dp", "mp"), pairs(lambda h, y, c, x, z, s: (h, y + s * step, c, x, z))
    )


def to_x(v):
    return lax.ppermute(v, ("dp", "mp"), pairs(lambda h, y, c, x, z, s: (h, y, c, 1 - x, z)))


def to_core(v):
    return lax.ppermute(v, ("dp", "mp"), pairs(lambda h, y, c, x, z, s: (h, y, 1 - c, x, z)))


def to_far(v):
    return lax.ppermute(v, ("dp", "mp"), pairs(lambda h, y, c, x, z, s: (1 - h, y, c, x, z)))


def after(v, *earlier):
    return lax.optimization_barrier((v,) + earlier)[0]


def wanted_slots(request_adapter, adapter_slot):
    every = adapter_slot.shape[0]
    ids = request_adapter[0]
    slots = jnp.sum(
        jnp.where(
            ids[:, None] == jnp.arange(every, dtype=jnp.int32)[None, :], adapter_slot[None, :], 0
        ),
        axis=1,
    )
    far = to_far(slots)
    here = lax.axis_index("dp").astype(jnp.int32)[None]
    ends = jnp.concatenate([slots, far])
    ends = jnp.concatenate([ends, to_y(ends, 2)])
    ring = to_y(ends, 1)
    return far, jnp.concatenate([ends, here]), jnp.concatenate([ring, here])


def offer_kernel(adds, offset, held, codes, own, other, *refs):
    out = refs[-1]
    i = pl.program_id(0)
    s = codes[offset + i]
    here = codes[codes.shape[0] - 1]
    owner = s // held
    none = jnp.zeros(out.shape, out.dtype)
    value = jnp.where(owner == here, own[...], jnp.where(owner == (here ^ 1), other[...], none))
    for (start, count), ref in zip(adds, refs[:-1]):
        inside = (i >= start) & (i < start + count)
        value = value + jnp.where(inside, ref[...], none)
    out[...] = value


def offer(own, other, codes, offset, count, adds=()):
    held, block = own.shape[0], (1,) + own.shape[1:]
    last = codes.shape[0] - 1

    def stored(flip):
        def index(i, codes):
            slot = codes[offset + i]
            return (jnp.where(slot // held == codes[last] ^ flip, slot % held, 0), 0, 0)

        return pl.BlockSpec(block, index)

    in_specs = [stored(0), stored(1)]
    for _, row, start, number in adds:
        in_specs.append(
            pl.BlockSpec(
                block,
                functools.partial(
                    lambda row, start, number, i, codes: (
                        row + jnp.clip(i - start, 0, number - 1),
                        0,
                        0,
                    ),
                    row,
                    start,
                    number,
                ),
            )
        )
    size = own.size // held * own.dtype.itemsize
    return pl.pallas_call(
        functools.partial(offer_kernel, [a[2:] for a in adds], offset, held),
        grid_spec=pltpu.PrefetchScalarGridSpec(
            num_scalar_prefetch=1,
            grid=(count,),
            in_specs=in_specs,
            out_specs=pl.BlockSpec(block, lambda i, codes: (i, 0, 0)),
        ),
        out_shape=jax.ShapeDtypeStruct((count,) + own.shape[1:], own.dtype),
        compiler_params=pltpu.CompilerParams(vmem_limit_bytes=16 * 1024 * 1024),
        cost_estimate=pl.CostEstimate(
            flops=own.size, bytes_accessed=4 * count * size, transcendentals=0
        ),
    )(codes, own, other, *[a[0] for a in adds])


def matmul_kernel(pieces, with_total, final, idx, *refs):
    operands = 1 + max(p[0] for p in pieces)
    weights = 1 + max(p[4] for p in pieces)
    at = 0
    blocks = refs[at : at + operands]
    at += operands
    wq = refs[at : at + weights]
    at += weights
    wv = refs[at : at + weights]
    at += weights
    if with_total:
        tq, tv = refs[at : at + 2]
        at += 2
    if final:
        shrink, lift_q, lift_v = refs[at : at + 3]
        at += 3
    out_q, out_v = refs[at : at + 2]
    rows = out_q.shape[0]

    def spread():
        s = shrink[...]
        first = lax.broadcasted_iota(jnp.int32, s.shape, 0) < idx[weights]
        none = jnp.zeros_like(s)
        return jnp.concatenate([jnp.where(first, s, none), jnp.where(first, none, s)], axis=1)

    def run(out, ws, total, lift):
        marks = sorted({p[2] for p in pieces} | {p[2] + p[3] for p in pieces})
        more = None
        if final:
            more = jnp.dot(spread(), lift[...], preferred_element_type=jnp.float32)
        for low, high in zip(marks[:-1], marks[1:]):
            acc = None
            if with_total:
                acc = total[low:high]
            if more is not None:
                acc = acc + more[low:high]
            for op, src, dst, count, w in pieces:
                if dst <= low and high <= dst + count:
                    begin = src + low - dst
                    part = jnp.dot(
                        blocks[op][begin : begin + high - low],
                        ws[w][...],
                        preferred_element_type=jnp.float32,
                    )
                    acc = part if acc is None else acc + part
            out[low:high] = acc.astype(out.dtype)

    run(out_q, wq, tq if with_total else None, lift_q if final else None)

    @pl.when(pl.program_id(0) == 0)
    def _():
        run(out_v, wv, tv if with_total else None, lift_v if final else None)


def matmul(blocks, index, pieces, w_query, w_value, total=None, extra=None):
    weights = 1 + max(p[4] for p in pieces)
    rows = max(p[2] + p[3] for p in pieces)
    width = blocks[0].shape[1]
    nq, nv = w_query.shape[1], w_value.shape[1]
    final = extra is not None
    dtype = jnp.bfloat16 if final else jnp.float32
    whole = lambda a: pl.BlockSpec(a.shape, lambda j, idx: (0,) * a.ndim)
    in_specs = [whole(b) for b in blocks]
    in_specs += [
        pl.BlockSpec((width, TILE), functools.partial(lambda k, j, idx: (idx[k], j), k))
        for k in range(weights)
    ]
    in_specs += [
        pl.BlockSpec((width, nv), functools.partial(lambda k, j, idx: (idx[k], 0), k))
        for k in range(weights)
    ]
    operands = list(blocks) + [w_query] * weights + [w_value] * weights
    if total is not None:
        in_specs += [
            pl.BlockSpec((rows, TILE), lambda j, idx: (0, j)),
            pl.BlockSpec((rows, nv), lambda j, idx: (0, 0)),
        ]
        operands += list(total)
    if final:
        shrink, lift_q, lift_v = extra
        in_specs += [
            whole(shrink),
            pl.BlockSpec((lift_q.shape[0], TILE), lambda j, idx: (0, j)),
            whole(lift_v),
        ]
        operands += [shrink, lift_q, lift_v]
    flops = 2 * sum(p[3] for p in pieces) * width * (nq + nv)
    moved = sum(o.size * o.dtype.itemsize for o in blocks) + weights * width * (nq + nv) * 2
    moved += rows * (nq + nv) * 4 * (2 if total is not None else 1)
    return pl.pallas_call(
        functools.partial(matmul_kernel, pieces, total is not None, final),
        grid_spec=pltpu.PrefetchScalarGridSpec(
            num_scalar_prefetch=1,
            grid=(nq // TILE,),
            in_specs=in_specs,
            out_specs=[
                pl.BlockSpec((rows, TILE), lambda j, idx: (0, j)),
                pl.BlockSpec((rows, nv), lambda j, idx: (0, 0)),
            ],
        ),
        out_shape=[
            jax.ShapeDtypeStruct((rows, nq), dtype),
            jax.ShapeDtypeStruct((rows, nv), dtype),
        ],
        compiler_params=pltpu.CompilerParams(vmem_limit_bytes=44 * 1024 * 1024),
        cost_estimate=pl.CostEstimate(flops=flops, bytes_accessed=moved, transcendentals=0),
    )(index, *operands)


def shrink_kernel(bound, tokens, maps, out):
    both = jnp.concatenate([maps[0], maps[1]], axis=1)
    sums = jnp.dot(tokens[...], both, preferred_element_type=jnp.float32)
    rank = out.shape[1]
    first = lax.broadcasted_iota(jnp.int32, out.shape, 0) < bound[0]
    out[...] = jnp.where(first, sums[:, :rank], sums[:, rank:])


def partial_shrink(bound, tokens, maps):
    return pl.pallas_call(
        shrink_kernel,
        in_specs=[
            pl.BlockSpec(memory_space=pltpu.SMEM),
            pl.BlockSpec(memory_space=pltpu.VMEM),
            pl.BlockSpec(memory_space=pltpu.VMEM),
        ],
        out_specs=pl.BlockSpec(memory_space=pltpu.VMEM),
        out_shape=jax.ShapeDtypeStruct((tokens.shape[0], maps.shape[2]), jnp.float32),
        compiler_params=pltpu.CompilerParams(vmem_limit_bytes=24 * 1024 * 1024),
        cost_estimate=pl.CostEstimate(
            flops=4 * tokens.size * maps.shape[2], bytes_accessed=4 << 20, transcendentals=0
        ),
    )(bound, tokens, maps)


def on_device(
    tokens, w_query, w_value, a_both, b_query, b_value, request_adapter, adapter_slot, block_request
):
    rows, width = tokens.shape
    rank = b_query.shape[1]
    mp = lax.axis_index("mp")
    x, z = mp // NZ, mp % NZ
    s = 1 - 2 * (lax.axis_index("dp") % 2)
    bound = (SEG * jnp.sum(block_request[0] == 0)).astype(jnp.int32)

    def place(bx, step):
        return (x ^ bx) * NZ + (z + s * step) % NZ

    def add(blocks, index, pieces, total=None, extra=None):
        return matmul(blocks, index, pieces, w_query, w_value, total, extra)

    far, ends, ring = wanted_slots(request_adapter, adapter_slot)
    behind = to_z(tokens, 1)
    ahead = to_z(tokens, -1)
    across = to_x(after(tokens, far))

    other_a = to_core(a_both)
    up_message = offer(a_both, other_a, ends, 4, 2)
    up = to_y(up_message, 1)
    down_message = offer(a_both, other_a, ends, 6, 2)
    down = to_y(down_message, -1)

    own_b = jnp.concatenate([after(b_query, up_message), b_value], axis=2)
    other_b = to_core(own_b)
    total = add(
        [tokens], after(place(0, 0)[None], down_message, own_b), [(0, 0, 0, rows, 0)]
    )

    ring = after(ring, total[1], other_b)
    up_message = offer(a_both, other_a, ring, 4, 4, [(up, 0, 0, 2)])
    up = to_y(up_message, 1)
    down_message = offer(a_both, other_a, ring, 0, 4, [(down, 0, 2, 2)])
    down = to_y(down_message, -1)

    behind = after(behind, up_message, down_message)
    opposite = to_z(behind, 1)
    across = after(across, up_message, down_message)
    across_ahead = to_z(across, -1)
    cross_message = behind[:EARLY]
    cross_low = to_x(cross_message)

    far_message = offer(
        a_both, other_a, after(ends, cross_message), 2, 2, [(up, 2, 0, 2), (down, 2, 0, 2)]
    )
    far_a = to_far(far_message)
    total = add(
        [behind, ahead, across],
        after(jnp.stack([place(0, -1), place(0, 1), place(1, 0)]), far_message),
        [(k, 0, 0, rows, k) for k in range(3)],
        total,
    )

    ends_b = after(ends, total[1], cross_low)
    up_b_message = offer(own_b, other_b, ends_b, 4, 2)
    up_b = to_y(up_b_message, 1)
    down_b_message = offer(own_b, other_b, ends_b, 6, 2)
    down_b = to_y(down_b_message, -1)

    chosen_a = offer(
        a_both,
        other_a,
        after(ends, up_b_message, down_b_message),
        0,
        2,
        [(up, 0, 0, 2), (down, 0, 0, 2), (far_a, 0, 0, 2)],
    )
    narrow = lambda v: v.astype(jnp.bfloat16)
    partial = partial_shrink(bound[None], tokens, chosen_a)
    message = narrow(partial)
    partial = partial + to_x(message)
    cross_message = after(behind, message)[EARLY:]
    cross_high = to_x(cross_message)

    ring_b = after(ring, cross_message)
    up_b_message = offer(own_b, other_b, ring_b, 4, 4, [(up_b, 0, 0, 2)])
    up_b = to_y(up_b_message, 1)
    down_b_message = offer(own_b, other_b, ring_b, 0, 4, [(down_b, 0, 2, 2)])
    down_b = to_y(down_b_message, -1)

    message = narrow(after(partial, up_b_message, down_b_message))
    partial = partial + to_z(message, 1)

    last = to_z(after(across_ahead, message), -1)
    message = narrow(partial)
    shrink = narrow(partial + to_z(message, 2))
    total = add(
        [opposite, across_ahead, cross_low],
        after(jnp.stack([place(0, 2), place(1, 1), place(1, -1)]), message),
        [(0, 0, 0, rows, 0), (1, 0, 0, rows, 1), (2, 0, 0, EARLY, 2)],
        total,
    )
    far_b = to_far(
        offer(own_b, other_b, after(ends, message), 2, 2, [(up_b, 2, 0, 2), (down_b, 2, 0, 2)])
    )
    wide = offer(
        own_b, other_b, ends, 0, 2, [(up_b, 0, 0, 2), (down_b, 0, 0, 2), (far_b, 0, 0, 2)]
    )
    nq = w_query.shape[1]
    none_q = jnp.zeros((rank, nq), jnp.bfloat16)
    none_v = jnp.zeros((rank, w_value.shape[1]), jnp.bfloat16)
    lift_q = jnp.concatenate([wide[0][:, :nq], none_q, wide[1][:, :nq], none_q])
    lift_v = jnp.concatenate([none_v, wide[0][:, nq:], none_v, wide[1][:, nq:]])

    return tuple(
        add(
            [last, cross_high],
            jnp.stack([place(1, 2), place(1, -1), bound]),
            [(0, 0, 0, rows, 0), (1, 0, EARLY, rows - EARLY, 1)],
            total,
            (shrink, lift_q, lift_v),
        )
    )


def solution(mesh):
    placed = (
        P("dp", "mp"),
        P(None, "mp"),
        P(None, "mp"),
        P("dp", "mp", None),
        P("dp", None, "mp"),
        P("dp", None, "mp"),
        P("dp", None),
        P(),
        P("dp", None),
    )
    return jax.shard_map(
        on_device,
        mesh=mesh,
        in_specs=placed,
        out_specs=(P("dp", "mp"), P("dp", "mp")),
        check_vma=False,
    )
```

time: 527 us -> 170 us (0.32)
  waiting for transfers between devices: 411 us -> 44.6 us
  Pallas kernels: 0 us -> 69.8 us
  matrix products: 40.3 us -> 0 us
  starting transfers between devices: 0.15 us -> 40 us
  blocking collectives: 39.2 us -> 0 us
  between operations: 13.9 us -> 1.67 us
  local copies, waits for them, and re-layouts: 15.7 us -> 8.27 us
    all_gather x4 -> x0, waiting for transfers between devices: 409 us -> none  [the longest x1 166 us: on_device(): piece = lax.all_gather(tokens, 'mp', axis=1, tiled=True)]
    pallas_call x0 -> x17, Pallas kernels: none -> 69.8 us  [the longest x4 44.4 us: matmul(): pl.pallas_call(functools.partial(matmul_kernel, pieces, total is not None...]
    ppermute x0 -> x26, waiting for transfers between devices: none -> 44.6 us  [the longest x10 17.5 us: to_y(): lax.ppermute(v, ('dp', 'mp'), pairs(lambda h, y, c, x, z, s: (h, y + s *...]
    dot_general x8 -> x0, matrix products: 40.3 us -> none  [the longest x1 26.2 us: on_device(): base_query = jnp.dot(piece, w_query, preferred_element_type=jnp.float32)]
    ppermute x0 -> x26, starting transfers between devices: none -> 40 us  [the longest x10 17.1 us: to_y(): lax.ppermute(v, ('dp', 'mp'), pairs(lambda h, y, c, x, z, s: (h, y + s *...]
    psum x1 -> x0, blocking collectives: 39.2 us -> none  [on_device(): shrink = lax.psum(partial_shrink, 'mp').astype(jnp.bfloat16)]
    gather x4 -> x0, local copies, waits for them, and re-layouts: 15.6 us -> none  [the longest x3 14 us: on_device(): jnp.take(part, offset, axis=0)]
  transfers between devices with their start and end apart: 4 -> 26, of which waited for: 4 -> 8; matrix products, arithmetic and copies ran while one was open for 4% -> 5% of each run, Pallas kernels for 0% -> 35%
where the time goes in v1:
time: 170 us; the launch traced here: 169 us
  Pallas kernels  69.8 us (41%)
  waiting for transfers between devices  44.6 us (26%)
  starting transfers between devices  40 us (24%)
  local copies, waits for them, and re-layouts  8.27 us (5%)
  other arithmetic  5.08 us (3%)
    pallas_call x4, Pallas kernels, matmul(): pl.pallas_call(functools.partial(matmul_kernel, pieces, total is not None...  44.4 us
    pallas_call x12, Pallas kernels, offer(): pl.pallas_call(functools.partial(offer_kernel, [a[2:] for a in adds], off...  23.1 us
    ppermute x10, waiting for transfers between devices, to_y(): lax.ppermute(v, ('dp', 'mp'), pairs(lambda h, y, c, x, z, s: (h, y + s *...  17.5 us
    ppermute x10, starting transfers between devices, to_y(): lax.ppermute(v, ('dp', 'mp'), pairs(lambda h, y, c, x, z, s: (h, y + s *...  17.1 us
    ppermute x3, waiting for transfers between devices, to_far(): lax.ppermute(v, ('dp', 'mp'), pairs(lambda h, y, c, x, z, s: (1 - h, y, c...  13.7 us
    ppermute x7, starting transfers between devices, to_z(): lax.ppermute(v, ('dp', 'mp'), pairs(lambda h, y, c, x, z, s: (h, y, c, x,...  11.4 us
    ppermute x7, waiting for transfers between devices, to_z(): lax.ppermute(v, ('dp', 'mp'), pairs(lambda h, y, c, x, z, s: (h, y, c, x,...  10.1 us
    ppermute x3, starting transfers between devices, to_far(): lax.ppermute(v, ('dp', 'mp'), pairs(lambda h, y, c, x, z, s: (1 - h, y, c...  6.96 us
  transfers between devices with their start and end apart: 26, of which 8 were waited for; matrix products, arithmetic and copies ran while one was open for 5% of the time, Pallas kernels for 35%

profile of v1, /device:TPU:0, one launch (start us, length us, event | category | flops | bytes accessed | tf_op | source)
XLA Modules:
  0.0 169.4 jit_solution(3646888014713533856)
XLA Ops:
  1.6 3.2 %collective-permute-start = (s32[2]{0:T(128)S(1)}, s32[2]{0:T(128)S(1)}, u32[]{:S(2)}, u32[]{:S(2)}) collective-permute-start(s32[2]{0:T(128)S(1)} %fusion.1), channel_id=1, source_target_pairs={{0,64},{1,65},{2,66},{3,67},{4,68},{5,69},{6,70},{7,71},{8,72},{9,... | collective-permute-start | bytes 32 | tf_op jit(solution)/shard_map/ppermute | solution.py:50
  4.8 1.9 %collective-permute-done = s32[2]{0:T(128)S(1)} collective-permute-done((s32[2]{0:T(128)S(1)}, s32[2]{0:T(128)S(1)}, u32[]{:S(2)}, u32[]{:S(2)}) %collective-permute-start) | collective-permute-done | bytes 40 | tf_op jit(solution)/shard_map/ppermute | solution.py:50
  8.3 1.9 %collective-permute-start.9 = (bf16[1024,1024]{1,0:T(8,128)(2,1)}, bf16[1024,1024]{1,0:T(8,128)(2,1)}, u32[]{:S(2)}, u32[]{:S(2)}) collective-permute-start(bf16[1024,1024]{1,0:T(8,128)(2,1)} %tokens.1), channel_id=1, source_target_pairs={{0,1},{1,2},{2,3},{3,0},{4,5},{5,6},{6,7},{7,4},{8,11},{9,8},{10,9... | collective-permute-start | bytes 6291464 | tf_op jit(solution)/shard_map/ppermute | solution.py:30
  10.3 3.2 %collective-permute-start.2 = (s32[4]{0:T(128)S(1)}, s32[4]{0:T(128)S(1)}, u32[]{:S(2)}, u32[]{:S(2)}) collective-permute-start(s32[4]{0:T(128)S(1)} %pad_add_fusion.1), channel_id=1, source_target_pairs={{0,32},{1,33},{2,34},{3,35},{4,36},{5,37},{6,38},{7,39},{8,40},{9,... | collective-permute-start | bytes 56 | tf_op jit(solution)/shard_map/ppermute | solution.py:36
  13.5 1.9 %collective-permute-done.2 = s32[4]{0:T(128)S(1)} collective-permute-done((s32[4]{0:T(128)S(1)}, s32[4]{0:T(128)S(1)}, u32[]{:S(2)}, u32[]{:S(2)}) %collective-permute-start.2) | collective-permute-done | bytes 48 | tf_op jit(solution)/shard_map/ppermute | solution.py:36
  18.5 2.2 %collective-permute-start.12 = (bf16[1024,1024]{1,0:T(8,128)(2,1)}, bf16[1024,1024]{1,0:T(8,128)(2,1)}, u32[]{:S(2)}, u32[]{:S(2)}) collective-permute-start(bf16[1024,1024]{1,0:T(8,128)(2,1)} %tokens.1), channel_id=1, source_target_pairs={{0,3},{1,0},{2,1},{3,2},{4,7},{5,4},{6,5},{7,6},{8,9},{9,10},{10,1... | collective-permute-start | bytes 6291464 | tf_op jit(solution)/shard_map/ppermute | solution.py:30
  23.8 1.7 collective-permute-done.3
  25.5 1.8 %collective-permute-start.7 = (bf16[2,1024,128]{2,1,0:T(8,128)(2,1)}, bf16[2,1024,128]{2,1,0:T(8,128)(2,1)}, u32[]{:S(2)}, u32[]{:S(2)}) collective-permute-start(bf16[2,1024,128]{2,1,0:T(8,128)(2,1)} %shard_map.104), channel_id=1, source_target_pairs={{0,48},{1,49},{2,50},{3,51},{4,52},{5,53},{6,54},{7,55},{8,24},{9,... | collective-permute-start | bytes 1572872 | tf_op jit(solution)/shard_map/ppermute | solution.py:36
  28.5 6.1 %shard_map.106 = (f32[1024,1024]{1,0:T(8,128)S(1)}, f32[1024,128]{1,0:T(8,128)S(1)}) custom-call(s32[1]{0:T(128)} %bitcast.5.idx, bf16[1024,1024]{1,0:T(8,128)(2,1)} %tokens.1, bf16[8192,1024]{1,0:T(8,128)(2,1)} %refs_3_.5, bf16[8192,128]{1,0:T(8,128)(2,1)S(1)} %copy-done), custom_call_target="tpu_custom_call" | custom-call | flops 2415919104 | bytes 9175040 | tf_op jit(solution)/shard_map/pallas_call | solution.py:222
  35.4 4.5 %collective-permute-done.7.refs_0_ = bf16[2,1024,128]{2,1,0:T(8,128)(2,1)} collective-permute-done((bf16[2,1024,128]{2,1,0:T(8,128)(2,1)}, bf16[2,1024,128]{2,1,0:T(8,128)(2,1)}, u32[]{:S(2)}, u32[]{:S(2)}) %collective-permute-start.7) | collective-permute-done | bytes 524320 | tf_op jit(solution)/shard_map/ppermute | solution.py:36
  40.0 4.1 %shard_map.108 = bf16[4,1024,128]{2,1,0:T(8,128)(2,1)} custom-call(s32[9]{0:T(128)S(1)} %pad_add_fusion.3.codes, bf16[5,1024,128]{2,1,0:T(8,128)(2,1)S(1)} %copy-done.2, bf16[5,1024,128]{2,1,0:T(8,128)(2,1)S(1)} %copy-done.4, bf16[2,1024,128]{2,1,0:T(8,128)(2,1)} %collective-permute-done.7.refs_0_), custom_call_target="tpu_custom_call" | custom-call | flops 655360 | bytes 4194304 | tf_op jit(solution)/shard_map/pallas_call | solution.py:117
  44.1 3.2 %collective-permute-start.11 = (bf16[4,1024,128]{2,1,0:T(8,128)(2,1)}, bf16[4,1024,128]{2,1,0:T(8,128)(2,1)}, u32[]{:S(2)}, u32[]{:S(2)}) collective-permute-start(bf16[4,1024,128]{2,1,0:T(8,128)(2,1)} %shard_map.108), channel_id=1, source_target_pairs={{0,48},{1,49},{2,50},{3,51},{4,52},{5,53},{6,54},{7,55},{8,24},{9,... | collective-permute-start | bytes 3145736 | tf_op jit(solution)/shard_map/ppermute | solution.py:36
  47.3 3.3 %shard_map.107 = bf16[4,1024,128]{2,1,0:T(8,128)(2,1)} custom-call(s32[9]{0:T(128)S(1)} %pad_add_fusion.3.codes, bf16[5,1024,128]{2,1,0:T(8,128)(2,1)S(1)} %copy-done.2, bf16[5,1024,128]{2,1,0:T(8,128)(2,1)S(1)} %copy-done.4, bf16[2,1024,128]{2,1,0:T(8,128)(2,1)} %collective-permute-done.6.refs_0_), custom_call_target="tpu_custom_call" | custom-call | flops 655360 | bytes 4194304 | tf_op jit(solution)/shard_map/pallas_call | solution.py:117
  50.6 3.3 %collective-permute-done.1.refs_2_ = bf16[1024,1024]{1,0:T(8,128)(2,1)} collective-permute-done((bf16[1024,1024]{1,0:T(8,128)(2,1)}, bf16[1024,1024]{1,0:T(8,128)(2,1)}, u32[]{:S(2)}, u32[]{:S(2)}) %collective-permute-start.1) | collective-permute-done | bytes 2097184 | tf_op jit(solution)/shard_map/ppermute | solution.py:42
  53.9 4.1 %collective-permute-start.8 = (bf16[1024,1024]{1,0:T(8,128)(2,1)}, bf16[1024,1024]{1,0:T(8,128)(2,1)}, u32[]{:S(2)}, u32[]{:S(2)}) collective-permute-start(bf16[1024,1024]{1,0:T(8,128)(2,1)} %collective-permute-done.1.refs_2_), channel_id=1, source_target_pairs={{0,3},{1,0},{2,1},{3,2},{4,7},{5,4},{6,5},{7,6},{8,9},{9,10},{10,1... | collective-permute-start | bytes 6291464 | tf_op jit(solution)/shard_map/ppermute | solution.py:30
  60.6 9.4 %collective-permute-done.11.refs_1_ = bf16[4,1024,128]{2,1,0:T(8,128)(2,1)} collective-permute-done((bf16[4,1024,128]{2,1,0:T(8,128)(2,1)}, bf16[4,1024,128]{2,1,0:T(8,128)(2,1)}, u32[]{:S(2)}, u32[]{:S(2)}) %collective-permute-start.11) | collective-permute-done | bytes 1048608 | tf_op jit(solution)/shard_map/ppermute | solution.py:36
  70.6 2.0 %shard_map.109 = bf16[2,1024,128]{2,1,0:T(8,128)(2,1)S(1)} custom-call(s32[9]{0:T(128)S(1)} %add_add_fusion.codes, bf16[5,1024,128]{2,1,0:T(8,128)(2,1)S(1)} %copy-done.2, bf16[5,1024,128]{2,1,0:T(8,128)(2,1)S(1)} %copy-done.5, bf16[4,1024,128]{2,1,0:T(8,128)(2,1)} %collective-permute-done.10.refs_0_, bf16[4,1024,128]{2,1,0:T(8,128)(2,1)} %collective-permute-done.11.refs_1_), custom_call_target="tpu_custom_call" | custom-call | flops 655360 | bytes 2097152 | tf_op jit(solution)/shard_map/pallas_call | solution.py:117
  72.6 3.1 %collective-permute-start.14 = (bf16[2,1024,128]{2,1,0:T(8,128)(2,1)S(1)}, bf16[2,1024,128]{2,1,0:T(8,128)(2,1)S(1)}, u32[]{:S(2)}, u32[]{:S(2)}) collective-permute-start(bf16[2,1024,128]{2,1,0:T(8,128)(2,1)S(1)} %shard_map.109), channel_id=1, source_target_pairs={{0,64},{1,65},{2,66},{3,67},{4,68},{5,69},{6,70},{7,71},{8,72},{9,... | collective-permute-start | bytes 1572872 | tf_op jit(solution)/shard_map/ppermute | solution.py:50
  75.7 14.8 %shard_map.110 = (f32[1024,1024]{1,0:T(8,128)}, f32[1024,128]{1,0:T(8,128)S(1)}) custom-call(s32[3]{0:T(128)S(1)} %pad_add_fusion.4.idx, bf16[1024,1024]{1,0:T(8,128)(2,1)} %collective-permute-done.9.refs_0_, bf16[1024,1024]{1,0:T(8,128)(2,1)} %collective-permute-done.12.refs_1_, bf16[1024,1024]{1,0:T(8,128)(2,1)} %collective-permute-done.1.refs_2_, ...), custom_call_target="tpu_custom_call" | custom-call | flops 7247757312 | bytes 22806528 | tf_op jit(solution)/shard_map/pallas_call | solution.py:222
  91.2 3.8 %collective-permute-start.17 = (bf16[2,64,1152]{2,1,0:T(8,128)(2,1)S(1)}, bf16[2,64,1152]{2,1,0:T(8,128)(2,1)S(1)}, u32[]{:S(2)}, u32[]{:S(2)}) collective-permute-start(bf16[2,64,1152]{2,1,0:T(8,128)(2,1)S(1)} %shard_map.112), channel_id=1, source_target_pairs={{0,48},{1,49},{2,50},{3,51},{4,52},{5,53},{6,54},{7,55},{8,24},{9,... | collective-permute-start | bytes 884744 | tf_op jit(solution)/shard_map/ppermute | solution.py:36
  95.7 2.0 %shard_map.113.maps = bf16[2,1024,128]{2,1,0:T(8,128)(2,1)S(1)} custom-call(s32[9]{0:T(128)S(1)} %add_add_fusion.codes, bf16[5,1024,128]{2,1,0:T(8,128)(2,1)S(1)} %copy-done.2, bf16[5,1024,128]{2,1,0:T(8,128)(2,1)S(1)} %copy-done.5, bf16[4,1024,128]{2,1,0:T(8,128)(2,1)} %collective-permute-done.10.refs_0_, ...), custom_call_target="tpu_custom_call" | custom-call | flops 655360 | bytes 2097152 | tf_op jit(solution)/shard_map/pallas_call | solution.py:117
  97.8 2.3 %shard_map.114 = f32[1024,128]{1,0:T(8,128)S(1)} custom-call(s32[1]{0:T(128)} %bitcast.2.bound, bf16[1024,1024]{1,0:T(8,128)(2,1)} %tokens.1, bf16[2,1024,128]{2,1,0:T(8,128)(2,1)S(1)} %shard_map.113.maps), custom_call_target="tpu_custom_call" | custom-call | flops 536870912 | bytes 4194304 | tf_op jit(solution)/shard_map/pallas_call | solution.py:251
  101.0 2.5 %slice.27 = bf16[640,1024]{1,0:T(8,128)(2,1)} slice(bf16[1024,1024]{1,0:T(8,128)(2,1)} %collective-permute-done.9.refs_0_), slice={[384:1024], [0:1024]} | slice | bytes 2621440 | tf_op jit(solution)/shard_map/slice | solution.py:342
  103.5 2.1 %shard_map.116 = bf16[4,64,1152]{2,1,0:T(8,128)(2,1)} custom-call(s32[9]{0:T(128)S(1)} %pad_add_fusion.3.codes, bf16[5,64,1152]{2,1,0:T(8,128)(2,1)S(1)} %copy-done.7, bf16[5,64,1152]{2,1,0:T(8,128)(2,1)S(1)} %copy-done.10, bf16[2,64,1152]{2,1,0:T(8,128)(2,1)S(1)} %collective-permute-done.17.refs_0_), custom_call_target="tpu_custom_call" | custom-call | flops 368640 | bytes 2359296 | tf_op jit(solution)/shard_map/pallas_call | solution.py:117
  105.5 2.0 %shard_map.115 = bf16[4,64,1152]{2,1,0:T(8,128)(2,1)} custom-call(s32[9]{0:T(128)S(1)} %pad_add_fusion.3.codes, bf16[5,64,1152]{2,1,0:T(8,128)(2,1)S(1)} %copy-done.7, bf16[5,64,1152]{2,1,0:T(8,128)(2,1)S(1)} %copy-done.10, bf16[2,64,1152]{2,1,0:T(8,128)(2,1)S(1)} %collective-permute-done.16.refs_0_), custom_call_target="tpu_custom_call" | custom-call | flops 368640 | bytes 2359296 | tf_op jit(solution)/shard_map/pallas_call | solution.py:117
  110.0 3.2 %collective-permute-start.24 = (bf16[4,64,1152]{2,1,0:T(8,128)(2,1)}, bf16[4,64,1152]{2,1,0:T(8,128)(2,1)S(1)}, u32[]{:S(2)}, u32[]{:S(2)}) collective-permute-start(bf16[4,64,1152]{2,1,0:T(8,128)(2,1)} %shard_map.116), channel_id=1, source_target_pairs={{0,48},{1,49},{2,50},{3,51},{4,52},{5,53},{6,54},{7,55},{8,24},{9,... | collective-permute-start | bytes 1769480 | tf_op jit(solution)/shard_map/ppermute | solution.py:36
  113.9 10.1 %collective-permute-done.20 = bf16[1024,128]{1,0:T(8,128)(2,1)} collective-permute-done((bf16[1024,128]{1,0:T(8,128)(2,1)}, bf16[1024,128]{1,0:T(8,128)(2,1)}, u32[]{:S(2)}, u32[]{:S(2)}) %collective-permute-start.20) | collective-permute-done | bytes 262176 | tf_op jit(solution)/shard_map/ppermute | solution.py:30
  128.9 1.6 shard_map.118
  131.2 13.0 %shard_map.117 = (f32[1024,1024]{1,0:T(8,128)}, f32[1024,128]{1,0:T(8,128)S(1)}) custom-call(s32[3]{0:T(128)S(1)} %pad_add_fusion.5.idx, bf16[1024,1024]{1,0:T(8,128)(2,1)} %collective-permute-done.21.refs_0_, bf16[1024,1024]{1,0:T(8,128)(2,1)} %collective-permute-done.8.refs_1_, bf16[384,1024]{1,0:T(8,128)(2,1)S(1)} %copy-done.15, ...), custom_call_target="tpu_custom_call" | custom-call | flops 5737807872 | bytes 21495808 | tf_op jit(solution)/shard_map/pallas_call | solution.py:222
  145.3 11.7 %collective-permute-done.25.refs_2_ = bf16[2,64,1152]{2,1,0:T(8,128)(2,1)S(1)} collective-permute-done((bf16[2,64,1152]{2,1,0:T(8,128)(2,1)S(1)}, bf16[2,64,1152]{2,1,0:T(8,128)(2,1)S(1)}, u32[]{:S(2)}, u32[]{:S(2)}) %collective-permute-start.25) | collective-permute-done | bytes 294944 | tf_op jit(solution)/shard_map/ppermute | solution.py:50
  157.0 1.7 shard_map.119
  158.9 10.5 %shard_map.120 = (bf16[1024,1024]{1,0:T(8,128)(2,1)}, bf16[1024,128]{1,0:T(8,128)(2,1)}) custom-call(s32[3]{0:T(128)S(1)} %pad_add_fusion.idx, bf16[1024,1024]{1,0:T(8,128)(2,1)} %collective-permute-done.18.refs_0_, bf16[640,1024]{1,0:T(8,128)(2,1)S(1)} %collective-permute-done.19.refs_1_, bf16[8192,1024]{1,0:T(8,128)(2,1)} %refs_3_.5, ...), custom_call_target="tpu_custom_call" | custom-call | flops 3925868544 | bytes 17563648 | tf_op jit(solution)/shard_map/pallas_call | solution.py:222
  (114 shorter events, 25.6 us)
Async XLA Ops:
  0.6 14.8 %collective-permute-start.4 = (bf16[5,1024,128]{2,1,0:T(8,128)(2,1)}, bf16[5,1024,128]{2,1,0:T(8,128)(2,1)S(1)}, u32[]{:S(2)}, u32[]{:S(2)}) collective-permute-start(bf16[5,1024,128]{2,1,0:T(8,128)(2,1)} %own.11), channel_id=1, source_target_pairs={{0,8},{1,9},{2,10},{3,11},{4,12},{5,13},{6,14},{7,15},{8,0},{9,1},... | collective-permute-start | bytes 3932168 | tf_op jit(solution)/shard_map/ppermute | solution.py:46
  1.6 5.1 %collective-permute-start = (s32[2]{0:T(128)S(1)}, s32[2]{0:T(128)S(1)}, u32[]{:S(2)}, u32[]{:S(2)}) collective-permute-start(s32[2]{0:T(128)S(1)} %fusion.1), channel_id=1, source_target_pairs={{0,64},{1,65},{2,66},{3,67},{4,68},{5,69},{6,70},{7,71},{8,72},{9,... | collective-permute-start | bytes 32 | tf_op jit(solution)/shard_map/ppermute | solution.py:50
  6.7 47.2 %collective-permute-start.1 = (bf16[1024,1024]{1,0:T(8,128)(2,1)}, bf16[1024,1024]{1,0:T(8,128)(2,1)}, u32[]{:S(2)}, u32[]{:S(2)}) collective-permute-start(bf16[1024,1024]{1,0:T(8,128)(2,1)} %tokens.1), channel_id=1, source_target_pairs={{0,4},{1,5},{2,6},{3,7},{4,0},{5,1},{6,2},{7,3},{8,12},{9,13},{10,... | collective-permute-start | bytes 6291464 | tf_op jit(solution)/shard_map/ppermute | solution.py:42
  8.3 49.7 %collective-permute-start.9 = (bf16[1024,1024]{1,0:T(8,128)(2,1)}, bf16[1024,1024]{1,0:T(8,128)(2,1)}, u32[]{:S(2)}, u32[]{:S(2)}) collective-permute-start(bf16[1024,1024]{1,0:T(8,128)(2,1)} %tokens.1), channel_id=1, source_target_pairs={{0,1},{1,2},{2,3},{3,0},{4,5},{5,6},{6,7},{7,4},{8,11},{9,8},{10,9... | collective-permute-start | bytes 6291464 | tf_op jit(solution)/shard_map/ppermute | solution.py:30
  10.3 5.1 %collective-permute-start.2 = (s32[4]{0:T(128)S(1)}, s32[4]{0:T(128)S(1)}, u32[]{:S(2)}, u32[]{:S(2)}) collective-permute-start(s32[4]{0:T(128)S(1)} %pad_add_fusion.1), channel_id=1, source_target_pairs={{0,32},{1,33},{2,34},{3,35},{4,36},{5,37},{6,38},{7,39},{8,40},{9,... | collective-permute-start | bytes 56 | tf_op jit(solution)/shard_map/ppermute | solution.py:36
  18.4 8.9 %collective-permute-start.5 = (bf16[5,64,1152]{2,1,0:T(8,128)(2,1)S(1)}, bf16[5,64,1152]{2,1,0:T(8,128)(2,1)S(1)}, u32[]{:S(2)}, u32[]{:S(2)}) collective-permute-start(bf16[5,64,1152]{2,1,0:T(8,128)(2,1)S(1)} %constant_dynamic-update-slice_fusion.own), channel_id=1, source_target_pairs={{0,8},{1,9},{2,10},{3,11},{4,12},{5,13},{6,14},{7,15},{8,0},{9,1},... | collective-permute-start | bytes 2211848 | tf_op jit(solution)/shard_map/ppermute | solution.py:46
  18.5 57.2 %collective-permute-start.12 = (bf16[1024,1024]{1,0:T(8,128)(2,1)}, bf16[1024,1024]{1,0:T(8,128)(2,1)}, u32[]{:S(2)}, u32[]{:S(2)}) collective-permute-start(bf16[1024,1024]{1,0:T(8,128)(2,1)} %tokens.1), channel_id=1, source_target_pairs={{0,3},{1,0},{2,1},{3,2},{4,7},{5,4},{6,5},{7,6},{8,9},{9,10},{10,1... | collective-permute-start | bytes 6291464 | tf_op jit(solution)/shard_map/ppermute | solution.py:30
  20.7 4.8 %collective-permute-start.3 = (s32[8]{0:T(128)S(1)}, s32[8]{0:T(128)S(1)}, u32[]{:S(2)}, u32[]{:S(2)}) collective-permute-start(s32[8]{0:T(128)S(1)} %pad_add_fusion.2), channel_id=1, source_target_pairs={{0,16},{1,17},{2,18},{3,19},{4,20},{5,21},{6,22},{7,23},{8,56},{9,... | collective-permute-start | bytes 104 | tf_op jit(solution)/shard_map/ppermute | solution.py:36
  25.5 14.5 %collective-permute-start.7 = (bf16[2,1024,128]{2,1,0:T(8,128)(2,1)}, bf16[2,1024,128]{2,1,0:T(8,128)(2,1)}, u32[]{:S(2)}, u32[]{:S(2)}) collective-permute-start(bf16[2,1024,128]{2,1,0:T(8,128)(2,1)} %shard_map.104), channel_id=1, source_target_pairs={{0,48},{1,49},{2,50},{3,51},{4,52},{5,53},{6,54},{7,55},{8,24},{9,... | collective-permute-start | bytes 1572872 | tf_op jit(solution)/shard_map/ppermute | solution.py:36
  28.2 19.1 %collective-permute-start.6 = (bf16[2,1024,128]{2,1,0:T(8,128)(2,1)}, bf16[2,1024,128]{2,1,0:T(8,128)(2,1)}, u32[]{:S(2)}, u32[]{:S(2)}) collective-permute-start(bf16[2,1024,128]{2,1,0:T(8,128)(2,1)} %shard_map.105), channel_id=1, source_target_pairs={{0,16},{1,17},{2,18},{3,19},{4,20},{5,21},{6,22},{7,23},{8,56},{9,... | collective-permute-start | bytes 1572872 | tf_op jit(solution)/shard_map/ppermute | solution.py:36
  44.1 14.0 %copy-start.24 = (s32[1,8]{1,0:T(1,128)S(1)}, s32[1,8]{1,0:T(1,128)}, u32[]{:S(2)}) copy-start(s32[1,8]{1,0:T(1,128)} %param.17) | copy-start | bytes 100
  44.1 25.9 %collective-permute-start.11 = (bf16[4,1024,128]{2,1,0:T(8,128)(2,1)}, bf16[4,1024,128]{2,1,0:T(8,128)(2,1)}, u32[]{:S(2)}, u32[]{:S(2)}) collective-permute-start(bf16[4,1024,128]{2,1,0:T(8,128)(2,1)} %shard_map.108), channel_id=1, source_target_pairs={{0,48},{1,49},{2,50},{3,51},{4,52},{5,53},{6,54},{7,55},{8,24},{9,... | collective-permute-start | bytes 3145736 | tf_op jit(solution)/shard_map/ppermute | solution.py:36
  50.6 20.0 %collective-permute-start.10 = (bf16[4,1024,128]{2,1,0:T(8,128)(2,1)}, bf16[4,1024,128]{2,1,0:T(8,128)(2,1)}, u32[]{:S(2)}, u32[]{:S(2)}) collective-permute-start(bf16[4,1024,128]{2,1,0:T(8,128)(2,1)} %shard_map.107), channel_id=1, source_target_pairs={{0,16},{1,17},{2,18},{3,19},{4,20},{5,21},{6,22},{7,23},{8,56},{9,... | collective-permute-start | bytes 3145736 | tf_op jit(solution)/shard_map/ppermute | solution.py:36
  53.9 54.5 %collective-permute-start.8 = (bf16[1024,1024]{1,0:T(8,128)(2,1)}, bf16[1024,1024]{1,0:T(8,128)(2,1)}, u32[]{:S(2)}, u32[]{:S(2)}) collective-permute-start(bf16[1024,1024]{1,0:T(8,128)(2,1)} %collective-permute-done.1.refs_2_), channel_id=1, source_target_pairs={{0,3},{1,0},{2,1},{3,2},{4,7},{5,4},{6,5},{7,6},{8,9},{9,10},{10,1... | collective-permute-start | bytes 6291464 | tf_op jit(solution)/shard_map/ppermute | solution.py:30
  58.0 73.2 %collective-permute-start.21 = (bf16[1024,1024]{1,0:T(8,128)(2,1)}, bf16[1024,1024]{1,0:T(8,128)(2,1)}, u32[]{:S(2)}, u32[]{:S(2)}) collective-permute-start(bf16[1024,1024]{1,0:T(8,128)(2,1)} %collective-permute-done.9.refs_0_), channel_id=1, source_target_pairs={{0,1},{1,2},{2,3},{3,0},{4,5},{5,6},{6,7},{7,4},{8,11},{9,8},{10,9... | collective-permute-start | bytes 6291464 | tf_op jit(solution)/shard_map/ppermute | solution.py:30
  70.0 20.5 %collective-permute-start.13 = (bf16[384,1024]{1,0:T(8,128)(2,1)S(1)}, bf16[384,1024]{1,0:T(8,128)(2,1)S(1)}, u32[]{:S(2)}, u32[]{:S(2)}) collective-permute-start(bf16[384,1024]{1,0:T(8,128)(2,1)S(1)} %slice.26), channel_id=1, source_target_pairs={{0,4},{1,5},{2,6},{3,7},{4,0},{5,1},{6,2},{7,3},{8,12},{9,13},{10,... | collective-permute-start | bytes 2359304 | tf_op jit(solution)/shard_map/ppermute | solution.py:42
  72.6 23.1 %collective-permute-start.14 = (bf16[2,1024,128]{2,1,0:T(8,128)(2,1)S(1)}, bf16[2,1024,128]{2,1,0:T(8,128)(2,1)S(1)}, u32[]{:S(2)}, u32[]{:S(2)}) collective-permute-start(bf16[2,1024,128]{2,1,0:T(8,128)(2,1)S(1)} %shard_map.109), channel_id=1, source_target_pairs={{0,64},{1,65},{2,66},{3,67},{4,68},{5,69},{6,70},{7,71},{8,72},{9,... | collective-permute-start | bytes 1572872 | tf_op jit(solution)/shard_map/ppermute | solution.py:50
  75.7 14.8 %copy-start.7 = (bf16[5,64,1152]{2,1,0:T(8,128)(2,1)S(1)}, bf16[5,64,1152]{2,1,0:T(8,128)(2,1)}, u32[]{:S(2)}) copy-start(bf16[5,64,1152]{2,1,0:T(8,128)(2,1)} %copy-done.6) | copy-start | bytes 2211844
  75.7 14.8 %copy-start.10 = (bf16[5,64,1152]{2,1,0:T(8,128)(2,1)S(1)}, bf16[5,64,1152]{2,1,0:T(8,128)(2,1)}, u32[]{:S(2)}) copy-start(bf16[5,64,1152]{2,1,0:T(8,128)(2,1)} %copy-done.9) | copy-start | bytes 2211844
  91.2 12.2 %collective-permute-start.17 = (bf16[2,64,1152]{2,1,0:T(8,128)(2,1)S(1)}, bf16[2,64,1152]{2,1,0:T(8,128)(2,1)S(1)}, u32[]{:S(2)}, u32[]{:S(2)}) collective-permute-start(bf16[2,64,1152]{2,1,0:T(8,128)(2,1)S(1)} %shard_map.112), channel_id=1, source_target_pairs={{0,48},{1,49},{2,50},{3,51},{4,52},{5,53},{6,54},{7,55},{8,24},{9,... | collective-permute-start | bytes 884744 | tf_op jit(solution)/shard_map/ppermute | solution.py:36
  95.6 9.9 %collective-permute-start.16 = (bf16[2,64,1152]{2,1,0:T(8,128)(2,1)S(1)}, bf16[2,64,1152]{2,1,0:T(8,128)(2,1)S(1)}, u32[]{:S(2)}, u32[]{:S(2)}) collective-permute-start(bf16[2,64,1152]{2,1,0:T(8,128)(2,1)S(1)} %shard_map.111), channel_id=1, source_target_pairs={{0,16},{1,17},{2,18},{3,19},{4,20},{5,21},{6,22},{7,23},{8,56},{9,... | collective-permute-start | bytes 884744 | tf_op jit(solution)/shard_map/ppermute | solution.py:36
  100.1 7.4 %collective-permute-start.15 = (bf16[1024,128]{1,0:T(8,128)(2,1)S(1)}, bf16[1024,128]{1,0:T(8,128)(2,1)S(1)}, u32[]{:S(2)}, u32[]{:S(2)}) collective-permute-start(bf16[1024,128]{1,0:T(8,128)(2,1)S(1)} %convert_element_type.26), channel_id=1, source_target_pairs={{0,4},{1,5},{2,6},{3,7},{4,0},{5,1},{6,2},{7,3},{8,12},{9,13},{10,... | collective-permute-start | bytes 786440 | tf_op jit(solution)/shard_map/ppermute | solution.py:42
  107.6 20.2 %copy-start.8 = (bf16[5,64,1152]{2,1,0:T(8,128)(2,1)S(1)}, bf16[5,64,1152]{2,1,0:T(8,128)(2,1)}, u32[]{:S(2)}) copy-start(bf16[5,64,1152]{2,1,0:T(8,128)(2,1)} %copy-done.6) | copy-start | bytes 2211844
  108.5 50.4 %collective-permute-start.18 = (bf16[1024,1024]{1,0:T(8,128)(2,1)}, bf16[1024,1024]{1,0:T(8,128)(2,1)}, u32[]{:S(2)}, u32[]{:S(2)}) collective-permute-start(bf16[1024,1024]{1,0:T(8,128)(2,1)} %collective-permute-done.8.refs_1_), channel_id=1, source_target_pairs={{0,3},{1,0},{2,1},{3,2},{4,7},{5,4},{6,5},{7,6},{8,9},{9,10},{10,1... | collective-permute-start | bytes 6291464 | tf_op jit(solution)/shard_map/ppermute | solution.py:30
  110.0 16.6 %collective-permute-start.24 = (bf16[4,64,1152]{2,1,0:T(8,128)(2,1)}, bf16[4,64,1152]{2,1,0:T(8,128)(2,1)S(1)}, u32[]{:S(2)}, u32[]{:S(2)}) collective-permute-start(bf16[4,64,1152]{2,1,0:T(8,128)(2,1)} %shard_map.116), channel_id=1, source_target_pairs={{0,48},{1,49},{2,50},{3,51},{4,52},{5,53},{6,54},{7,55},{8,24},{9,... | collective-permute-start | bytes 1769480 | tf_op jit(solution)/shard_map/ppermute | solution.py:36
  113.2 14.5 %collective-permute-start.23 = (bf16[4,64,1152]{2,1,0:T(8,128)(2,1)}, bf16[4,64,1152]{2,1,0:T(8,128)(2,1)}, u32[]{:S(2)}, u32[]{:S(2)}) collective-permute-start(bf16[4,64,1152]{2,1,0:T(8,128)(2,1)} %shard_map.115), channel_id=1, source_target_pairs={{0,16},{1,17},{2,18},{3,19},{4,20},{5,21},{6,22},{7,23},{8,56},{9,... | collective-permute-start | bytes 1769480 | tf_op jit(solution)/shard_map/ppermute | solution.py:36
  113.2 10.8 %collective-permute-start.20 = (bf16[1024,128]{1,0:T(8,128)(2,1)}, bf16[1024,128]{1,0:T(8,128)(2,1)}, u32[]{:S(2)}, u32[]{:S(2)}) collective-permute-start(bf16[1024,128]{1,0:T(8,128)(2,1)} %convert_element_type.28), channel_id=1, source_target_pairs={{0,1},{1,2},{2,3},{3,0},{4,5},{5,6},{6,7},{7,4},{8,11},{9,8},{10,9... | collective-permute-start | bytes 786440 | tf_op jit(solution)/shard_map/ppermute | solution.py:30
  113.7 17.5 %copy-start.15 = (bf16[384,1024]{1,0:T(8,128)(2,1)S(1)}, bf16[384,1024]{1,0:T(8,128)(2,1)}, u32[]{:S(2)}) copy-start(bf16[384,1024]{1,0:T(8,128)(2,1)} %copy-done.14) | copy-start | bytes 2359300
  124.0 34.9 %collective-permute-start.19 = (bf16[640,1024]{1,0:T(8,128)(2,1)}, bf16[640,1024]{1,0:T(8,128)(2,1)S(1)}, u32[]{:S(2)}, u32[]{:S(2)}) collective-permute-start(bf16[640,1024]{1,0:T(8,128)(2,1)} %slice.27), channel_id=1, source_target_pairs={{0,4},{1,5},{2,6},{3,7},{4,0},{5,1},{6,2},{7,3},{8,12},{9,13},{10,... | collective-permute-start | bytes 3932168 | tf_op jit(solution)/shard_map/ppermute | solution.py:42
  126.6 17.6 %collective-permute-start.22 = (bf16[1024,128]{1,0:T(8,128)(2,1)S(1)}, bf16[1024,128]{1,0:T(8,128)(2,1)S(1)}, u32[]{:S(2)}, u32[]{:S(2)}) collective-permute-start(bf16[1024,128]{1,0:T(8,128)(2,1)S(1)} %fusion), channel_id=1, source_target_pairs={{0,2},{1,3},{2,0},{3,1},{4,6},{5,7},{6,4},{7,5},{8,10},{9,11},{10,... | collective-permute-start | bytes 786440 | tf_op jit(solution)/shard_map/ppermute | solution.py:30
  130.5 26.5 %collective-permute-start.25 = (bf16[2,64,1152]{2,1,0:T(8,128)(2,1)S(1)}, bf16[2,64,1152]{2,1,0:T(8,128)(2,1)S(1)}, u32[]{:S(2)}, u32[]{:S(2)}) collective-permute-start(bf16[2,64,1152]{2,1,0:T(8,128)(2,1)S(1)} %shard_map.118), channel_id=1, source_target_pairs={{0,64},{1,65},{2,66},{3,67},{4,68},{5,69},{6,70},{7,71},{8,72},{9,... | collective-permute-start | bytes 884744 | tf_op jit(solution)/shard_map/ppermute | solution.py:50
  131.2 25.8 %copy-start.12 = (bf16[5,64,1152]{2,1,0:T(8,128)(2,1)S(1)}, bf16[5,64,1152]{2,1,0:T(8,128)(2,1)}, u32[]{:S(2)}) copy-start(bf16[5,64,1152]{2,1,0:T(8,128)(2,1)} %copy-done.9) | copy-start | bytes 2211844
  (19 other events, 107.3 us)

commit v2 on v1

v2 whole, which is shorter than its diff:
```python
import functools

import jax
import jax.numpy as jnp
from jax import lax
from jax.experimental import pallas as pl
from jax.experimental.pallas import tpu as pltpu
from jax.sharding import PartitionSpec as P

SEG = 128
NX, NZ = 2, 4
TILE, STEP = 512, 256
EARLY, MIDDLE = 256, 512


def pairs(move):
    found = []
    for h in range(2):
        for y in range(4):
            for c in range(2):
                for x in range(NX):
                    for z in range(NZ):
                        th, ty, tc, tx, tz = move(h, y, c, x, z, 1 - 2 * c)
                        there = ((th * 4 + ty % 4) * 2 + tc) * NX * NZ + tx * NZ + tz % NZ
                        found.append((((h * 4 + y) * 2 + c) * NX * NZ + x * NZ + z, there))
    return found


def to_z(v, step):
    return lax.ppermute(
        v, ("dp", "mp"), pairs(lambda h, y, c, x, z, s: (h, y, c, x, z + s * step))
    )


def to_y(v, step):
    return lax.ppermute(
        v, ("dp", "mp"), pairs(lambda h, y, c, x, z, s: (h, y + s * step, c, x, z))
    )


def to_x(v):
    return lax.ppermute(v, ("dp", "mp"), pairs(lambda h, y, c, x, z, s: (h, y, c, 1 - x, z)))


def to_core(v):
    return lax.ppermute(v, ("dp", "mp"), pairs(lambda h, y, c, x, z, s: (h, y, 1 - c, x, z)))


def to_far(v):
    return lax.ppermute(v, ("dp", "mp"), pairs(lambda h, y, c, x, z, s: (1 - h, y, c, x, z)))


def after(v, *earlier):
    return lax.optimization_barrier((v,) + earlier)[0]


def wanted_slots(request_adapter, adapter_slot):
    every = adapter_slot.shape[0]
    ids = request_adapter[0]
    slots = jnp.sum(
        jnp.where(
            ids[:, None] == jnp.arange(every, dtype=jnp.int32)[None, :], adapter_slot[None, :], 0
        ),
        axis=1,
    )
    far = to_far(slots)
    here = lax.axis_index("dp").astype(jnp.int32)[None]
    ends = jnp.concatenate([slots, far])
    ends = jnp.concatenate([ends, to_y(ends, 2)])
    ring = to_y(ends, 1)
    return far, jnp.concatenate([ends, here]), jnp.concatenate([ring, here])


def offer_kernel(adds, offset, count, held, codes, own, other, *refs):
    out = refs[-1]
    here = codes[codes.shape[0] - 1]
    none = jnp.zeros(out.shape[1:], out.dtype)
    for i in range(count):
        slot = codes[offset + i]
        owner, at = slot // held, slot % held
        given = [ref[row + i] for ref, (row, number) in zip(refs[:-1], adds) if i < number]
        rest = None
        for g in given:
            rest = g if rest is None else rest + g
        if rest is None:
            rest = none
        out[i] = rest

        @pl.when(owner == here)
        def _():
            out[i] = rest + own[at]

        @pl.when(owner == (here ^ 1))
        def _():
            out[i] = rest + other[at]


def offer(own, other, codes, offset, count, adds=()):
    size = own.size // own.shape[0] * own.dtype.itemsize
    vmem = pl.BlockSpec(memory_space=pltpu.VMEM)
    return pl.pallas_call(
        functools.partial(offer_kernel, [a[1:] for a in adds], offset, count, own.shape[0]),
        in_specs=[pl.BlockSpec(memory_space=pltpu.SMEM)] + [vmem] * (2 + len(adds)),
        out_specs=vmem,
        out_shape=jax.ShapeDtypeStruct((count,) + own.shape[1:], own.dtype),
        compiler_params=pltpu.CompilerParams(vmem_limit_bytes=16 * 1024 * 1024),
        cost_estimate=pl.CostEstimate(
            flops=own.size, bytes_accessed=4 * count * size, transcendentals=0
        ),
    )(codes, own, other, *[a[0] for a in adds])


def matmul_kernel(pieces, with_total, final, emit, tile, step, idx, *refs):
    operands = 1 + max(p[0] for p in pieces)
    weights = 1 + max(p[4] for p in pieces)
    refs = list(refs)
    take = lambda n: [refs.pop(0) for _ in range(n)]
    blocks = take(operands)
    w_query, w_value = take(2)
    totals = take(2) if with_total else []
    extra = take(3) if final else []
    outs = take(2)
    emitted = take(len(emit))
    held = take(operands)
    wq, wv = take(2)
    held_totals = take(2) if with_total else []
    held_extra = take(3) if final else []
    accs = take(2)
    sems, total_sems, out_sems = take(3)
    bound = idx[weights] if final else 0
    width = wq.shape[1]
    rows, nq = accs[0].shape
    copies = {}

    def fetch(name, src, dst):
        copies[name] = pltpu.make_async_copy(src, dst, sems.at[len(copies)])
        copies[name].start()

    order = []
    for p in pieces:
        if p[4] not in order:
            order.append(p[4])

    def fetch_step(n):
        for p in pieces:
            if p[4] == order[n] and ("x", p[0]) not in copies:
                fetch(("x", p[0]), blocks[p[0]], held[p[0]])
        at = pl.ds(pl.multiple_of(idx[order[n]] * width, width), width)
        fetch(("q", order[n]), w_query.at[at], wq.at[order[n]])
        fetch(("v", order[n]), w_value.at[at], wv.at[order[n]])

    for i in range(len(extra)):
        fetch(("e", i), extra[i], held_extra[i])
    fetch_step(0)

    def total_tile(j):
        at = pl.ds(pl.multiple_of(j * tile, tile), tile)
        return pltpu.make_async_copy(
            totals[0].at[:, at], held_totals[0].at[:, at], total_sems.at[j]
        )

    if with_total:
        for j in range(nq // tile):
            total_tile(j).start()
        total_value = pltpu.make_async_copy(
            totals[1], held_totals[1], total_sems.at[nq // tile]
        )
        total_value.start()
    waited = set()

    def wait(name):
        if name not in waited:
            waited.add(name)
            copies[name].wait()

    sent = []
    for n, w in enumerate(order):
        mine = [p for p in pieces if p[4] == w]
        for p in mine:
            wait(("x", p[0]))
            for i, (op, low, high) in enumerate(emit):
                if op == p[0]:
                    piece = pltpu.make_async_copy(
                        held[op].at[pl.ds(low, high - low)],
                        emitted[i],
                        out_sems.at[nq // tile + 1 + i],
                    )
                    piece.start()
                    sent.append(piece)
        wait(("q", w))
        wait(("v", w))
        last = n == len(order) - 1
        if not last:
            fetch_step(n + 1)
        if last:
            for i in range(len(extra)):
                wait(("e", i))

        def column(low, size, acc, weight, total, lift):
            for op, src, dst, count, _ in mine:
                for m in range(0, count, step):
                    mm = min(step, count - m)
                    at = pl.ds(dst + m, mm)
                    part = jnp.dot(
                        held[op][src + m : src + m + mm],
                        weight[w, :, pl.ds(low, size)],
                        preferred_element_type=jnp.float32,
                    )
                    if last and final:
                        s = held_extra[0][at]
                        row = lax.broadcasted_iota(jnp.int32, s.shape, 0) + (dst + m)
                        none = jnp.zeros_like(s)
                        s = jnp.concatenate(
                            [jnp.where(row < bound, s, none), jnp.where(row < bound, none, s)],
                            axis=1,
                        )
                        high = s.astype(jnp.bfloat16)
                        rest = (s - high.astype(jnp.float32)).astype(jnp.bfloat16)
                        for half in (high, rest):
                            part = part + jnp.dot(
                                half, lift[:, pl.ds(low, size)], preferred_element_type=jnp.float32
                            )
                    if any(
                        p[2] <= dst + m and dst + m + mm <= p[2] + p[3]
                        for p in pieces
                        if p[4] in order[:n]
                    ):
                        part = part + acc[at, pl.ds(low, size)]
                    if total is not None:
                        part = part + total[at, pl.ds(low, size)]
                    acc[at, pl.ds(low, size)] = part.astype(acc.dtype)

        nothing = (None, None)
        tq, tv = held_totals if (with_total and last) else nothing
        lq, lv = held_extra[1:] if (final and last) else nothing
        if not last:
            column(0, nq, accs[0], wq, None, None)
        else:

            @pl.loop(0, nq // tile)
            def _(j):
                low = pl.multiple_of(j * tile, tile)
                if with_total:
                    total_tile(j).wait()
                column(low, tile, accs[0], wq, tq, lq)
                at = pl.ds(low, tile)
                pltpu.make_async_copy(
                    accs[0].at[:, at], outs[0].at[:, at], out_sems.at[j]
                ).start()

            if with_total:
                total_value.wait()
        column(0, accs[1].shape[1], accs[1], wv, tv, lv)
    end = pltpu.make_async_copy(accs[1], outs[1], out_sems.at[nq // tile])
    end.start()
    for j in range(nq // tile):
        at = pl.ds(j * tile, tile)
        pltpu.make_async_copy(accs[0].at[:, at], outs[0].at[:, at], out_sems.at[j]).wait()
    end.wait()
    for piece in sent:
        piece.wait()


def matmul(blocks, index, pieces, w_query, w_value, total=None, extra=None, emit=(), tile=TILE, step=STEP):
    weights = 1 + max(p[4] for p in pieces)
    rows = max(p[2] + p[3] for p in pieces)
    width = blocks[0].shape[1]
    nq, nv = w_query.shape[1], w_value.shape[1]
    final = extra is not None
    dtype = jnp.bfloat16 if final else jnp.float32
    operands = list(blocks) + [w_query, w_value]
    scratch = [pltpu.VMEM(b.shape, b.dtype) for b in blocks]
    scratch += [pltpu.VMEM((weights, width, nq), jnp.bfloat16), pltpu.VMEM((weights, width, nv), jnp.bfloat16)]
    if total is not None:
        operands += list(total)
        scratch += [pltpu.VMEM(m.shape, m.dtype) for m in total]
    if final:
        operands += list(extra)
        scratch += [pltpu.VMEM(m.shape, m.dtype) for m in extra]
    scratch += [pltpu.VMEM((rows, nq), dtype), pltpu.VMEM((rows, nv), dtype)]
    copies = len(blocks) + 2 * weights + (3 if final else 0)
    scratch += [pltpu.SemaphoreType.DMA((copies,)), pltpu.SemaphoreType.DMA((nq // tile + 1,))]
    scratch += [pltpu.SemaphoreType.DMA((nq // tile + 1 + len(emit),))]
    hbm = pl.BlockSpec(memory_space=pltpu.HBM)
    in_specs = [hbm] * len(operands)
    flops = 2 * sum(p[3] for p in pieces) * width * (nq + nv)
    moved = sum(o.size * o.dtype.itemsize for o in blocks) + weights * width * (nq + nv) * 2
    moved += rows * (nq + nv) * 4 * (2 if total is not None else 1)
    return pl.pallas_call(
        functools.partial(matmul_kernel, pieces, total is not None, final, emit, tile, step),
        in_specs=[pl.BlockSpec(memory_space=pltpu.SMEM)] + in_specs,
        out_specs=[hbm] * (2 + len(emit)),
        out_shape=[jax.ShapeDtypeStruct((rows, nq), dtype), jax.ShapeDtypeStruct((rows, nv), dtype)]
        + [jax.ShapeDtypeStruct((high - low, width), jnp.bfloat16) for _, low, high in emit],
        scratch_shapes=scratch,
        compiler_params=pltpu.CompilerParams(vmem_limit_bytes=44 * 1024 * 1024),
        cost_estimate=pl.CostEstimate(flops=flops, bytes_accessed=moved, transcendentals=0),
    )(index, *operands)


def shrink_kernel(bound, tokens, maps, out, narrow):
    both = jnp.concatenate([maps[0], maps[1]], axis=1)
    sums = jnp.dot(tokens[...], both, preferred_element_type=jnp.float32)
    rank = out.shape[1]
    first = lax.broadcasted_iota(jnp.int32, out.shape, 0) < bound[0]
    out[...] = jnp.where(first, sums[:, :rank], sums[:, rank:])
    narrow[...] = out[...].astype(narrow.dtype)


def partial_shrink(bound, tokens, maps):
    return pl.pallas_call(
        shrink_kernel,
        in_specs=[
            pl.BlockSpec(memory_space=pltpu.SMEM),
            pl.BlockSpec(memory_space=pltpu.VMEM),
            pl.BlockSpec(memory_space=pltpu.VMEM),
        ],
        out_specs=[pl.BlockSpec(memory_space=pltpu.VMEM)] * 2,
        out_shape=[
            jax.ShapeDtypeStruct((tokens.shape[0], maps.shape[2]), jnp.float32),
            jax.ShapeDtypeStruct((tokens.shape[0], maps.shape[2]), jnp.bfloat16),
        ],
        compiler_params=pltpu.CompilerParams(vmem_limit_bytes=24 * 1024 * 1024),
        cost_estimate=pl.CostEstimate(
            flops=4 * tokens.size * maps.shape[2], bytes_accessed=4 << 20, transcendentals=0
        ),
    )(bound, tokens, maps)


def on_device(
    tokens, w_query, w_value, a_both, b_query, b_value, request_adapter, adapter_slot, block_request
):
    rows, width = tokens.shape
    rank = b_query.shape[1]
    mp = lax.axis_index("mp")
    x, z = mp // NZ, mp % NZ
    s = 1 - 2 * (lax.axis_index("dp") % 2)
    bound = (SEG * jnp.sum(block_request[0] == 0)).astype(jnp.int32)

    def place(bx, step):
        return (x ^ bx) * NZ + (z + s * step) % NZ

    def add(blocks, index, pieces, total=None, extra=None, emit=()):
        return matmul(blocks, index, pieces, w_query, w_value, total, extra, emit)

    far, ends, ring = wanted_slots(request_adapter, adapter_slot)
    behind = to_z(tokens, 1)
    ahead = to_z(tokens, -1)
    across = to_x(after(tokens, far))

    other_a = to_core(a_both)
    message = offer(a_both, other_a, after(ends, ring), 4, 4)
    up = to_y(message, 1)
    own_b = jnp.concatenate([after(b_query, message), b_value], axis=2)
    other_b = to_core(own_b)
    total = add([tokens], after(place(0, 0)[None], message, own_b), [(0, 0, 0, rows, 0)])

    ring = after(ring, total[1], other_b)
    down_message = offer(a_both, other_a, ring, 0, 4)
    down = to_y(down_message, -1)
    up_message = offer(a_both, other_a, after(ring, down_message), 4, 4, [(up, 0, 4)])
    up = to_y(up_message, 1)
    first_b_message = offer(own_b, other_b, after(ends, up_message), 4, 4)
    down_b_message = offer(own_b, other_b, after(ring, first_b_message), 0, 4)

    behind = after(behind, down_b_message)
    opposite = to_z(behind, 1)
    cross_message = behind[:EARLY]
    cross_low = to_x(cross_message)
    across = after(across, cross_message)
    across_ahead = to_z(across, -1)

    *total, middle_message, high_message = add(
        [behind],
        after(place(0, -1)[None], cross_message),
        [(0, 0, 0, rows, 0)],
        total,
        emit=((0, EARLY, MIDDLE), (0, MIDDLE, rows)),
    )
    far_message = offer(a_both, other_a, after(ends, total[1]), 2, 2, [(up, 2, 2), (down, 2, 2)])
    far_a = to_far(far_message)
    message = after(first_b_message, far_message)
    up_b = to_y(message, 1)
    total = add(
        [ahead, across],
        after(jnp.stack([place(0, 1), place(1, 0)]), message),
        [(k, 0, 0, rows, k) for k in range(2)],
        total,
    )
    cross_message = after(middle_message, total[1], cross_low)
    cross_middle = to_x(cross_message)
    ends = after(ends, cross_message)

    chosen_a = offer(
        a_both,
        other_a,
        ends,
        0,
        2,
        [(up, 0, 2), (down, 0, 2), (far_a, 0, 2)],
    )
    narrow = lambda v: v.astype(jnp.bfloat16)
    partial, message = partial_shrink(bound[None], tokens, chosen_a)
    half = partial + to_x(message)
    down_b_message = after(down_b_message, message, far_a)
    down_b = to_y(down_b_message, -1)
    ring_b = after(ring, down_b_message)
    up_b_message = offer(own_b, other_b, ring_b, 4, 4, [(up_b, 0, 4)])
    up_b = to_y(up_b_message, 1)

    last_message = after(across_ahead, up_b_message, opposite)
    last = to_z(last_message, -1)
    cross_message = after(high_message, message, cross_middle)
    cross_high = to_x(cross_message)
    message = narrow(half)
    pair = half + to_z(message, 1)
    total = add(
        [opposite],
        after(place(0, 2)[None], cross_message, message),
        [(0, 0, 0, rows, 0)],
        total,
    )
    message = after(narrow(pair), total[1])
    shrink = pair + to_z(message, 2)
    far_b = to_far(
        offer(own_b, other_b, after(ends, message, cross_high), 2, 2, [(up_b, 2, 2), (down_b, 2, 2)])
    )
    total = add(
        [cross_low, cross_middle, across_ahead],
        after(jnp.stack([place(1, -1), place(1, 1)]), message),
        [
            (0, 0, 0, EARLY, 0),
            (1, 0, EARLY, MIDDLE - EARLY, 0),
            (2, 0, 0, rows, 1),
        ],
        total,
    )
    ends = after(ends, total[1])
    wide = offer(
        own_b, other_b, ends, 0, 2, [(up_b, 0, 2), (down_b, 0, 2), (far_b, 0, 2)]
    )
    nq = w_query.shape[1]
    none_q = jnp.zeros((rank, nq), jnp.bfloat16)
    none_v = jnp.zeros((rank, w_value.shape[1]), jnp.bfloat16)
    lift_q = jnp.concatenate([wide[0][:, :nq], none_q, wide[1][:, :nq], none_q])
    lift_v = jnp.concatenate([none_v, wide[0][:, nq:], none_v, wide[1][:, nq:]])

    return tuple(
        add(
            [cross_high, last],
            jnp.stack([place(1, -1), place(1, 2), bound]),
            [(0, 0, MIDDLE, rows - MIDDLE, 0), (1, 0, 0, rows, 1)],
            total,
            (shrink, lift_q, lift_v),
        )
    )


def solution(mesh):
    placed = (
        P("dp", "mp"),
        P(None, "mp"),
        P(None, "mp"),
        P("dp", "mp", None),
        P("dp", None, "mp"),
        P("dp", None, "mp"),
        P("dp", None),
        P(),
        P("dp", None),
    )
    return jax.shard_map(
        on_device,
        mesh=mesh,
        in_specs=placed,
        out_specs=(P("dp", "mp"), P("dp", "mp")),
        check_vma=False,
    )
```

time: 170 us -> 156 us (0.918); the launches traced: 169 us -> 153 us
  waiting for transfers between devices: 44.6 us -> 26.9 us
  starting transfers between devices: 40 us -> 32.9 us
  local copies, waits for them, and re-layouts: 8.27 us -> 13.6 us
  Pallas kernels: 69.8 us -> 72.7 us
    ppermute x3, waiting for transfers between devices: 13.7 us -> 2.03 us  [to_far(): lax.ppermute(v, ('dp', 'mp'), pairs(lambda h, y, c, x, z, s: (1 - h, y, c...]
    ppermute x7, waiting for transfers between devices: 10.1 us -> 2.11 us  [to_z(): lax.ppermute(v, ('dp', 'mp'), pairs(lambda h, y, c, x, z, s: (h, y, c, x,...]
    unnamed x51 -> x43, local copies, waits for them, and re-layouts: 4.42 us -> 11 us
    pallas_call x4 -> x6, Pallas kernels: 44.4 us -> 51 us  [matmul(): pl.pallas_call(functools.partial(matmul_kernel, pieces, total is not None...]
    ppermute x4 -> x5, waiting for transfers between devices: 3.3 us -> 9.65 us  [to_x(): lax.ppermute(v, ('dp', 'mp'), pairs(lambda h, y, c, x, z, s: (h, y, c, 1...]
    ppermute x10 -> x8, waiting for transfers between devices: 17.5 us -> 13.1 us  [to_y(): lax.ppermute(v, ('dp', 'mp'), pairs(lambda h, y, c, x, z, s: (h, y + s *...]
    ppermute x7, starting transfers between devices: 11.4 us -> 7.55 us  [to_z(): lax.ppermute(v, ('dp', 'mp'), pairs(lambda h, y, c, x, z, s: (h, y, c, x,...]
    ppermute x10 -> x8, starting transfers between devices: 17.1 us -> 13.3 us  [to_y(): lax.ppermute(v, ('dp', 'mp'), pairs(lambda h, y, c, x, z, s: (h, y + s *...]
  transfers between devices with their start and end apart: 26 -> 25, of which waited for: 8 -> 10; matrix products, arithmetic and copies ran while one was open for 5% -> 6% of each run, Pallas kernels for 35% -> 40%
where the time goes in v2:
time: 156 us; the launch traced here: 153 us
  Pallas kernels  72.7 us (47%)
  starting transfers between devices  32.9 us (21%)
  waiting for transfers between devices  26.9 us (17%)
  local copies, waits for them, and re-layouts  13.6 us (9%)
  other arithmetic  5.37 us (3%)
  between operations  1.77 us (1%)
    pallas_call x6, Pallas kernels, matmul(): pl.pallas_call(functools.partial(matmul_kernel, pieces, total is not None...  51 us
    pallas_call x10, Pallas kernels, offer(): pl.pallas_call(functools.partial(offer_kernel, [a[1:] for a in adds], off...  20.3 us
    ppermute x8, starting transfers between devices, to_y(): lax.ppermute(v, ('dp', 'mp'), pairs(lambda h, y, c, x, z, s: (h, y + s *...  13.3 us
    ppermute x8, waiting for transfers between devices, to_y(): lax.ppermute(v, ('dp', 'mp'), pairs(lambda h, y, c, x, z, s: (h, y + s *...  13.1 us
    unnamed x43, local copies, waits for them, and re-layouts  11 us
    ppermute x5, waiting for transfers between devices, to_x(): lax.ppermute(v, ('dp', 'mp'), pairs(lambda h, y, c, x, z, s: (h, y, c, 1...  9.65 us
    ppermute x3, starting transfers between devices, to_far(): lax.ppermute(v, ('dp', 'mp'), pairs(lambda h, y, c, x, z, s: (1 - h, y, c...  7.9 us
    ppermute x7, starting transfers between devices, to_z(): lax.ppermute(v, ('dp', 'mp'), pairs(lambda h, y, c, x, z, s: (h, y, c, x,...  7.55 us
  transfers between devices with their start and end apart: 25, of which 10 were waited for; matrix products, arithmetic and copies ran while one was open for 6% of the time, Pallas kernels for 40%

profile of v2, /device:TPU:0, one launch (start us, length us, event | category | flops | bytes accessed | tf_op | source)
XLA Modules:
  0.0 153.2 jit_solution(12481373115383459635)
XLA Ops:
  0.7 2.1 %collective-permute-start = (bf16[1024,1024]{1,0:T(8,128)(2,1)}, bf16[1024,1024]{1,0:T(8,128)(2,1)}, u32[]{:S(2)}, u32[]{:S(2)}) collective-permute-start(bf16[1024,1024]{1,0:T(8,128)(2,1)} %tokens.1), channel_id=1, source_target_pairs={{0,1},{1,2},{2,3},{3,0},{4,5},{5,6},{6,7},{7,4},{8,11},{9,8},{10,9... | collective-permute-start | bytes 6291464 | tf_op jit(solution)/shard_map/ppermute | solution.py:30
  3.6 3.1 %collective-permute-start.1 = (s32[2]{0:T(128)S(1)}, s32[2]{0:T(128)S(1)}, u32[]{:S(2)}, u32[]{:S(2)}) collective-permute-start(s32[2]{0:T(128)S(1)} %fusion.2), channel_id=1, source_target_pairs={{0,64},{1,65},{2,66},{3,67},{4,68},{5,69},{6,70},{7,71},{8,72},{9,... | collective-permute-start | bytes 32 | tf_op jit(solution)/shard_map/ppermute | solution.py:50
  6.7 2.0 %collective-permute-done.1 = s32[2]{0:T(128)S(1)} collective-permute-done((s32[2]{0:T(128)S(1)}, s32[2]{0:T(128)S(1)}, u32[]{:S(2)}, u32[]{:S(2)}) %collective-permute-start.1) | collective-permute-done | bytes 40 | tf_op jit(solution)/shard_map/ppermute | solution.py:50
  10.3 2.1 %collective-permute-start.9 = (bf16[1024,1024]{1,0:T(8,128)(2,1)}, bf16[1024,1024]{1,0:T(8,128)(2,1)}, u32[]{:S(2)}, u32[]{:S(2)}) collective-permute-start(bf16[1024,1024]{1,0:T(8,128)(2,1)} %tokens.1), channel_id=1, source_target_pairs={{0,3},{1,0},{2,1},{3,2},{4,7},{5,4},{6,5},{7,6},{8,9},{9,10},{10,1... | collective-permute-start | bytes 6291464 | tf_op jit(solution)/shard_map/ppermute | solution.py:30
  12.5 3.2 %collective-permute-start.2 = (s32[4]{0:T(128)S(1)}, s32[4]{0:T(128)S(1)}, u32[]{:S(2)}, u32[]{:S(2)}) collective-permute-start(s32[4]{0:T(128)S(1)} %pad_add_fusion.1), channel_id=1, source_target_pairs={{0,32},{1,33},{2,34},{3,35},{4,36},{5,37},{6,38},{7,39},{8,40},{9,... | collective-permute-start | bytes 56 | tf_op jit(solution)/shard_map/ppermute | solution.py:36
  15.7 1.9 %collective-permute-done.2 = s32[4]{0:T(128)S(1)} collective-permute-done((s32[4]{0:T(128)S(1)}, s32[4]{0:T(128)S(1)}, u32[]{:S(2)}, u32[]{:S(2)}) %collective-permute-start.2) | collective-permute-done | bytes 48 | tf_op jit(solution)/shard_map/ppermute | solution.py:36
  19.3 3.1 %collective-permute-done.3 = s32[8]{0:T(128)S(1)} collective-permute-done((s32[8]{0:T(128)S(1)}, s32[8]{0:T(128)S(1)}, u32[]{:S(2)}, u32[]{:S(2)}) %collective-permute-start.3) | collective-permute-done | bytes 64 | tf_op jit(solution)/shard_map/ppermute | solution.py:36
  23.9 1.7 %shard_map.104 = bf16[4,1024,128]{2,1,0:T(8,128)(2,1)} custom-call(s32[9]{0:T(128)S(1)} %add_add_fusion.codes, bf16[5,1024,128]{2,1,0:T(8,128)(2,1)S(1)} %copy-done.1, bf16[5,1024,128]{2,1,0:T(8,128)(2,1)S(1)} %collective-permute-done.4.other), custom_call_target="tpu_custom_call" | custom-call | flops 655360 | bytes 4194304 | tf_op jit(solution)/shard_map/pallas_call | solution.py:101
  29.3 6.3 %shard_map.105 = (f32[1024,1024]{1,0:T(8,128)S(1)}, f32[1024,128]{1,0:T(8,128)S(1)}) custom-call(s32[1]{0:T(128)} %bitcast.6.idx, bf16[1024,1024]{1,0:T(8,128)(2,1)S(1)} %copy-done.7, bf16[8192,1024]{1,0:T(8,128)(2,1)} %refs_2_.9, bf16[8192,128]{1,0:T(8,128)(2,1)S(1)} %copy-done), custom_call_target="tpu_custom_call" | custom-call | flops 2415919104 | bytes 9175040 | tf_op jit(solution)/shard_map/pallas_call | solution.py:289
  36.3 2.2 %shard_map.106 = bf16[4,1024,128]{2,1,0:T(8,128)(2,1)} custom-call(s32[9]{0:T(128)S(1)} %pad_add_fusion.3.codes, bf16[5,1024,128]{2,1,0:T(8,128)(2,1)S(1)} %copy-done.2, bf16[5,1024,128]{2,1,0:T(8,128)(2,1)S(1)} %copy-done.4), custom_call_target="tpu_custom_call" | custom-call | flops 655360 | bytes 4194304 | tf_op jit(solution)/shard_map/pallas_call | solution.py:101
  38.5 2.8 %collective-permute-start.8 = (bf16[4,1024,128]{2,1,0:T(8,128)(2,1)}, bf16[4,1024,128]{2,1,0:T(8,128)(2,1)}, u32[]{:S(2)}, u32[]{:S(2)}) collective-permute-start(bf16[4,1024,128]{2,1,0:T(8,128)(2,1)} %shard_map.106), channel_id=1, source_target_pairs={{0,48},{1,49},{2,50},{3,51},{4,52},{5,53},{6,54},{7,55},{8,24},{9,... | collective-permute-start | bytes 3145736 | tf_op jit(solution)/shard_map/ppermute | solution.py:36
  42.0 2.6 %shard_map.107 = bf16[4,1024,128]{2,1,0:T(8,128)(2,1)} custom-call(s32[9]{0:T(128)S(1)} %pad_add_fusion.3.codes, bf16[5,1024,128]{2,1,0:T(8,128)(2,1)S(1)} %copy-done.2, bf16[5,1024,128]{2,1,0:T(8,128)(2,1)S(1)} %copy-done.4, bf16[4,1024,128]{2,1,0:T(8,128)(2,1)} %collective-permute-done.6.refs_0_), custom_call_target="tpu_custom_call" | custom-call | flops 655360 | bytes 4194304 | tf_op jit(solution)/shard_map/pallas_call | solution.py:101
  44.5 2.3 %shard_map.108 = bf16[4,64,1152]{2,1,0:T(8,128)(2,1)} custom-call(s32[9]{0:T(128)S(1)} %add_add_fusion.codes, bf16[5,64,1152]{2,1,0:T(8,128)(2,1)} %constant_dynamic-update-slice_fusion.own, bf16[5,64,1152]{2,1,0:T(8,128)(2,1)} %collective-permute-done.5.other), custom_call_target="tpu_custom_call" | custom-call | flops 368640 | bytes 2359296 | tf_op jit(solution)/shard_map/pallas_call | solution.py:101
  49.1 1.9 %slice.23 = bf16[256,1024]{1,0:T(8,128)(2,1)} slice(bf16[1024,1024]{1,0:T(8,128)(2,1)} %collective-permute-done.refs_0_), slice={[0:256], [0:1024]} | slice | bytes 1048576 | tf_op jit(solution)/shard_map/slice | solution.py:368
  51.0 6.3 %collective-permute-done.10.refs_1_ = bf16[1024,1024]{1,0:T(8,128)(2,1)} collective-permute-done((bf16[1024,1024]{1,0:T(8,128)(2,1)}, bf16[1024,1024]{1,0:T(8,128)(2,1)}, u32[]{:S(2)}, u32[]{:S(2)}) %collective-permute-start.10) | collective-permute-done | bytes 2097184 | tf_op jit(solution)/shard_map/ppermute | solution.py:42
  58.2 4.7 %collective-permute-done.8.refs_1_ = bf16[4,1024,128]{2,1,0:T(8,128)(2,1)} collective-permute-done((bf16[4,1024,128]{2,1,0:T(8,128)(2,1)}, bf16[4,1024,128]{2,1,0:T(8,128)(2,1)}, u32[]{:S(2)}, u32[]{:S(2)}) %collective-permute-start.8) | collective-permute-done | bytes 1048608 | tf_op jit(solution)/shard_map/ppermute | solution.py:36
  64.4 7.7 %shard_map.110 = (f32[1024,1024]{1,0:T(8,128)}, f32[1024,128]{1,0:T(8,128)S(1)}, bf16[256,1024]{1,0:T(8,128)(2,1)}, bf16[512,1024]{1,0:T(8,128)(2,1)}) custom-call(s32[1]{0:T(128)} %bitcast.3.idx, bf16[1024,1024]{1,0:T(8,128)(2,1)} %collective-permute-done.refs_0_, bf16[8192,1024]{1,0:T(8,128)(2,1)} %refs_2_.9, bf16[8192,128]{1,0:T(8,128)(2,1)S(1)} %copy-done, ...), custom_call_target="tpu_custom_call" | custom-call | flops 2415919104 | bytes 13893632 | tf_op jit(solution)/shard_map/pallas_call | solution.py:289
  72.1 2.5 %shard_map.111 = bf16[2,1024,128]{2,1,0:T(8,128)(2,1)} custom-call(s32[9]{0:T(128)S(1)} %add_add_fusion.codes, bf16[5,1024,128]{2,1,0:T(8,128)(2,1)S(1)} %copy-done.2, bf16[5,1024,128]{2,1,0:T(8,128)(2,1)S(1)} %copy-done.5, bf16[4,1024,128]{2,1,0:T(8,128)(2,1)} %collective-permute-done.7.refs_0_, bf16[4,1024,128]{2,1,0:T(8,128)(2,1)} %collective-permute-done.8.refs_1_), custom_call_target="tpu_custom_call" | custom-call | flops 655360 | bytes 2097152 | tf_op jit(solution)/shard_map/pallas_call | solution.py:101
  74.6 3.2 %collective-permute-start.12 = (bf16[2,1024,128]{2,1,0:T(8,128)(2,1)}, bf16[2,1024,128]{2,1,0:T(8,128)(2,1)}, u32[]{:S(2)}, u32[]{:S(2)}) collective-permute-start(bf16[2,1024,128]{2,1,0:T(8,128)(2,1)} %shard_map.111), channel_id=1, source_target_pairs={{0,64},{1,65},{2,66},{3,67},{4,68},{5,69},{6,70},{7,71},{8,72},{9,... | collective-permute-start | bytes 1572872 | tf_op jit(solution)/shard_map/ppermute | solution.py:50
  77.8 9.8 %shard_map.112 = (f32[1024,1024]{1,0:T(8,128)}, f32[1024,128]{1,0:T(8,128)S(1)}) custom-call(s32[2]{0:T(128)S(1)} %pad_add_fusion.4.idx, bf16[1024,1024]{1,0:T(8,128)(2,1)} %collective-permute-done.9.refs_0_, bf16[1024,1024]{1,0:T(8,128)(2,1)} %collective-permute-done.10.refs_1_, bf16[8192,1024]{1,0:T(8,128)(2,1)} %refs_2_.9, bf16[8192,128]{1,0:T(8,128)(2,1)S(1)} %copy-done, ...), custom_call_target="tpu_custom_call" | custom-call | flops 4831838208 | bytes 18350080 | tf_op jit(solution)/shard_map/pallas_call | solution.py:289
  92.7 2.0 %shard_map.113.maps = bf16[2,1024,128]{2,1,0:T(8,128)(2,1)S(1)} custom-call(s32[9]{0:T(128)S(1)} %add_add_fusion.codes, bf16[5,1024,128]{2,1,0:T(8,128)(2,1)S(1)} %copy-done.2, bf16[5,1024,128]{2,1,0:T(8,128)(2,1)S(1)} %copy-done.6, bf16[4,1024,128]{2,1,0:T(8,128)(2,1)} %collective-permute-done.7.refs_0_, ...), custom_call_target="tpu_custom_call" | custom-call | flops 655360 | bytes 2097152 | tf_op jit(solution)/shard_map/pallas_call | solution.py:101
  99.5 2.8 %collective-permute-done.16.refs_0_ = bf16[4,64,1152]{2,1,0:T(8,128)(2,1)} collective-permute-done((bf16[4,64,1152]{2,1,0:T(8,128)(2,1)}, bf16[4,64,1152]{2,1,0:T(8,128)(2,1)}, u32[]{:S(2)}, u32[]{:S(2)}) %collective-permute-start.16) | collective-permute-done | bytes 589856 | tf_op jit(solution)/shard_map/ppermute | solution.py:36
  102.4 5.0 %collective-permute-start.23 = (bf16[4,64,1152]{2,1,0:T(8,128)(2,1)}, bf16[4,64,1152]{2,1,0:T(8,128)(2,1)S(1)}, u32[]{:S(2)}, u32[]{:S(2)}) collective-permute-start(bf16[4,64,1152]{2,1,0:T(8,128)(2,1)} %copy-done.11), channel_id=1, source_target_pairs={{0,48},{1,49},{2,50},{3,51},{4,52},{5,53},{6,54},{7,55},{8,24},{9,... | collective-permute-start | bytes 1769480 | tf_op jit(solution)/shard_map/ppermute | solution.py:36
  107.4 2.4 %shard_map.115 = bf16[4,64,1152]{2,1,0:T(8,128)(2,1)} custom-call(s32[9]{0:T(128)S(1)} %pad_add_fusion.3.codes, bf16[5,64,1152]{2,1,0:T(8,128)(2,1)} %constant_dynamic-update-slice_fusion.own, bf16[5,64,1152]{2,1,0:T(8,128)(2,1)} %collective-permute-done.5.other, bf16[4,64,1152]{2,1,0:T(8,128)(2,1)} %collective-permute-done.16.refs_0_), custom_call_target="tpu_custom_call" | custom-call | flops 368640 | bytes 2359296 | tf_op jit(solution)/shard_map/pallas_call | solution.py:101
  109.8 2.1 %collective-permute-start.18 = (bf16[1024,1024]{1,0:T(8,128)(2,1)}, bf16[1024,1024]{1,0:T(8,128)(2,1)}, u32[]{:S(2)}, u32[]{:S(2)}) collective-permute-start(bf16[1024,1024]{1,0:T(8,128)(2,1)} %collective-permute-done.15.refs_2_), channel_id=1, source_target_pairs={{0,3},{1,0},{2,1},{3,2},{4,7},{5,4},{6,5},{7,6},{8,9},{9,10},{10,1... | collective-permute-start | bytes 6291464 | tf_op jit(solution)/shard_map/ppermute | solution.py:30
  114.1 7.3 %shard_map.116 = (f32[1024,1024]{1,0:T(8,128)S(1)}, f32[1024,128]{1,0:T(8,128)S(1)}) custom-call(s32[1]{0:T(128)} %bitcast.10.idx, bf16[1024,1024]{1,0:T(8,128)(2,1)} %collective-permute-done.17.refs_0_, bf16[8192,1024]{1,0:T(8,128)(2,1)} %refs_2_.9, bf16[8192,128]{1,0:T(8,128)(2,1)S(1)} %copy-done, f32[1024,1024]{1,0:T(8,128)} %get-tuple-element.71.refs_3_, ...), custom_call_target="tpu_custom_call" | custom-call | flops 2415919104 | bytes 13893632 | tf_op jit(solution)/shard_map/pallas_call | solution.py:289
  121.4 2.1 %collective-permute-done.20 = bf16[1024,128]{1,0:T(8,128)(2,1)} collective-permute-done((bf16[1024,128]{1,0:T(8,128)(2,1)S(1)}, bf16[1024,128]{1,0:T(8,128)(2,1)}, u32[]{:S(2)}, u32[]{:S(2)}) %collective-permute-start.20) | collective-permute-done | bytes 262176 | tf_op jit(solution)/shard_map/ppermute | solution.py:30
  125.0 1.9 %collective-permute-done.14.refs_0_ = bf16[512,1024]{1,0:T(8,128)(2,1)} collective-permute-done((bf16[512,1024]{1,0:T(8,128)(2,1)}, bf16[512,1024]{1,0:T(8,128)(2,1)}, u32[]{:S(2)}, u32[]{:S(2)}) %collective-permute-start.14) | collective-permute-done | bytes 1048608 | tf_op jit(solution)/shard_map/ppermute | solution.py:42
  128.5 1.6 %collective-permute-start.24 = (bf16[2,64,1152]{2,1,0:T(8,128)(2,1)S(1)}, bf16[2,64,1152]{2,1,0:T(8,128)(2,1)S(1)}, u32[]{:S(2)}, u32[]{:S(2)}) collective-permute-start(bf16[2,64,1152]{2,1,0:T(8,128)(2,1)S(1)} %shard_map.118), channel_id=1, source_target_pairs={{0,64},{1,65},{2,66},{3,67},{4,68},{5,69},{6,70},{7,71},{8,72},{9,... | collective-permute-start | bytes 884744 | tf_op jit(solution)/shard_map/ppermute | solution.py:50
  130.1 9.1 %shard_map.117 = (f32[1024,1024]{1,0:T(8,128)}, f32[1024,128]{1,0:T(8,128)S(1)}) custom-call(s32[2]{0:T(128)S(1)} %pad_add_fusion.5.idx, bf16[256,1024]{1,0:T(8,128)(2,1)S(1)} %copy-done.13, bf16[256,1024]{1,0:T(8,128)(2,1)} %collective-permute-done.13.refs_1_, bf16[1024,1024]{1,0:T(8,128)(2,1)} %collective-permute-done.15.refs_2_, ...), custom_call_target="tpu_custom_call" | custom-call | flops 3623878656 | bytes 17301504 | tf_op jit(solution)/shard_map/pallas_call | solution.py:289
  140.4 1.6 %shard_map.119 = bf16[2,64,1152]{2,1,0:T(8,128)(2,1)S(1)} custom-call(s32[9]{0:T(128)S(1)} %add_add_fusion.codes, bf16[5,64,1152]{2,1,0:T(8,128)(2,1)} %constant_dynamic-update-slice_fusion.own, bf16[5,64,1152]{2,1,0:T(8,128)(2,1)} %collective-permute-done.5.other, bf16[4,64,1152]{2,1,0:T(8,128)(2,1)} %collective-permute-done.22.refs_0_, ...), custom_call_target="tpu_custom_call" | custom-call | flops 368640 | bytes 1179648 | tf_op jit(solution)/shard_map/pallas_call | solution.py:101
  142.2 10.8 %shard_map.120 = (bf16[1024,1024]{1,0:T(8,128)(2,1)}, bf16[1024,128]{1,0:T(8,128)(2,1)}) custom-call(s32[3]{0:T(128)S(1)} %pad_add_fusion.idx, bf16[512,1024]{1,0:T(8,128)(2,1)} %collective-permute-done.14.refs_0_, bf16[1024,1024]{1,0:T(8,128)(2,1)} %collective-permute-done.18.refs_1_, bf16[8192,1024]{1,0:T(8,128)(2,1)} %refs_2_.9, ...), custom_call_target="tpu_custom_call" | custom-call | flops 3623878656 | bytes 17301504 | tf_op jit(solution)/shard_map/pallas_call | solution.py:289
  (101 shorter events, 31.4 us)
Async XLA Ops:
  0.6 21.8 %collective-permute-start.4 = (bf16[5,1024,128]{2,1,0:T(8,128)(2,1)}, bf16[5,1024,128]{2,1,0:T(8,128)(2,1)S(1)}, u32[]{:S(2)}, u32[]{:S(2)}) collective-permute-start(bf16[5,1024,128]{2,1,0:T(8,128)(2,1)} %own.9), channel_id=1, source_target_pairs={{0,8},{1,9},{2,10},{3,11},{4,12},{5,13},{6,14},{7,15},{8,0},{9,1},... | collective-permute-start | bytes 3932168 | tf_op jit(solution)/shard_map/ppermute | solution.py:46
  0.7 48.4 %collective-permute-start = (bf16[1024,1024]{1,0:T(8,128)(2,1)}, bf16[1024,1024]{1,0:T(8,128)(2,1)}, u32[]{:S(2)}, u32[]{:S(2)}) collective-permute-start(bf16[1024,1024]{1,0:T(8,128)(2,1)} %tokens.1), channel_id=1, source_target_pairs={{0,1},{1,2},{2,3},{3,0},{4,5},{5,6},{6,7},{7,4},{8,11},{9,8},{10,9... | collective-permute-start | bytes 6291464 | tf_op jit(solution)/shard_map/ppermute | solution.py:30
  3.6 5.1 %collective-permute-start.1 = (s32[2]{0:T(128)S(1)}, s32[2]{0:T(128)S(1)}, u32[]{:S(2)}, u32[]{:S(2)}) collective-permute-start(s32[2]{0:T(128)S(1)} %fusion.2), channel_id=1, source_target_pairs={{0,64},{1,65},{2,66},{3,67},{4,68},{5,69},{6,70},{7,71},{8,72},{9,... | collective-permute-start | bytes 32 | tf_op jit(solution)/shard_map/ppermute | solution.py:50
  8.8 48.5 %collective-permute-start.10 = (bf16[1024,1024]{1,0:T(8,128)(2,1)}, bf16[1024,1024]{1,0:T(8,128)(2,1)}, u32[]{:S(2)}, u32[]{:S(2)}) collective-permute-start(bf16[1024,1024]{1,0:T(8,128)(2,1)} %tokens.1), channel_id=1, source_target_pairs={{0,4},{1,5},{2,6},{3,7},{4,0},{5,1},{6,2},{7,3},{8,12},{9,13},{10,... | collective-permute-start | bytes 6291464 | tf_op jit(solution)/shard_map/ppermute | solution.py:42
  10.3 67.6 %collective-permute-start.9 = (bf16[1024,1024]{1,0:T(8,128)(2,1)}, bf16[1024,1024]{1,0:T(8,128)(2,1)}, u32[]{:S(2)}, u32[]{:S(2)}) collective-permute-start(bf16[1024,1024]{1,0:T(8,128)(2,1)} %tokens.1), channel_id=1, source_target_pairs={{0,3},{1,0},{2,1},{3,2},{4,7},{5,4},{6,5},{7,6},{8,9},{9,10},{10,1... | collective-permute-start | bytes 6291464 | tf_op jit(solution)/shard_map/ppermute | solution.py:30
  12.5 5.1 %collective-permute-start.2 = (s32[4]{0:T(128)S(1)}, s32[4]{0:T(128)S(1)}, u32[]{:S(2)}, u32[]{:S(2)}) collective-permute-start(s32[4]{0:T(128)S(1)} %pad_add_fusion.1), channel_id=1, source_target_pairs={{0,32},{1,33},{2,34},{3,35},{4,36},{5,37},{6,38},{7,39},{8,40},{9,... | collective-permute-start | bytes 56 | tf_op jit(solution)/shard_map/ppermute | solution.py:36
  17.6 4.8 %collective-permute-start.3 = (s32[8]{0:T(128)S(1)}, s32[8]{0:T(128)S(1)}, u32[]{:S(2)}, u32[]{:S(2)}) collective-permute-start(s32[8]{0:T(128)S(1)} %pad_add_fusion.2), channel_id=1, source_target_pairs={{0,16},{1,17},{2,18},{3,19},{4,20},{5,21},{6,22},{7,23},{8,56},{9,... | collective-permute-start | bytes 104 | tf_op jit(solution)/shard_map/ppermute | solution.py:36
  25.6 16.3 %collective-permute-start.6 = (bf16[4,1024,128]{2,1,0:T(8,128)(2,1)}, bf16[4,1024,128]{2,1,0:T(8,128)(2,1)}, u32[]{:S(2)}, u32[]{:S(2)}) collective-permute-start(bf16[4,1024,128]{2,1,0:T(8,128)(2,1)} %shard_map.104), channel_id=1, source_target_pairs={{0,16},{1,17},{2,18},{3,19},{4,20},{5,21},{6,22},{7,23},{8,56},{9,... | collective-permute-start | bytes 3145736 | tf_op jit(solution)/shard_map/ppermute | solution.py:36
  27.7 8.7 %collective-permute-start.5 = (bf16[5,64,1152]{2,1,0:T(8,128)(2,1)}, bf16[5,64,1152]{2,1,0:T(8,128)(2,1)}, u32[]{:S(2)}, u32[]{:S(2)}) collective-permute-start(bf16[5,64,1152]{2,1,0:T(8,128)(2,1)} %constant_dynamic-update-slice_fusion.own), channel_id=1, source_target_pairs={{0,8},{1,9},{2,10},{3,11},{4,12},{5,13},{6,14},{7,15},{8,0},{9,1},... | collective-permute-start | bytes 2211848 | tf_op jit(solution)/shard_map/ppermute | solution.py:46
  29.3 7.1 %copy-start.2 = (bf16[5,1024,128]{2,1,0:T(8,128)(2,1)S(1)}, bf16[5,1024,128]{2,1,0:T(8,128)(2,1)}, u32[]{:S(2)}) copy-start(bf16[5,1024,128]{2,1,0:T(8,128)(2,1)} %own.9) | copy-start | bytes 3932164
  29.3 7.1 %copy-start.4 = (bf16[5,1024,128]{2,1,0:T(8,128)(2,1)S(1)}, bf16[5,1024,128]{2,1,0:T(8,128)(2,1)}, u32[]{:S(2)}) copy-start(bf16[5,1024,128]{2,1,0:T(8,128)(2,1)} %copy-done.3) | copy-start | bytes 3932164
  36.3 8.2 %copy-start.9 = (f32[1024,1024]{1,0:T(8,128)}, f32[1024,1024]{1,0:T(8,128)S(1)}, u32[]{:S(2)}) copy-start(f32[1024,1024]{1,0:T(8,128)S(1)} %get-tuple-element.51.refs_3_) | copy-start | bytes 12582916
  38.5 24.4 %collective-permute-start.8 = (bf16[4,1024,128]{2,1,0:T(8,128)(2,1)}, bf16[4,1024,128]{2,1,0:T(8,128)(2,1)}, u32[]{:S(2)}, u32[]{:S(2)}) collective-permute-start(bf16[4,1024,128]{2,1,0:T(8,128)(2,1)} %shard_map.106), channel_id=1, source_target_pairs={{0,48},{1,49},{2,50},{3,51},{4,52},{5,53},{6,54},{7,55},{8,24},{9,... | collective-permute-start | bytes 3145736 | tf_op jit(solution)/shard_map/ppermute | solution.py:36
  44.5 27.6 %collective-permute-start.7 = (bf16[4,1024,128]{2,1,0:T(8,128)(2,1)}, bf16[4,1024,128]{2,1,0:T(8,128)(2,1)}, u32[]{:S(2)}, u32[]{:S(2)}) collective-permute-start(bf16[4,1024,128]{2,1,0:T(8,128)(2,1)} %shard_map.107), channel_id=1, source_target_pairs={{0,16},{1,17},{2,18},{3,19},{4,20},{5,21},{6,22},{7,23},{8,56},{9,... | collective-permute-start | bytes 3145736 | tf_op jit(solution)/shard_map/ppermute | solution.py:36
  51.0 58.8 %collective-permute-start.17 = (bf16[1024,1024]{1,0:T(8,128)(2,1)}, bf16[1024,1024]{1,0:T(8,128)(2,1)}, u32[]{:S(2)}, u32[]{:S(2)}) collective-permute-start(bf16[1024,1024]{1,0:T(8,128)(2,1)} %collective-permute-done.refs_0_), channel_id=1, source_target_pairs={{0,1},{1,2},{2,3},{3,0},{4,5},{5,6},{6,7},{7,4},{8,11},{9,8},{10,9... | collective-permute-start | bytes 6291464 | tf_op jit(solution)/shard_map/ppermute | solution.py:30
  57.3 52.5 %collective-permute-start.15 = (bf16[1024,1024]{1,0:T(8,128)(2,1)}, bf16[1024,1024]{1,0:T(8,128)(2,1)}, u32[]{:S(2)}, u32[]{:S(2)}) collective-permute-start(bf16[1024,1024]{1,0:T(8,128)(2,1)} %collective-permute-done.10.refs_1_), channel_id=1, source_target_pairs={{0,3},{1,0},{2,1},{3,2},{4,7},{5,4},{6,5},{7,6},{8,9},{9,10},{10,1... | collective-permute-start | bytes 6291464 | tf_op jit(solution)/shard_map/ppermute | solution.py:30
  62.9 25.6 %collective-permute-start.11 = (bf16[256,1024]{1,0:T(8,128)(2,1)}, bf16[256,1024]{1,0:T(8,128)(2,1)S(1)}, u32[]{:S(2)}, u32[]{:S(2)}) collective-permute-start(bf16[256,1024]{1,0:T(8,128)(2,1)} %slice.23), channel_id=1, source_target_pairs={{0,4},{1,5},{2,6},{3,7},{4,0},{5,1},{6,2},{7,3},{8,12},{9,13},{10,... | collective-permute-start | bytes 1572872 | tf_op jit(solution)/shard_map/ppermute | solution.py:42
  64.4 7.7 %copy-start.5 = (bf16[5,1024,128]{2,1,0:T(8,128)(2,1)S(1)}, bf16[5,1024,128]{2,1,0:T(8,128)(2,1)}, u32[]{:S(2)}) copy-start(bf16[5,1024,128]{2,1,0:T(8,128)(2,1)} %copy-done.3) | copy-start | bytes 3932164
  74.6 16.8 %collective-permute-start.12 = (bf16[2,1024,128]{2,1,0:T(8,128)(2,1)}, bf16[2,1024,128]{2,1,0:T(8,128)(2,1)}, u32[]{:S(2)}, u32[]{:S(2)}) collective-permute-start(bf16[2,1024,128]{2,1,0:T(8,128)(2,1)} %shard_map.111), channel_id=1, source_target_pairs={{0,64},{1,65},{2,66},{3,67},{4,68},{5,69},{6,70},{7,71},{8,72},{9,... | collective-permute-start | bytes 1572872 | tf_op jit(solution)/shard_map/ppermute | solution.py:50
  77.8 12.3 %copy-start.20 = (s32[1,8]{1,0:T(1,128)S(1)}, s32[1,8]{1,0:T(1,128)}, u32[]{:S(2)}) copy-start(s32[1,8]{1,0:T(1,128)} %param.17) | copy-start | bytes 100
  89.3 10.2 %collective-permute-start.13 = (bf16[256,1024]{1,0:T(8,128)(2,1)}, bf16[256,1024]{1,0:T(8,128)(2,1)}, u32[]{:S(2)}, u32[]{:S(2)}) collective-permute-start(bf16[256,1024]{1,0:T(8,128)(2,1)} %get-tuple-element.62), channel_id=1, source_target_pairs={{0,4},{1,5},{2,6},{3,7},{4,0},{5,1},{6,2},{7,3},{8,12},{9,13},{10,... | collective-permute-start | bytes 1572872 | tf_op jit(solution)/shard_map/ppermute | solution.py:42
  89.9 12.5 %collective-permute-start.16 = (bf16[4,64,1152]{2,1,0:T(8,128)(2,1)}, bf16[4,64,1152]{2,1,0:T(8,128)(2,1)}, u32[]{:S(2)}, u32[]{:S(2)}) collective-permute-start(bf16[4,64,1152]{2,1,0:T(8,128)(2,1)} %shard_map.108), channel_id=1, source_target_pairs={{0,16},{1,17},{2,18},{3,19},{4,20},{5,21},{6,22},{7,23},{8,56},{9,... | collective-permute-start | bytes 1769480 | tf_op jit(solution)/shard_map/ppermute | solution.py:36
  96.5 15.4 %collective-permute-start.19 = (bf16[1024,128]{1,0:T(8,128)(2,1)}, bf16[1024,128]{1,0:T(8,128)(2,1)}, u32[]{:S(2)}, u32[]{:S(2)}) collective-permute-start(bf16[1024,128]{1,0:T(8,128)(2,1)} %get-tuple-element.64), channel_id=1, source_target_pairs={{0,4},{1,5},{2,6},{3,7},{4,0},{5,1},{6,2},{7,3},{8,12},{9,13},{10,... | collective-permute-start | bytes 786440 | tf_op jit(solution)/shard_map/ppermute | solution.py:42
  99.5 27.4 %collective-permute-start.14 = (bf16[512,1024]{1,0:T(8,128)(2,1)}, bf16[512,1024]{1,0:T(8,128)(2,1)}, u32[]{:S(2)}, u32[]{:S(2)}) collective-permute-start(bf16[512,1024]{1,0:T(8,128)(2,1)} %get-tuple-element.65), channel_id=1, source_target_pairs={{0,4},{1,5},{2,6},{3,7},{4,0},{5,1},{6,2},{7,3},{8,12},{9,13},{10,... | collective-permute-start | bytes 3145736 | tf_op jit(solution)/shard_map/ppermute | solution.py:42
  102.4 24.5 %collective-permute-start.23 = (bf16[4,64,1152]{2,1,0:T(8,128)(2,1)}, bf16[4,64,1152]{2,1,0:T(8,128)(2,1)S(1)}, u32[]{:S(2)}, u32[]{:S(2)}) collective-permute-start(bf16[4,64,1152]{2,1,0:T(8,128)(2,1)} %copy-done.11), channel_id=1, source_target_pairs={{0,48},{1,49},{2,50},{3,51},{4,52},{5,53},{6,54},{7,55},{8,24},{9,... | collective-permute-start | bytes 1769480 | tf_op jit(solution)/shard_map/ppermute | solution.py:36
  109.8 17.1 %collective-permute-start.22 = (bf16[4,64,1152]{2,1,0:T(8,128)(2,1)}, bf16[4,64,1152]{2,1,0:T(8,128)(2,1)}, u32[]{:S(2)}, u32[]{:S(2)}) collective-permute-start(bf16[4,64,1152]{2,1,0:T(8,128)(2,1)} %shard_map.115), channel_id=1, source_target_pairs={{0,16},{1,17},{2,18},{3,19},{4,20},{5,21},{6,22},{7,23},{8,56},{9,... | collective-permute-start | bytes 1769480 | tf_op jit(solution)/shard_map/ppermute | solution.py:36
  109.8 32.4 %collective-permute-start.18 = (bf16[1024,1024]{1,0:T(8,128)(2,1)}, bf16[1024,1024]{1,0:T(8,128)(2,1)}, u32[]{:S(2)}, u32[]{:S(2)}) collective-permute-start(bf16[1024,1024]{1,0:T(8,128)(2,1)} %collective-permute-done.15.refs_2_), channel_id=1, source_target_pairs={{0,3},{1,0},{2,1},{3,2},{4,7},{5,4},{6,5},{7,6},{8,9},{9,10},{10,1... | collective-permute-start | bytes 6291464 | tf_op jit(solution)/shard_map/ppermute | solution.py:30
  112.9 10.6 %collective-permute-start.20 = (bf16[1024,128]{1,0:T(8,128)(2,1)S(1)}, bf16[1024,128]{1,0:T(8,128)(2,1)}, u32[]{:S(2)}, u32[]{:S(2)}) collective-permute-start(bf16[1024,128]{1,0:T(8,128)(2,1)S(1)} %fusion), channel_id=1, source_target_pairs={{0,1},{1,2},{2,3},{3,0},{4,5},{5,6},{6,7},{7,4},{8,11},{9,8},{10,9... | collective-permute-start | bytes 786440 | tf_op jit(solution)/shard_map/ppermute | solution.py:30
  121.4 7.0 %copy-start.10 = (f32[1024,1024]{1,0:T(8,128)}, f32[1024,1024]{1,0:T(8,128)S(1)}, u32[]{:S(2)}) copy-start(f32[1024,1024]{1,0:T(8,128)S(1)} %get-tuple-element.75.refs_5_) | copy-start | bytes 12582916
  121.4 8.6 %copy-start.13 = (bf16[256,1024]{1,0:T(8,128)(2,1)S(1)}, bf16[256,1024]{1,0:T(8,128)(2,1)}, u32[]{:S(2)}) copy-start(bf16[256,1024]{1,0:T(8,128)(2,1)} %copy-done.12) | copy-start | bytes 1572868
  124.7 14.6 %collective-permute-start.21 = (bf16[1024,128]{1,0:T(8,128)(2,1)S(1)}, bf16[1024,128]{1,0:T(8,128)(2,1)S(1)}, u32[]{:S(2)}, u32[]{:S(2)}) collective-permute-start(bf16[1024,128]{1,0:T(8,128)(2,1)S(1)} %fusion.1), channel_id=1, source_target_pairs={{0,2},{1,3},{2,0},{3,1},{4,6},{5,7},{6,4},{7,5},{8,10},{9,11},{10,... | collective-permute-start | bytes 786440 | tf_op jit(solution)/shard_map/ppermute | solution.py:30
  128.5 11.9 %collective-permute-start.24 = (bf16[2,64,1152]{2,1,0:T(8,128)(2,1)S(1)}, bf16[2,64,1152]{2,1,0:T(8,128)(2,1)S(1)}, u32[]{:S(2)}, u32[]{:S(2)}) collective-permute-start(bf16[2,64,1152]{2,1,0:T(8,128)(2,1)S(1)} %shard_map.118), channel_id=1, source_target_pairs={{0,64},{1,65},{2,66},{3,67},{4,68},{5,69},{6,70},{7,71},{8,72},{9,... | collective-permute-start | bytes 884744 | tf_op jit(solution)/shard_map/ppermute | solution.py:50
  (14 other events, 25.8 us)

commit v3 on v2

--- a/solution.py
+++ b/solution.py
@@ -118,13 +118,13 @@
     blocks = take(operands)
     w_query, w_value = take(2)
     totals = take(2) if with_total else []
-    extra = take(3) if final else []
+    extra = take(4) if final else []
     outs = take(2)
     emitted = take(len(emit))
     held = take(operands)
     wq, wv = take(2)
     held_totals = take(2) if with_total else []
-    held_extra = take(3) if final else []
+    held_extra = take(4) if final else []
     accs = take(2)
     sems, total_sems, out_sems = take(3)
     bound = idx[weights] if final else 0
@@ -207,7 +207,7 @@
                         preferred_element_type=jnp.float32,
                     )
                     if last and final:
-                        s = held_extra[0][at]
+                        s = held_extra[0][at] + held_extra[1][at].astype(jnp.float32)
                         row = lax.broadcasted_iota(jnp.int32, s.shape, 0) + (dst + m)
                         none = jnp.zeros_like(s)
                         s = jnp.concatenate(
@@ -232,7 +232,7 @@
 
         nothing = (None, None)
         tq, tv = held_totals if (with_total and last) else nothing
-        lq, lv = held_extra[1:] if (final and last) else nothing
+        lq, lv = held_extra[2:] if (final and last) else nothing
         if not last:
             column(0, nq, accs[0], wq, None, None)
         else:
@@ -278,7 +278,7 @@
         operands += list(extra)
         scratch += [pltpu.VMEM(m.shape, m.dtype) for m in extra]
     scratch += [pltpu.VMEM((rows, nq), dtype), pltpu.VMEM((rows, nv), dtype)]
-    copies = len(blocks) + 2 * weights + (3 if final else 0)
+    copies = len(blocks) + 2 * weights + (4 if final else 0)
     scratch += [pltpu.SemaphoreType.DMA((copies,)), pltpu.SemaphoreType.DMA((nq // tile + 1,))]
     scratch += [pltpu.SemaphoreType.DMA((nq // tile + 1 + len(emit),))]
     hbm = pl.BlockSpec(memory_space=pltpu.HBM)
@@ -421,17 +421,18 @@
         total,
     )
     message = after(narrow(pair), total[1])
-    shrink = pair + to_z(message, 2)
+    pair_opposite = to_z(message, 2)
     far_b = to_far(
         offer(own_b, other_b, after(ends, message, cross_high), 2, 2, [(up_b, 2, 2), (down_b, 2, 2)])
     )
     total = add(
-        [cross_low, cross_middle, across_ahead],
+        [cross_low, cross_middle, cross_high, across_ahead],
         after(jnp.stack([place(1, -1), place(1, 1)]), message),
         [
             (0, 0, 0, EARLY, 0),
             (1, 0, EARLY, MIDDLE - EARLY, 0),
-            (2, 0, 0, rows, 1),
+            (2, 0, MIDDLE, rows - MIDDLE, 0),
+            (3, 0, 0, rows, 1),
         ],
         total,
     )
@@ -447,11 +448,11 @@
 
     return tuple(
         add(
-            [cross_high, last],
-            jnp.stack([place(1, -1), place(1, 2), bound]),
-            [(0, 0, MIDDLE, rows - MIDDLE, 0), (1, 0, 0, rows, 1)],
+            [last],
+            jnp.stack([place(1, 2), bound]),
+            [(0, 0, 0, rows, 0)],
             total,
-            (shrink, lift_q, lift_v),
+            (pair, pair_opposite, lift_q, lift_v),
         )
     )
 

time: 156 us -> 151 us (0.968); the launches traced: 153 us -> 150 us
    pallas_call x6, Pallas kernels: 51 us -> 49.2 us  [matmul(): pl.pallas_call(functools.partial(matmul_kernel, pieces, total is not None...]
    unnamed x43 -> x49, local copies, waits for them, and re-layouts: 11 us -> 10.9 us
  transfers between devices with their start and end apart: 25 -> 25, of which waited for: 10 -> 10; matrix products, arithmetic and copies ran while one was open for 6% -> 6% of each run, Pallas kernels for 40% -> 42%
where the time goes in v3:
time: 151 us; the launch traced here: 150 us
  Pallas kernels  71.7 us (47%)
  starting transfers between devices  32.4 us (21%)
  waiting for transfers between devices  25.9 us (17%)
  local copies, waits for them, and re-layouts  13.5 us (9%)
  other arithmetic  4.85 us (3%)
  between operations  1.81 us (1%)
    pallas_call x6, Pallas kernels, matmul(): pl.pallas_call(functools.partial(matmul_kernel, pieces, total is not None...  49.2 us
    pallas_call x10, Pallas kernels, offer(): pl.pallas_call(functools.partial(offer_kernel, [a[1:] for a in adds], off...  21.1 us
    ppermute x8, starting transfers between devices, to_y(): lax.ppermute(v, ('dp', 'mp'), pairs(lambda h, y, c, x, z, s: (h, y + s *...  13.8 us
    ppermute x8, waiting for transfers between devices, to_y(): lax.ppermute(v, ('dp', 'mp'), pairs(lambda h, y, c, x, z, s: (h, y + s *...  11.8 us
    unnamed x49, local copies, waits for them, and re-layouts  10.9 us
    ppermute x5, waiting for transfers between devices, to_x(): lax.ppermute(v, ('dp', 'mp'), pairs(lambda h, y, c, x, z, s: (h, y, c, 1...  9.94 us
    ppermute x3, starting transfers between devices, to_far(): lax.ppermute(v, ('dp', 'mp'), pairs(lambda h, y, c, x, z, s: (1 - h, y, c...  7.24 us
    ppermute x7, starting transfers between devices, to_z(): lax.ppermute(v, ('dp', 'mp'), pairs(lambda h, y, c, x, z, s: (h, y, c, x,...  6.9 us
  transfers between devices with their start and end apart: 25, of which 10 were waited for; matrix products, arithmetic and copies ran while one was open for 6% of the time, Pallas kernels for 42%

profile of v3, /device:TPU:0, one launch (start us, length us, event | category | flops | bytes accessed | tf_op | source)
XLA Modules:
  0.0 150.2 jit_solution(10237215897031831533)
XLA Ops:
  0.7 2.1 %collective-permute-start.2 = (bf16[1024,1024]{1,0:T(8,128)(2,1)}, bf16[1024,1024]{1,0:T(8,128)(2,1)}, u32[]{:S(2)}, u32[]{:S(2)}) collective-permute-start(bf16[1024,1024]{1,0:T(8,128)(2,1)} %tokens.1), channel_id=1, source_target_pairs={{0,1},{1,2},{2,3},{3,0},{4,5},{5,6},{6,7},{7,4},{8,11},{9,8},{10,9... | collective-permute-start | bytes 6291464 | tf_op jit(solution)/shard_map/ppermute | solution.py:30
  3.6 3.1 %collective-permute-start = (s32[2]{0:T(128)S(1)}, s32[2]{0:T(128)S(1)}, u32[]{:S(2)}, u32[]{:S(2)}) collective-permute-start(s32[2]{0:T(128)S(1)} %fusion.1), channel_id=1, source_target_pairs={{0,64},{1,65},{2,66},{3,67},{4,68},{5,69},{6,70},{7,71},{8,72},{9,... | collective-permute-start | bytes 32 | tf_op jit(solution)/shard_map/ppermute | solution.py:50
  6.7 2.0 %collective-permute-done = s32[2]{0:T(128)S(1)} collective-permute-done((s32[2]{0:T(128)S(1)}, s32[2]{0:T(128)S(1)}, u32[]{:S(2)}, u32[]{:S(2)}) %collective-permute-start) | collective-permute-done | bytes 40 | tf_op jit(solution)/shard_map/ppermute | solution.py:50
  10.3 2.1 %collective-permute-start.11 = (bf16[1024,1024]{1,0:T(8,128)(2,1)}, bf16[1024,1024]{1,0:T(8,128)(2,1)}, u32[]{:S(2)}, u32[]{:S(2)}) collective-permute-start(bf16[1024,1024]{1,0:T(8,128)(2,1)} %tokens.1), channel_id=1, source_target_pairs={{0,3},{1,0},{2,1},{3,2},{4,7},{5,4},{6,5},{7,6},{8,9},{9,10},{10,1... | collective-permute-start | bytes 6291464 | tf_op jit(solution)/shard_map/ppermute | solution.py:30
  12.5 3.2 %collective-permute-start.3 = (s32[4]{0:T(128)S(1)}, s32[4]{0:T(128)S(1)}, u32[]{:S(2)}, u32[]{:S(2)}) collective-permute-start(s32[4]{0:T(128)S(1)} %pad_add_fusion.1), channel_id=1, source_target_pairs={{0,32},{1,33},{2,34},{3,35},{4,36},{5,37},{6,38},{7,39},{8,40},{9,... | collective-permute-start | bytes 56 | tf_op jit(solution)/shard_map/ppermute | solution.py:36
  15.7 1.9 %collective-permute-done.3 = s32[4]{0:T(128)S(1)} collective-permute-done((s32[4]{0:T(128)S(1)}, s32[4]{0:T(128)S(1)}, u32[]{:S(2)}, u32[]{:S(2)}) %collective-permute-start.3) | collective-permute-done | bytes 48 | tf_op jit(solution)/shard_map/ppermute | solution.py:36
  19.3 3.1 %collective-permute-done.4 = s32[8]{0:T(128)S(1)} collective-permute-done((s32[8]{0:T(128)S(1)}, s32[8]{0:T(128)S(1)}, u32[]{:S(2)}, u32[]{:S(2)}) %collective-permute-start.4) | collective-permute-done | bytes 64 | tf_op jit(solution)/shard_map/ppermute | solution.py:36
  23.9 1.7 %shard_map.104 = bf16[4,1024,128]{2,1,0:T(8,128)(2,1)} custom-call(s32[9]{0:T(128)S(1)} %add_add_fusion.codes, bf16[5,1024,128]{2,1,0:T(8,128)(2,1)S(1)} %copy-done.1, bf16[5,1024,128]{2,1,0:T(8,128)(2,1)S(1)} %collective-permute-done.5.other), custom_call_target="tpu_custom_call" | custom-call | flops 655360 | bytes 4194304 | tf_op jit(solution)/shard_map/pallas_call | solution.py:101
  27.5 1.6 %copy-done.7 = bf16[1024,1024]{1,0:T(8,128)(2,1)S(1)} copy-done((bf16[1024,1024]{1,0:T(8,128)(2,1)S(1)}, bf16[1024,1024]{1,0:T(8,128)(2,1)}, u32[]{:S(2)}) %copy-start.7) | copy-done | bytes 2097176
  29.1 6.3 %shard_map.105 = (f32[1024,1024]{1,0:T(8,128)S(1)}, f32[1024,128]{1,0:T(8,128)S(1)}) custom-call(s32[1]{0:T(128)} %bitcast.4.idx, bf16[1024,1024]{1,0:T(8,128)(2,1)S(1)} %copy-done.7, bf16[8192,1024]{1,0:T(8,128)(2,1)} %refs_1_.7, bf16[8192,128]{1,0:T(8,128)(2,1)S(1)} %copy-done), custom_call_target="tpu_custom_call" | custom-call | flops 2415919104 | bytes 9175040 | tf_op jit(solution)/shard_map/pallas_call | solution.py:289
  35.4 2.2 %shard_map.106 = bf16[4,1024,128]{2,1,0:T(8,128)(2,1)} custom-call(s32[9]{0:T(128)S(1)} %pad_add_fusion.3.codes, bf16[5,1024,128]{2,1,0:T(8,128)(2,1)S(1)} %copy-done.2, bf16[5,1024,128]{2,1,0:T(8,128)(2,1)S(1)} %copy-done.4), custom_call_target="tpu_custom_call" | custom-call | flops 655360 | bytes 4194304 | tf_op jit(solution)/shard_map/pallas_call | solution.py:101
  37.7 2.9 %collective-permute-start.10 = (bf16[4,1024,128]{2,1,0:T(8,128)(2,1)}, bf16[4,1024,128]{2,1,0:T(8,128)(2,1)}, u32[]{:S(2)}, u32[]{:S(2)}) collective-permute-start(bf16[4,1024,128]{2,1,0:T(8,128)(2,1)} %shard_map.106), channel_id=1, source_target_pairs={{0,48},{1,49},{2,50},{3,51},{4,52},{5,53},{6,54},{7,55},{8,24},{9,... | collective-permute-start | bytes 3145736 | tf_op jit(solution)/shard_map/ppermute | solution.py:36
  42.0 2.5 %shard_map.107 = bf16[4,1024,128]{2,1,0:T(8,128)(2,1)} custom-call(s32[9]{0:T(128)S(1)} %pad_add_fusion.3.codes, bf16[5,1024,128]{2,1,0:T(8,128)(2,1)S(1)} %copy-done.2, bf16[5,1024,128]{2,1,0:T(8,128)(2,1)S(1)} %copy-done.4, bf16[4,1024,128]{2,1,0:T(8,128)(2,1)} %collective-permute-done.7.refs_0_), custom_call_target="tpu_custom_call" | custom-call | flops 655360 | bytes 4194304 | tf_op jit(solution)/shard_map/pallas_call | solution.py:101
  44.5 2.3 %shard_map.108 = bf16[4,64,1152]{2,1,0:T(8,128)(2,1)} custom-call(s32[9]{0:T(128)S(1)} %add_add_fusion.codes, bf16[5,64,1152]{2,1,0:T(8,128)(2,1)} %constant_dynamic-update-slice_fusion.own, bf16[5,64,1152]{2,1,0:T(8,128)(2,1)} %collective-permute-done.6.other), custom_call_target="tpu_custom_call" | custom-call | flops 368640 | bytes 2359296 | tf_op jit(solution)/shard_map/pallas_call | solution.py:101
  46.8 2.3 %shard_map.109 = bf16[4,64,1152]{2,1,0:T(8,128)(2,1)} custom-call(s32[9]{0:T(128)S(1)} %pad_add_fusion.3.codes, bf16[5,64,1152]{2,1,0:T(8,128)(2,1)} %constant_dynamic-update-slice_fusion.own, bf16[5,64,1152]{2,1,0:T(8,128)(2,1)} %collective-permute-done.6.other), custom_call_target="tpu_custom_call" | custom-call | flops 368640 | bytes 2359296 | tf_op jit(solution)/shard_map/pallas_call | solution.py:101
  49.2 1.9 %slice.23 = bf16[256,1024]{1,0:T(8,128)(2,1)} slice(bf16[1024,1024]{1,0:T(8,128)(2,1)} %collective-permute-done.2.refs_0_), slice={[0:256], [0:1024]} | slice | bytes 1048576 | tf_op jit(solution)/shard_map/slice | solution.py:368
  51.0 6.2 %collective-permute-done.1.refs_1_ = bf16[1024,1024]{1,0:T(8,128)(2,1)} collective-permute-done((bf16[1024,1024]{1,0:T(8,128)(2,1)}, bf16[1024,1024]{1,0:T(8,128)(2,1)}, u32[]{:S(2)}, u32[]{:S(2)}) %collective-permute-start.1) | collective-permute-done | bytes 2097184 | tf_op jit(solution)/shard_map/ppermute | solution.py:42
  58.2 3.9 %collective-permute-done.10.refs_1_ = bf16[4,1024,128]{2,1,0:T(8,128)(2,1)} collective-permute-done((bf16[4,1024,128]{2,1,0:T(8,128)(2,1)}, bf16[4,1024,128]{2,1,0:T(8,128)(2,1)}, u32[]{:S(2)}, u32[]{:S(2)}) %collective-permute-start.10) | collective-permute-done | bytes 1048608 | tf_op jit(solution)/shard_map/ppermute | solution.py:36
  63.9 7.6 %shard_map.110 = (f32[1024,1024]{1,0:T(8,128)}, f32[1024,128]{1,0:T(8,128)S(1)}, bf16[256,1024]{1,0:T(8,128)(2,1)}, bf16[512,1024]{1,0:T(8,128)(2,1)}) custom-call(s32[1]{0:T(128)} %bitcast.5.idx, bf16[1024,1024]{1,0:T(8,128)(2,1)} %collective-permute-done.2.refs_0_, bf16[8192,1024]{1,0:T(8,128)(2,1)} %refs_1_.7, bf16[8192,128]{1,0:T(8,128)(2,1)S(1)} %copy-done, ...), custom_call_target="tpu_custom_call" | custom-call | flops 2415919104 | bytes 13893632 | tf_op jit(solution)/shard_map/pallas_call | solution.py:289
  71.5 2.5 %shard_map.111 = bf16[2,1024,128]{2,1,0:T(8,128)(2,1)} custom-call(s32[9]{0:T(128)S(1)} %add_add_fusion.codes, bf16[5,1024,128]{2,1,0:T(8,128)(2,1)S(1)} %copy-done.2, bf16[5,1024,128]{2,1,0:T(8,128)(2,1)S(1)} %copy-done.5, bf16[4,1024,128]{2,1,0:T(8,128)(2,1)} %collective-permute-done.9.refs_0_, bf16[4,1024,128]{2,1,0:T(8,128)(2,1)} %collective-permute-done.10.refs_1_), custom_call_target="tpu_custom_call" | custom-call | flops 655360 | bytes 2097152 | tf_op jit(solution)/shard_map/pallas_call | solution.py:101
  74.0 2.7 %collective-permute-start.13 = (bf16[2,1024,128]{2,1,0:T(8,128)(2,1)}, bf16[2,1024,128]{2,1,0:T(8,128)(2,1)}, u32[]{:S(2)}, u32[]{:S(2)}) collective-permute-start(bf16[2,1024,128]{2,1,0:T(8,128)(2,1)} %shard_map.111), channel_id=1, source_target_pairs={{0,64},{1,65},{2,66},{3,67},{4,68},{5,69},{6,70},{7,71},{8,72},{9,... | collective-permute-start | bytes 1572872 | tf_op jit(solution)/shard_map/ppermute | solution.py:50
  76.6 9.8 %shard_map.112 = (f32[1024,1024]{1,0:T(8,128)}, f32[1024,128]{1,0:T(8,128)S(1)}) custom-call(s32[2]{0:T(128)S(1)} %pad_add_fusion.4.idx, bf16[1024,1024]{1,0:T(8,128)(2,1)} %collective-permute-done.11.refs_0_, bf16[1024,1024]{1,0:T(8,128)(2,1)} %collective-permute-done.1.refs_1_, bf16[8192,1024]{1,0:T(8,128)(2,1)} %refs_1_.7, bf16[8192,128]{1,0:T(8,128)(2,1)S(1)} %copy-done, ...), custom_call_target="tpu_custom_call" | custom-call | flops 4831838208 | bytes 18350080 | tf_op jit(solution)/shard_map/pallas_call | solution.py:289
  91.9 2.1 %shard_map.113.maps = bf16[2,1024,128]{2,1,0:T(8,128)(2,1)S(1)} custom-call(s32[9]{0:T(128)S(1)} %add_add_fusion.codes, bf16[5,1024,128]{2,1,0:T(8,128)(2,1)S(1)} %copy-done.2, bf16[5,1024,128]{2,1,0:T(8,128)(2,1)S(1)} %copy-done.6, bf16[4,1024,128]{2,1,0:T(8,128)(2,1)} %collective-permute-done.9.refs_0_, ...), custom_call_target="tpu_custom_call" | custom-call | flops 655360 | bytes 2097152 | tf_op jit(solution)/shard_map/pallas_call | solution.py:101
  100.7 2.4 %shard_map.115 = bf16[4,64,1152]{2,1,0:T(8,128)(2,1)} custom-call(s32[9]{0:T(128)S(1)} %pad_add_fusion.3.codes, bf16[5,64,1152]{2,1,0:T(8,128)(2,1)} %constant_dynamic-update-slice_fusion.own, bf16[5,64,1152]{2,1,0:T(8,128)(2,1)} %collective-permute-done.6.other, bf16[4,64,1152]{2,1,0:T(8,128)(2,1)} %collective-permute-done.14.refs_0_), custom_call_target="tpu_custom_call" | custom-call | flops 368640 | bytes 2359296 | tf_op jit(solution)/shard_map/pallas_call | solution.py:101
  103.1 1.8 %collective-permute-start.16 = (bf16[1024,1024]{1,0:T(8,128)(2,1)}, bf16[1024,1024]{1,0:T(8,128)(2,1)}, u32[]{:S(2)}, u32[]{:S(2)}) collective-permute-start(bf16[1024,1024]{1,0:T(8,128)(2,1)} %collective-permute-done.8.refs_3_), channel_id=1, source_target_pairs={{0,3},{1,0},{2,1},{3,2},{4,7},{5,4},{6,5},{7,6},{8,9},{9,10},{10,1... | collective-permute-start | bytes 6291464 | tf_op jit(solution)/shard_map/ppermute | solution.py:30
  105.0 5.3 %collective-permute-start.23 = (bf16[4,64,1152]{2,1,0:T(8,128)(2,1)}, bf16[4,64,1152]{2,1,0:T(8,128)(2,1)S(1)}, u32[]{:S(2)}, u32[]{:S(2)}) collective-permute-start(bf16[4,64,1152]{2,1,0:T(8,128)(2,1)} %shard_map.109), channel_id=1, source_target_pairs={{0,48},{1,49},{2,50},{3,51},{4,52},{5,53},{6,54},{7,55},{8,24},{9,... | collective-permute-start | bytes 1769480 | tf_op jit(solution)/shard_map/ppermute | solution.py:36
  110.3 1.7 %fusion = bf16[1024,128]{1,0:T(8,128)(2,1)} fusion(f32[1024,128]{1,0:T(8,128)S(1)} %copy-done.13, bf16[1024,128]{1,0:T(8,128)(2,1)} %collective-permute-done.17), kind=kLoop, calls=%fused_computation.3 | loop fusion | flops 393216 | bytes 1048576 | tf_op jit(solution)/shard_map/convert_element_type | solution.py:402
  113.1 7.4 %shard_map.116 = (f32[1024,1024]{1,0:T(8,128)S(1)}, f32[1024,128]{1,0:T(8,128)S(1)}) custom-call(s32[1]{0:T(128)} %bitcast.10.idx, bf16[1024,1024]{1,0:T(8,128)(2,1)} %collective-permute-done.15.refs_0_, bf16[8192,1024]{1,0:T(8,128)(2,1)} %refs_1_.7, bf16[8192,128]{1,0:T(8,128)(2,1)S(1)} %copy-done, f32[1024,1024]{1,0:T(8,128)} %get-tuple-element.71.refs_3_, ...), custom_call_target="tpu_custom_call" | custom-call | flops 2415919104 | bytes 13893632 | tf_op jit(solution)/shard_map/pallas_call | solution.py:289
  120.5 2.2 %collective-permute-done.18 = bf16[1024,128]{1,0:T(8,128)(2,1)S(1)} collective-permute-done((bf16[1024,128]{1,0:T(8,128)(2,1)}, bf16[1024,128]{1,0:T(8,128)(2,1)S(1)}, u32[]{:S(2)}, u32[]{:S(2)}) %collective-permute-start.18) | collective-permute-done | bytes 262176 | tf_op jit(solution)/shard_map/ppermute | solution.py:30
  123.8 2.4 %collective-permute-done.20.refs_2_ = bf16[512,1024]{1,0:T(8,128)(2,1)} collective-permute-done((bf16[512,1024]{1,0:T(8,128)(2,1)}, bf16[512,1024]{1,0:T(8,128)(2,1)}, u32[]{:S(2)}, u32[]{:S(2)}) %collective-permute-start.20) | collective-permute-done | bytes 1048608 | tf_op jit(solution)/shard_map/ppermute | solution.py:42
  129.2 9.8 %shard_map.117 = (f32[1024,1024]{1,0:T(8,128)}, f32[1024,128]{1,0:T(8,128)S(1)}) custom-call(s32[2]{0:T(128)S(1)} %pad_add_fusion.5.idx, bf16[256,1024]{1,0:T(8,128)(2,1)S(1)} %copy-done.16, bf16[256,1024]{1,0:T(8,128)(2,1)} %collective-permute-done.19.refs_1_, bf16[512,1024]{1,0:T(8,128)(2,1)} %collective-permute-done.20.refs_2_, ...), custom_call_target="tpu_custom_call" | custom-call | flops 4831838208 | bytes 18350080 | tf_op jit(solution)/shard_map/pallas_call | solution.py:289
  141.6 8.4 %shard_map.120 = (bf16[1024,1024]{1,0:T(8,128)(2,1)}, bf16[1024,128]{1,0:T(8,128)(2,1)}) custom-call(s32[2]{0:T(128)S(1)} %pad_add_fusion.idx, bf16[1024,1024]{1,0:T(8,128)(2,1)} %collective-permute-done.16.refs_0_, bf16[8192,1024]{1,0:T(8,128)(2,1)} %refs_1_.7, bf16[8192,128]{1,0:T(8,128)(2,1)S(1)} %copy-done, f32[1024,1024]{1,0:T(8,128)S(1)} %copy-done.10, ...), custom_call_target="tpu_custom_call" | custom-call | flops 2415919104 | bytes 13893632 | tf_op jit(solution)/shard_map/pallas_call | solution.py:289
  (106 shorter events, 31.1 us)
Async XLA Ops:
  0.6 21.8 %collective-permute-start.5 = (bf16[5,1024,128]{2,1,0:T(8,128)(2,1)}, bf16[5,1024,128]{2,1,0:T(8,128)(2,1)S(1)}, u32[]{:S(2)}, u32[]{:S(2)}) collective-permute-start(bf16[5,1024,128]{2,1,0:T(8,128)(2,1)} %own.9), channel_id=1, source_target_pairs={{0,8},{1,9},{2,10},{3,11},{4,12},{5,13},{6,14},{7,15},{8,0},{9,1},... | collective-permute-start | bytes 3932168 | tf_op jit(solution)/shard_map/ppermute | solution.py:46
  0.7 48.5 %collective-permute-start.2 = (bf16[1024,1024]{1,0:T(8,128)(2,1)}, bf16[1024,1024]{1,0:T(8,128)(2,1)}, u32[]{:S(2)}, u32[]{:S(2)}) collective-permute-start(bf16[1024,1024]{1,0:T(8,128)(2,1)} %tokens.1), channel_id=1, source_target_pairs={{0,1},{1,2},{2,3},{3,0},{4,5},{5,6},{6,7},{7,4},{8,11},{9,8},{10,9... | collective-permute-start | bytes 6291464 | tf_op jit(solution)/shard_map/ppermute | solution.py:30
  3.6 5.1 %collective-permute-start = (s32[2]{0:T(128)S(1)}, s32[2]{0:T(128)S(1)}, u32[]{:S(2)}, u32[]{:S(2)}) collective-permute-start(s32[2]{0:T(128)S(1)} %fusion.1), channel_id=1, source_target_pairs={{0,64},{1,65},{2,66},{3,67},{4,68},{5,69},{6,70},{7,71},{8,72},{9,... | collective-permute-start | bytes 32 | tf_op jit(solution)/shard_map/ppermute | solution.py:50
  8.8 48.5 %collective-permute-start.1 = (bf16[1024,1024]{1,0:T(8,128)(2,1)}, bf16[1024,1024]{1,0:T(8,128)(2,1)}, u32[]{:S(2)}, u32[]{:S(2)}) collective-permute-start(bf16[1024,1024]{1,0:T(8,128)(2,1)} %tokens.1), channel_id=1, source_target_pairs={{0,4},{1,5},{2,6},{3,7},{4,0},{5,1},{6,2},{7,3},{8,12},{9,13},{10,... | collective-permute-start | bytes 6291464 | tf_op jit(solution)/shard_map/ppermute | solution.py:42
  10.3 66.4 %collective-permute-start.11 = (bf16[1024,1024]{1,0:T(8,128)(2,1)}, bf16[1024,1024]{1,0:T(8,128)(2,1)}, u32[]{:S(2)}, u32[]{:S(2)}) collective-permute-start(bf16[1024,1024]{1,0:T(8,128)(2,1)} %tokens.1), channel_id=1, source_target_pairs={{0,3},{1,0},{2,1},{3,2},{4,7},{5,4},{6,5},{7,6},{8,9},{9,10},{10,1... | collective-permute-start | bytes 6291464 | tf_op jit(solution)/shard_map/ppermute | solution.py:30
  12.5 5.1 %collective-permute-start.3 = (s32[4]{0:T(128)S(1)}, s32[4]{0:T(128)S(1)}, u32[]{:S(2)}, u32[]{:S(2)}) collective-permute-start(s32[4]{0:T(128)S(1)} %pad_add_fusion.1), channel_id=1, source_target_pairs={{0,32},{1,33},{2,34},{3,35},{4,36},{5,37},{6,38},{7,39},{8,40},{9,... | collective-permute-start | bytes 56 | tf_op jit(solution)/shard_map/ppermute | solution.py:36
  17.6 4.8 %collective-permute-start.4 = (s32[8]{0:T(128)S(1)}, s32[8]{0:T(128)S(1)}, u32[]{:S(2)}, u32[]{:S(2)}) collective-permute-start(s32[8]{0:T(128)S(1)} %pad_add_fusion.2), channel_id=1, source_target_pairs={{0,16},{1,17},{2,18},{3,19},{4,20},{5,21},{6,22},{7,23},{8,56},{9,... | collective-permute-start | bytes 104 | tf_op jit(solution)/shard_map/ppermute | solution.py:36
  25.7 16.3 %collective-permute-start.7 = (bf16[4,1024,128]{2,1,0:T(8,128)(2,1)}, bf16[4,1024,128]{2,1,0:T(8,128)(2,1)}, u32[]{:S(2)}, u32[]{:S(2)}) collective-permute-start(bf16[4,1024,128]{2,1,0:T(8,128)(2,1)} %shard_map.104), channel_id=1, source_target_pairs={{0,16},{1,17},{2,18},{3,19},{4,20},{5,21},{6,22},{7,23},{8,56},{9,... | collective-permute-start | bytes 3145736 | tf_op jit(solution)/shard_map/ppermute | solution.py:36
  27.5 7.9 %collective-permute-start.6 = (bf16[5,64,1152]{2,1,0:T(8,128)(2,1)}, bf16[5,64,1152]{2,1,0:T(8,128)(2,1)}, u32[]{:S(2)}, u32[]{:S(2)}) collective-permute-start(bf16[5,64,1152]{2,1,0:T(8,128)(2,1)} %constant_dynamic-update-slice_fusion.own), channel_id=1, source_target_pairs={{0,8},{1,9},{2,10},{3,11},{4,12},{5,13},{6,14},{7,15},{8,0},{9,1},... | collective-permute-start | bytes 2211848 | tf_op jit(solution)/shard_map/ppermute | solution.py:46
  35.4 9.1 %copy-start.9 = (f32[1024,1024]{1,0:T(8,128)}, f32[1024,1024]{1,0:T(8,128)S(1)}, u32[]{:S(2)}) copy-start(f32[1024,1024]{1,0:T(8,128)S(1)} %get-tuple-element.53.refs_3_) | copy-start | bytes 12582916
  35.4 9.1 %copy-start.17 = (f32[1024,128]{1,0:T(8,128)}, f32[1024,128]{1,0:T(8,128)S(1)}, u32[]{:S(2)}) copy-start(f32[1024,128]{1,0:T(8,128)S(1)} %get-tuple-element.45.refs_4_) | copy-start | bytes 1572868
  37.7 24.4 %collective-permute-start.10 = (bf16[4,1024,128]{2,1,0:T(8,128)(2,1)}, bf16[4,1024,128]{2,1,0:T(8,128)(2,1)}, u32[]{:S(2)}, u32[]{:S(2)}) collective-permute-start(bf16[4,1024,128]{2,1,0:T(8,128)(2,1)} %shard_map.106), channel_id=1, source_target_pairs={{0,48},{1,49},{2,50},{3,51},{4,52},{5,53},{6,54},{7,55},{8,24},{9,... | collective-permute-start | bytes 3145736 | tf_op jit(solution)/shard_map/ppermute | solution.py:36
  44.5 26.9 %collective-permute-start.9 = (bf16[4,1024,128]{2,1,0:T(8,128)(2,1)}, bf16[4,1024,128]{2,1,0:T(8,128)(2,1)}, u32[]{:S(2)}, u32[]{:S(2)}) collective-permute-start(bf16[4,1024,128]{2,1,0:T(8,128)(2,1)} %shard_map.107), channel_id=1, source_target_pairs={{0,16},{1,17},{2,18},{3,19},{4,20},{5,21},{6,22},{7,23},{8,56},{9,... | collective-permute-start | bytes 3145736 | tf_op jit(solution)/shard_map/ppermute | solution.py:36
  51.0 52.1 %collective-permute-start.15 = (bf16[1024,1024]{1,0:T(8,128)(2,1)}, bf16[1024,1024]{1,0:T(8,128)(2,1)}, u32[]{:S(2)}, u32[]{:S(2)}) collective-permute-start(bf16[1024,1024]{1,0:T(8,128)(2,1)} %collective-permute-done.2.refs_0_), channel_id=1, source_target_pairs={{0,1},{1,2},{2,3},{3,0},{4,5},{5,6},{6,7},{7,4},{8,11},{9,8},{10,9... | collective-permute-start | bytes 6291464 | tf_op jit(solution)/shard_map/ppermute | solution.py:30
  57.3 45.9 %collective-permute-start.8 = (bf16[1024,1024]{1,0:T(8,128)(2,1)}, bf16[1024,1024]{1,0:T(8,128)(2,1)}, u32[]{:S(2)}, u32[]{:S(2)}) collective-permute-start(bf16[1024,1024]{1,0:T(8,128)(2,1)} %collective-permute-done.1.refs_1_), channel_id=1, source_target_pairs={{0,3},{1,0},{2,1},{3,2},{4,7},{5,4},{6,5},{7,6},{8,9},{9,10},{10,1... | collective-permute-start | bytes 6291464 | tf_op jit(solution)/shard_map/ppermute | solution.py:30
  62.1 25.2 %collective-permute-start.12 = (bf16[256,1024]{1,0:T(8,128)(2,1)}, bf16[256,1024]{1,0:T(8,128)(2,1)S(1)}, u32[]{:S(2)}, u32[]{:S(2)}) collective-permute-start(bf16[256,1024]{1,0:T(8,128)(2,1)} %slice.23), channel_id=1, source_target_pairs={{0,4},{1,5},{2,6},{3,7},{4,0},{5,1},{6,2},{7,3},{8,12},{9,13},{10,... | collective-permute-start | bytes 1572872 | tf_op jit(solution)/shard_map/ppermute | solution.py:42
  63.9 7.6 %copy-start.5 = (bf16[5,1024,128]{2,1,0:T(8,128)(2,1)S(1)}, bf16[5,1024,128]{2,1,0:T(8,128)(2,1)}, u32[]{:S(2)}) copy-start(bf16[5,1024,128]{2,1,0:T(8,128)(2,1)} %copy-done.3) | copy-start | bytes 3932164
  74.0 16.6 %collective-permute-start.13 = (bf16[2,1024,128]{2,1,0:T(8,128)(2,1)}, bf16[2,1024,128]{2,1,0:T(8,128)(2,1)}, u32[]{:S(2)}, u32[]{:S(2)}) collective-permute-start(bf16[2,1024,128]{2,1,0:T(8,128)(2,1)} %shard_map.111), channel_id=1, source_target_pairs={{0,64},{1,65},{2,66},{3,67},{4,68},{5,69},{6,70},{7,71},{8,72},{9,... | collective-permute-start | bytes 1572872 | tf_op jit(solution)/shard_map/ppermute | solution.py:50
  76.6 12.6 %copy-start.23 = (s32[1,8]{1,0:T(1,128)S(1)}, s32[1,8]{1,0:T(1,128)}, u32[]{:S(2)}) copy-start(s32[1,8]{1,0:T(1,128)} %param.17) | copy-start | bytes 100
  88.0 11.1 %collective-permute-start.19 = (bf16[256,1024]{1,0:T(8,128)(2,1)}, bf16[256,1024]{1,0:T(8,128)(2,1)}, u32[]{:S(2)}, u32[]{:S(2)}) collective-permute-start(bf16[256,1024]{1,0:T(8,128)(2,1)} %get-tuple-element.61), channel_id=1, source_target_pairs={{0,4},{1,5},{2,6},{3,7},{4,0},{5,1},{6,2},{7,3},{8,12},{9,13},{10,... | collective-permute-start | bytes 1572872 | tf_op jit(solution)/shard_map/ppermute | solution.py:42
  88.8 11.9 %collective-permute-start.14 = (bf16[4,64,1152]{2,1,0:T(8,128)(2,1)}, bf16[4,64,1152]{2,1,0:T(8,128)(2,1)}, u32[]{:S(2)}, u32[]{:S(2)}) collective-permute-start(bf16[4,64,1152]{2,1,0:T(8,128)(2,1)} %shard_map.108), channel_id=1, source_target_pairs={{0,16},{1,17},{2,18},{3,19},{4,20},{5,21},{6,22},{7,23},{8,56},{9,... | collective-permute-start | bytes 1769480 | tf_op jit(solution)/shard_map/ppermute | solution.py:36
  96.5 13.8 %collective-permute-start.17 = (bf16[1024,128]{1,0:T(8,128)(2,1)}, bf16[1024,128]{1,0:T(8,128)(2,1)}, u32[]{:S(2)}, u32[]{:S(2)}) collective-permute-start(bf16[1024,128]{1,0:T(8,128)(2,1)} %get-tuple-element.63), channel_id=1, source_target_pairs={{0,4},{1,5},{2,6},{3,7},{4,0},{5,1},{6,2},{7,3},{8,12},{9,13},{10,... | collective-permute-start | bytes 786440 | tf_op jit(solution)/shard_map/ppermute | solution.py:42
  99.2 27.1 %collective-permute-start.20 = (bf16[512,1024]{1,0:T(8,128)(2,1)}, bf16[512,1024]{1,0:T(8,128)(2,1)}, u32[]{:S(2)}, u32[]{:S(2)}) collective-permute-start(bf16[512,1024]{1,0:T(8,128)(2,1)} %get-tuple-element.69), channel_id=1, source_target_pairs={{0,4},{1,5},{2,6},{3,7},{4,0},{5,1},{6,2},{7,3},{8,12},{9,13},{10,... | collective-permute-start | bytes 3145736 | tf_op jit(solution)/shard_map/ppermute | solution.py:42
  99.2 11.1 %copy-start.13 = (f32[1024,128]{1,0:T(8,128)S(1)}, f32[1024,128]{1,0:T(8,128)}, u32[]{:S(2)}) copy-start(f32[1024,128]{1,0:T(8,128)} %copy-done.12) | copy-start | bytes 1572868
  103.1 37.6 %collective-permute-start.16 = (bf16[1024,1024]{1,0:T(8,128)(2,1)}, bf16[1024,1024]{1,0:T(8,128)(2,1)}, u32[]{:S(2)}, u32[]{:S(2)}) collective-permute-start(bf16[1024,1024]{1,0:T(8,128)(2,1)} %collective-permute-done.8.refs_3_), channel_id=1, source_target_pairs={{0,3},{1,0},{2,1},{3,2},{4,7},{5,4},{6,5},{7,6},{8,9},{9,10},{10,1... | collective-permute-start | bytes 6291464 | tf_op jit(solution)/shard_map/ppermute | solution.py:30
  105.0 21.3 %collective-permute-start.23 = (bf16[4,64,1152]{2,1,0:T(8,128)(2,1)}, bf16[4,64,1152]{2,1,0:T(8,128)(2,1)S(1)}, u32[]{:S(2)}, u32[]{:S(2)}) collective-permute-start(bf16[4,64,1152]{2,1,0:T(8,128)(2,1)} %shard_map.109), channel_id=1, source_target_pairs={{0,48},{1,49},{2,50},{3,51},{4,52},{5,53},{6,54},{7,55},{8,24},{9,... | collective-permute-start | bytes 1769480 | tf_op jit(solution)/shard_map/ppermute | solution.py:36
  110.3 16.0 %collective-permute-start.22 = (bf16[4,64,1152]{2,1,0:T(8,128)(2,1)}, bf16[4,64,1152]{2,1,0:T(8,128)(2,1)S(1)}, u32[]{:S(2)}, u32[]{:S(2)}) collective-permute-start(bf16[4,64,1152]{2,1,0:T(8,128)(2,1)} %shard_map.115), channel_id=1, source_target_pairs={{0,16},{1,17},{2,18},{3,19},{4,20},{5,21},{6,22},{7,23},{8,56},{9,... | collective-permute-start | bytes 1769480 | tf_op jit(solution)/shard_map/ppermute | solution.py:36
  112.0 10.7 %collective-permute-start.18 = (bf16[1024,128]{1,0:T(8,128)(2,1)}, bf16[1024,128]{1,0:T(8,128)(2,1)S(1)}, u32[]{:S(2)}, u32[]{:S(2)}) collective-permute-start(bf16[1024,128]{1,0:T(8,128)(2,1)} %fusion), channel_id=1, source_target_pairs={{0,1},{1,2},{2,3},{3,0},{4,5},{5,6},{6,7},{7,4},{8,11},{9,8},{10,9... | collective-permute-start | bytes 786440 | tf_op jit(solution)/shard_map/ppermute | solution.py:30
  113.1 9.5 %copy-start.14 = (f32[1024,128]{1,0:T(8,128)S(1)}, f32[1024,128]{1,0:T(8,128)}, u32[]{:S(2)}) copy-start(f32[1024,128]{1,0:T(8,128)} %copy-done.12) | copy-start | bytes 1572868
  120.5 8.7 %copy-start.16 = (bf16[256,1024]{1,0:T(8,128)(2,1)S(1)}, bf16[256,1024]{1,0:T(8,128)(2,1)}, u32[]{:S(2)}) copy-start(bf16[256,1024]{1,0:T(8,128)(2,1)} %copy-done.15) | copy-start | bytes 1572868
  123.7 17.0 %collective-permute-start.21 = (bf16[1024,128]{1,0:T(8,128)(2,1)S(1)}, bf16[1024,128]{1,0:T(8,128)(2,1)S(1)}, u32[]{:S(2)}, u32[]{:S(2)}) collective-permute-start(bf16[1024,128]{1,0:T(8,128)(2,1)S(1)} %get-tuple-element.73), channel_id=1, source_target_pairs={{0,2},{1,3},{2,0},{3,1},{4,6},{5,7},{6,4},{7,5},{8,10},{9,11},{10,... | collective-permute-start | bytes 786440 | tf_op jit(solution)/shard_map/ppermute | solution.py:30
  127.7 11.3 %collective-permute-start.24 = (bf16[2,64,1152]{2,1,0:T(8,128)(2,1)S(1)}, bf16[2,64,1152]{2,1,0:T(8,128)(2,1)S(1)}, u32[]{:S(2)}, u32[]{:S(2)}) collective-permute-start(bf16[2,64,1152]{2,1,0:T(8,128)(2,1)S(1)} %shard_map.118), channel_id=1, source_target_pairs={{0,64},{1,65},{2,66},{3,67},{4,68},{5,69},{6,70},{7,71},{8,72},{9,... | collective-permute-start | bytes 884744 | tf_op jit(solution)/shard_map/ppermute | solution.py:50
  (17 other events, 46.8 us)

commit v4 on v3

--- a/solution.py
+++ b/solution.py
@@ -294,7 +294,9 @@
         + [jax.ShapeDtypeStruct((high - low, width), jnp.bfloat16) for _, low, high in emit],
         scratch_shapes=scratch,
         compiler_params=pltpu.CompilerParams(vmem_limit_bytes=44 * 1024 * 1024),
-        cost_estimate=pl.CostEstimate(flops=flops, bytes_accessed=moved, transcendentals=0),
+        cost_estimate=pl.CostEstimate(
+            flops=1 if emit else flops, bytes_accessed=1 if emit else moved, transcendentals=0
+        ),
     )(index, *operands)
 
 

time: 151 us -> 151 us (level)
  no operation moved by 1% of the time
where the time goes in v4:
time: 151 us; the launch traced here: 150 us
  Pallas kernels  71.5 us (47%)
  starting transfers between devices  32.4 us (21%)
  waiting for transfers between devices  26 us (17%)
  local copies, waits for them, and re-layouts  13.5 us (9%)
  other arithmetic  4.85 us (3%)
  between operations  1.8 us (1%)
    pallas_call x6, Pallas kernels, matmul(): pl.pallas_call(functools.partial(matmul_kernel, pieces, total is not None...  49.2 us
    pallas_call x10, Pallas kernels, offer(): pl.pallas_call(functools.partial(offer_kernel, [a[1:] for a in adds], off...  20.9 us
    ppermute x8, starting transfers between devices, to_y(): lax.ppermute(v, ('dp', 'mp'), pairs(lambda h, y, c, x, z, s: (h, y + s *...  13.2 us
    ppermute x8, waiting for transfers between devices, to_y(): lax.ppermute(v, ('dp', 'mp'), pairs(lambda h, y, c, x, z, s: (h, y + s *...  12.3 us
    unnamed x49, local copies, waits for them, and re-layouts  10.9 us
    ppermute x5, waiting for transfers between devices, to_x(): lax.ppermute(v, ('dp', 'mp'), pairs(lambda h, y, c, x, z, s: (h, y, c, 1...  9.59 us
    ppermute x3, starting transfers between devices, to_far(): lax.ppermute(v, ('dp', 'mp'), pairs(lambda h, y, c, x, z, s: (1 - h, y, c...  7.68 us
    ppermute x7, starting transfers between devices, to_z(): lax.ppermute(v, ('dp', 'mp'), pairs(lambda h, y, c, x, z, s: (h, y, c, x,...  6.98 us
  transfers between devices with their start and end apart: 25, of which 10 were waited for; matrix products, arithmetic and copies ran while one was open for 6% of the time, Pallas kernels for 42%

profile of v4, /device:TPU:0, one launch (start us, length us, event | category | flops | bytes accessed | tf_op | source)
XLA Modules:
  0.0 150.1 jit_solution(16960622420569749986)
XLA Ops:
  0.7 2.1 %collective-permute-start.2 = (bf16[1024,1024]{1,0:T(8,128)(2,1)}, bf16[1024,1024]{1,0:T(8,128)(2,1)}, u32[]{:S(2)}, u32[]{:S(2)}) collective-permute-start(bf16[1024,1024]{1,0:T(8,128)(2,1)} %tokens.1), channel_id=1, source_target_pairs={{0,1},{1,2},{2,3},{3,0},{4,5},{5,6},{6,7},{7,4},{8,11},{9,8},{10,9... | collective-permute-start | bytes 6291464 | tf_op jit(solution)/shard_map/ppermute | solution.py:30
  3.6 3.1 %collective-permute-start = (s32[2]{0:T(128)S(1)}, s32[2]{0:T(128)S(1)}, u32[]{:S(2)}, u32[]{:S(2)}) collective-permute-start(s32[2]{0:T(128)S(1)} %fusion.1), channel_id=1, source_target_pairs={{0,64},{1,65},{2,66},{3,67},{4,68},{5,69},{6,70},{7,71},{8,72},{9,... | collective-permute-start | bytes 32 | tf_op jit(solution)/shard_map/ppermute | solution.py:50
  6.7 2.0 %collective-permute-done = s32[2]{0:T(128)S(1)} collective-permute-done((s32[2]{0:T(128)S(1)}, s32[2]{0:T(128)S(1)}, u32[]{:S(2)}, u32[]{:S(2)}) %collective-permute-start) | collective-permute-done | bytes 40 | tf_op jit(solution)/shard_map/ppermute | solution.py:50
  10.3 2.1 %collective-permute-start.11 = (bf16[1024,1024]{1,0:T(8,128)(2,1)}, bf16[1024,1024]{1,0:T(8,128)(2,1)}, u32[]{:S(2)}, u32[]{:S(2)}) collective-permute-start(bf16[1024,1024]{1,0:T(8,128)(2,1)} %tokens.1), channel_id=1, source_target_pairs={{0,3},{1,0},{2,1},{3,2},{4,7},{5,4},{6,5},{7,6},{8,9},{9,10},{10,1... | collective-permute-start | bytes 6291464 | tf_op jit(solution)/shard_map/ppermute | solution.py:30
  12.5 3.2 %collective-permute-start.3 = (s32[4]{0:T(128)S(1)}, s32[4]{0:T(128)S(1)}, u32[]{:S(2)}, u32[]{:S(2)}) collective-permute-start(s32[4]{0:T(128)S(1)} %pad_add_fusion.1), channel_id=1, source_target_pairs={{0,32},{1,33},{2,34},{3,35},{4,36},{5,37},{6,38},{7,39},{8,40},{9,... | collective-permute-start | bytes 56 | tf_op jit(solution)/shard_map/ppermute | solution.py:36
  15.7 1.9 %collective-permute-done.3 = s32[4]{0:T(128)S(1)} collective-permute-done((s32[4]{0:T(128)S(1)}, s32[4]{0:T(128)S(1)}, u32[]{:S(2)}, u32[]{:S(2)}) %collective-permute-start.3) | collective-permute-done | bytes 48 | tf_op jit(solution)/shard_map/ppermute | solution.py:36
  19.3 3.1 %collective-permute-done.4 = s32[8]{0:T(128)S(1)} collective-permute-done((s32[8]{0:T(128)S(1)}, s32[8]{0:T(128)S(1)}, u32[]{:S(2)}, u32[]{:S(2)}) %collective-permute-start.4) | collective-permute-done | bytes 64 | tf_op jit(solution)/shard_map/ppermute | solution.py:36
  23.9 1.7 %shard_map.104 = bf16[4,1024,128]{2,1,0:T(8,128)(2,1)} custom-call(s32[9]{0:T(128)S(1)} %add_add_fusion.codes, bf16[5,1024,128]{2,1,0:T(8,128)(2,1)S(1)} %copy-done.1, bf16[5,1024,128]{2,1,0:T(8,128)(2,1)S(1)} %collective-permute-done.5.other), custom_call_target="tpu_custom_call" | custom-call | flops 655360 | bytes 4194304 | tf_op jit(solution)/shard_map/pallas_call | solution.py:101
  27.5 1.6 %copy-done.7 = bf16[1024,1024]{1,0:T(8,128)(2,1)S(1)} copy-done((bf16[1024,1024]{1,0:T(8,128)(2,1)S(1)}, bf16[1024,1024]{1,0:T(8,128)(2,1)}, u32[]{:S(2)}) %copy-start.7) | copy-done | bytes 2097176
  29.1 6.3 %shard_map.105 = (f32[1024,1024]{1,0:T(8,128)S(1)}, f32[1024,128]{1,0:T(8,128)S(1)}) custom-call(s32[1]{0:T(128)} %bitcast.4.idx, bf16[1024,1024]{1,0:T(8,128)(2,1)S(1)} %copy-done.7, bf16[8192,1024]{1,0:T(8,128)(2,1)} %refs_1_.7, bf16[8192,128]{1,0:T(8,128)(2,1)S(1)} %copy-done), custom_call_target="tpu_custom_call" | custom-call | flops 2415919104 | bytes 9175040 | tf_op jit(solution)/shard_map/pallas_call | solution.py:289
  35.4 2.2 %shard_map.106 = bf16[4,1024,128]{2,1,0:T(8,128)(2,1)} custom-call(s32[9]{0:T(128)S(1)} %pad_add_fusion.3.codes, bf16[5,1024,128]{2,1,0:T(8,128)(2,1)S(1)} %copy-done.2, bf16[5,1024,128]{2,1,0:T(8,128)(2,1)S(1)} %copy-done.4), custom_call_target="tpu_custom_call" | custom-call | flops 655360 | bytes 4194304 | tf_op jit(solution)/shard_map/pallas_call | solution.py:101
  37.6 2.9 %collective-permute-start.10 = (bf16[4,1024,128]{2,1,0:T(8,128)(2,1)}, bf16[4,1024,128]{2,1,0:T(8,128)(2,1)}, u32[]{:S(2)}, u32[]{:S(2)}) collective-permute-start(bf16[4,1024,128]{2,1,0:T(8,128)(2,1)} %shard_map.106), channel_id=1, source_target_pairs={{0,48},{1,49},{2,50},{3,51},{4,52},{5,53},{6,54},{7,55},{8,24},{9,... | collective-permute-start | bytes 3145736 | tf_op jit(solution)/shard_map/ppermute | solution.py:36
  41.9 2.5 %shard_map.107 = bf16[4,1024,128]{2,1,0:T(8,128)(2,1)} custom-call(s32[9]{0:T(128)S(1)} %pad_add_fusion.3.codes, bf16[5,1024,128]{2,1,0:T(8,128)(2,1)S(1)} %copy-done.2, bf16[5,1024,128]{2,1,0:T(8,128)(2,1)S(1)} %copy-done.4, bf16[4,1024,128]{2,1,0:T(8,128)(2,1)} %collective-permute-done.7.refs_0_), custom_call_target="tpu_custom_call" | custom-call | flops 655360 | bytes 4194304 | tf_op jit(solution)/shard_map/pallas_call | solution.py:101
  44.4 2.3 %shard_map.108 = bf16[4,64,1152]{2,1,0:T(8,128)(2,1)} custom-call(s32[9]{0:T(128)S(1)} %add_add_fusion.codes, bf16[5,64,1152]{2,1,0:T(8,128)(2,1)} %constant_dynamic-update-slice_fusion.own, bf16[5,64,1152]{2,1,0:T(8,128)(2,1)} %collective-permute-done.6.other), custom_call_target="tpu_custom_call" | custom-call | flops 368640 | bytes 2359296 | tf_op jit(solution)/shard_map/pallas_call | solution.py:101
  46.7 2.3 %shard_map.109 = bf16[4,64,1152]{2,1,0:T(8,128)(2,1)} custom-call(s32[9]{0:T(128)S(1)} %pad_add_fusion.3.codes, bf16[5,64,1152]{2,1,0:T(8,128)(2,1)} %constant_dynamic-update-slice_fusion.own, bf16[5,64,1152]{2,1,0:T(8,128)(2,1)} %collective-permute-done.6.other), custom_call_target="tpu_custom_call" | custom-call | flops 368640 | bytes 2359296 | tf_op jit(solution)/shard_map/pallas_call | solution.py:101
  49.0 1.9 %slice.23 = bf16[256,1024]{1,0:T(8,128)(2,1)} slice(bf16[1024,1024]{1,0:T(8,128)(2,1)} %collective-permute-done.2.refs_0_), slice={[0:256], [0:1024]} | slice | bytes 1048576 | tf_op jit(solution)/shard_map/slice | solution.py:370
  50.9 6.4 %collective-permute-done.1.refs_1_ = bf16[1024,1024]{1,0:T(8,128)(2,1)} collective-permute-done((bf16[1024,1024]{1,0:T(8,128)(2,1)}, bf16[1024,1024]{1,0:T(8,128)(2,1)}, u32[]{:S(2)}, u32[]{:S(2)}) %collective-permute-start.1) | collective-permute-done | bytes 2097184 | tf_op jit(solution)/shard_map/ppermute | solution.py:42
  58.1 3.7 %collective-permute-done.10.refs_1_ = bf16[4,1024,128]{2,1,0:T(8,128)(2,1)} collective-permute-done((bf16[4,1024,128]{2,1,0:T(8,128)(2,1)}, bf16[4,1024,128]{2,1,0:T(8,128)(2,1)}, u32[]{:S(2)}, u32[]{:S(2)}) %collective-permute-start.10) | collective-permute-done | bytes 1048608 | tf_op jit(solution)/shard_map/ppermute | solution.py:36
  63.6 7.6 %shard_map.110 = (f32[1024,1024]{1,0:T(8,128)}, f32[1024,128]{1,0:T(8,128)S(1)}, bf16[256,1024]{1,0:T(8,128)(2,1)}, bf16[512,1024]{1,0:T(8,128)(2,1)}) custom-call(s32[1]{0:T(128)} %bitcast.5.idx, bf16[1024,1024]{1,0:T(8,128)(2,1)} %collective-permute-done.2.refs_0_, bf16[8192,1024]{1,0:T(8,128)(2,1)} %refs_1_.7, bf16[8192,128]{1,0:T(8,128)(2,1)S(1)} %copy-done, ...), custom_call_target="tpu_custom_call" | custom-call | flops 1 | bytes 1 | tf_op jit(solution)/shard_map/pallas_call | solution.py:289
  71.3 2.5 %shard_map.111 = bf16[2,1024,128]{2,1,0:T(8,128)(2,1)} custom-call(s32[9]{0:T(128)S(1)} %add_add_fusion.codes, bf16[5,1024,128]{2,1,0:T(8,128)(2,1)S(1)} %copy-done.2, bf16[5,1024,128]{2,1,0:T(8,128)(2,1)S(1)} %copy-done.5, bf16[4,1024,128]{2,1,0:T(8,128)(2,1)} %collective-permute-done.9.refs_0_, bf16[4,1024,128]{2,1,0:T(8,128)(2,1)} %collective-permute-done.10.refs_1_), custom_call_target="tpu_custom_call" | custom-call | flops 655360 | bytes 2097152 | tf_op jit(solution)/shard_map/pallas_call | solution.py:101
  73.8 3.2 %collective-permute-start.13 = (bf16[2,1024,128]{2,1,0:T(8,128)(2,1)}, bf16[2,1024,128]{2,1,0:T(8,128)(2,1)}, u32[]{:S(2)}, u32[]{:S(2)}) collective-permute-start(bf16[2,1024,128]{2,1,0:T(8,128)(2,1)} %shard_map.111), channel_id=1, source_target_pairs={{0,64},{1,65},{2,66},{3,67},{4,68},{5,69},{6,70},{7,71},{8,72},{9,... | collective-permute-start | bytes 1572872 | tf_op jit(solution)/shard_map/ppermute | solution.py:50
  77.0 9.8 %shard_map.112 = (f32[1024,1024]{1,0:T(8,128)}, f32[1024,128]{1,0:T(8,128)S(1)}) custom-call(s32[2]{0:T(128)S(1)} %pad_add_fusion.4.idx, bf16[1024,1024]{1,0:T(8,128)(2,1)} %collective-permute-done.11.refs_0_, bf16[1024,1024]{1,0:T(8,128)(2,1)} %collective-permute-done.1.refs_1_, bf16[8192,1024]{1,0:T(8,128)(2,1)} %refs_1_.7, bf16[8192,128]{1,0:T(8,128)(2,1)S(1)} %copy-done, ...), custom_call_target="tpu_custom_call" | custom-call | flops 4831838208 | bytes 18350080 | tf_op jit(solution)/shard_map/pallas_call | solution.py:289
  91.9 2.1 %shard_map.113.maps = bf16[2,1024,128]{2,1,0:T(8,128)(2,1)S(1)} custom-call(s32[9]{0:T(128)S(1)} %add_add_fusion.codes, bf16[5,1024,128]{2,1,0:T(8,128)(2,1)S(1)} %copy-done.2, bf16[5,1024,128]{2,1,0:T(8,128)(2,1)S(1)} %copy-done.6, bf16[4,1024,128]{2,1,0:T(8,128)(2,1)} %collective-permute-done.9.refs_0_, ...), custom_call_target="tpu_custom_call" | custom-call | flops 655360 | bytes 2097152 | tf_op jit(solution)/shard_map/pallas_call | solution.py:101
  99.0 2.2 %collective-permute-done.14.refs_0_ = bf16[4,64,1152]{2,1,0:T(8,128)(2,1)} collective-permute-done((bf16[4,64,1152]{2,1,0:T(8,128)(2,1)}, bf16[4,64,1152]{2,1,0:T(8,128)(2,1)}, u32[]{:S(2)}, u32[]{:S(2)}) %collective-permute-start.14) | collective-permute-done | bytes 589856 | tf_op jit(solution)/shard_map/ppermute | solution.py:36
  101.2 2.4 %shard_map.115 = bf16[4,64,1152]{2,1,0:T(8,128)(2,1)} custom-call(s32[9]{0:T(128)S(1)} %pad_add_fusion.3.codes, bf16[5,64,1152]{2,1,0:T(8,128)(2,1)} %constant_dynamic-update-slice_fusion.own, bf16[5,64,1152]{2,1,0:T(8,128)(2,1)} %collective-permute-done.6.other, bf16[4,64,1152]{2,1,0:T(8,128)(2,1)} %collective-permute-done.14.refs_0_), custom_call_target="tpu_custom_call" | custom-call | flops 368640 | bytes 2359296 | tf_op jit(solution)/shard_map/pallas_call | solution.py:101
  105.0 5.2 %collective-permute-start.23 = (bf16[4,64,1152]{2,1,0:T(8,128)(2,1)}, bf16[4,64,1152]{2,1,0:T(8,128)(2,1)S(1)}, u32[]{:S(2)}, u32[]{:S(2)}) collective-permute-start(bf16[4,64,1152]{2,1,0:T(8,128)(2,1)} %shard_map.109), channel_id=1, source_target_pairs={{0,48},{1,49},{2,50},{3,51},{4,52},{5,53},{6,54},{7,55},{8,24},{9,... | collective-permute-start | bytes 1769480 | tf_op jit(solution)/shard_map/ppermute | solution.py:36
  110.3 1.7 %fusion = bf16[1024,128]{1,0:T(8,128)(2,1)} fusion(f32[1024,128]{1,0:T(8,128)S(1)} %copy-done.13, bf16[1024,128]{1,0:T(8,128)(2,1)} %collective-permute-done.17), kind=kLoop, calls=%fused_computation.3 | loop fusion | flops 393216 | bytes 1048576 | tf_op jit(solution)/shard_map/convert_element_type | solution.py:404
  113.2 7.3 %shard_map.116 = (f32[1024,1024]{1,0:T(8,128)S(1)}, f32[1024,128]{1,0:T(8,128)S(1)}) custom-call(s32[1]{0:T(128)} %bitcast.10.idx, bf16[1024,1024]{1,0:T(8,128)(2,1)} %collective-permute-done.15.refs_0_, bf16[8192,1024]{1,0:T(8,128)(2,1)} %refs_1_.7, bf16[8192,128]{1,0:T(8,128)(2,1)S(1)} %copy-done, f32[1024,1024]{1,0:T(8,128)} %get-tuple-element.71.refs_3_, ...), custom_call_target="tpu_custom_call" | custom-call | flops 2415919104 | bytes 13893632 | tf_op jit(solution)/shard_map/pallas_call | solution.py:289
  120.5 2.1 %collective-permute-done.18 = bf16[1024,128]{1,0:T(8,128)(2,1)S(1)} collective-permute-done((bf16[1024,128]{1,0:T(8,128)(2,1)}, bf16[1024,128]{1,0:T(8,128)(2,1)S(1)}, u32[]{:S(2)}, u32[]{:S(2)}) %collective-permute-start.18) | collective-permute-done | bytes 262176 | tf_op jit(solution)/shard_map/ppermute | solution.py:30
  124.3 2.0 %collective-permute-done.20.refs_2_ = bf16[512,1024]{1,0:T(8,128)(2,1)} collective-permute-done((bf16[512,1024]{1,0:T(8,128)(2,1)}, bf16[512,1024]{1,0:T(8,128)(2,1)}, u32[]{:S(2)}, u32[]{:S(2)}) %collective-permute-start.20) | collective-permute-done | bytes 1048608 | tf_op jit(solution)/shard_map/ppermute | solution.py:42
  129.0 9.8 %shard_map.117 = (f32[1024,1024]{1,0:T(8,128)}, f32[1024,128]{1,0:T(8,128)S(1)}) custom-call(s32[2]{0:T(128)S(1)} %pad_add_fusion.5.idx, bf16[256,1024]{1,0:T(8,128)(2,1)S(1)} %copy-done.16, bf16[256,1024]{1,0:T(8,128)(2,1)} %collective-permute-done.19.refs_1_, bf16[512,1024]{1,0:T(8,128)(2,1)} %collective-permute-done.20.refs_2_, ...), custom_call_target="tpu_custom_call" | custom-call | flops 4831838208 | bytes 18350080 | tf_op jit(solution)/shard_map/pallas_call | solution.py:289
  141.4 8.4 %shard_map.120 = (bf16[1024,1024]{1,0:T(8,128)(2,1)}, bf16[1024,128]{1,0:T(8,128)(2,1)}) custom-call(s32[2]{0:T(128)S(1)} %pad_add_fusion.idx, bf16[1024,1024]{1,0:T(8,128)(2,1)} %collective-permute-done.16.refs_0_, bf16[8192,1024]{1,0:T(8,128)(2,1)} %refs_1_.7, bf16[8192,128]{1,0:T(8,128)(2,1)S(1)} %copy-done, f32[1024,1024]{1,0:T(8,128)S(1)} %copy-done.10, ...), custom_call_target="tpu_custom_call" | custom-call | flops 2415919104 | bytes 13893632 | tf_op jit(solution)/shard_map/pallas_call | solution.py:289
  (106 shorter events, 30.8 us)
Async XLA Ops:
  0.6 21.8 %collective-permute-start.5 = (bf16[5,1024,128]{2,1,0:T(8,128)(2,1)}, bf16[5,1024,128]{2,1,0:T(8,128)(2,1)S(1)}, u32[]{:S(2)}, u32[]{:S(2)}) collective-permute-start(bf16[5,1024,128]{2,1,0:T(8,128)(2,1)} %own.9), channel_id=1, source_target_pairs={{0,8},{1,9},{2,10},{3,11},{4,12},{5,13},{6,14},{7,15},{8,0},{9,1},... | collective-permute-start | bytes 3932168 | tf_op jit(solution)/shard_map/ppermute | solution.py:46
  0.7 48.3 %collective-permute-start.2 = (bf16[1024,1024]{1,0:T(8,128)(2,1)}, bf16[1024,1024]{1,0:T(8,128)(2,1)}, u32[]{:S(2)}, u32[]{:S(2)}) collective-permute-start(bf16[1024,1024]{1,0:T(8,128)(2,1)} %tokens.1), channel_id=1, source_target_pairs={{0,1},{1,2},{2,3},{3,0},{4,5},{5,6},{6,7},{7,4},{8,11},{9,8},{10,9... | collective-permute-start | bytes 6291464 | tf_op jit(solution)/shard_map/ppermute | solution.py:30
  3.6 5.1 %collective-permute-start = (s32[2]{0:T(128)S(1)}, s32[2]{0:T(128)S(1)}, u32[]{:S(2)}, u32[]{:S(2)}) collective-permute-start(s32[2]{0:T(128)S(1)} %fusion.1), channel_id=1, source_target_pairs={{0,64},{1,65},{2,66},{3,67},{4,68},{5,69},{6,70},{7,71},{8,72},{9,... | collective-permute-start | bytes 32 | tf_op jit(solution)/shard_map/ppermute | solution.py:50
  8.8 48.5 %collective-permute-start.1 = (bf16[1024,1024]{1,0:T(8,128)(2,1)}, bf16[1024,1024]{1,0:T(8,128)(2,1)}, u32[]{:S(2)}, u32[]{:S(2)}) collective-permute-start(bf16[1024,1024]{1,0:T(8,128)(2,1)} %tokens.1), channel_id=1, source_target_pairs={{0,4},{1,5},{2,6},{3,7},{4,0},{5,1},{6,2},{7,3},{8,12},{9,13},{10,... | collective-permute-start | bytes 6291464 | tf_op jit(solution)/shard_map/ppermute | solution.py:42
  10.3 66.7 %collective-permute-start.11 = (bf16[1024,1024]{1,0:T(8,128)(2,1)}, bf16[1024,1024]{1,0:T(8,128)(2,1)}, u32[]{:S(2)}, u32[]{:S(2)}) collective-permute-start(bf16[1024,1024]{1,0:T(8,128)(2,1)} %tokens.1), channel_id=1, source_target_pairs={{0,3},{1,0},{2,1},{3,2},{4,7},{5,4},{6,5},{7,6},{8,9},{9,10},{10,1... | collective-permute-start | bytes 6291464 | tf_op jit(solution)/shard_map/ppermute | solution.py:30
  12.5 5.1 %collective-permute-start.3 = (s32[4]{0:T(128)S(1)}, s32[4]{0:T(128)S(1)}, u32[]{:S(2)}, u32[]{:S(2)}) collective-permute-start(s32[4]{0:T(128)S(1)} %pad_add_fusion.1), channel_id=1, source_target_pairs={{0,32},{1,33},{2,34},{3,35},{4,36},{5,37},{6,38},{7,39},{8,40},{9,... | collective-permute-start | bytes 56 | tf_op jit(solution)/shard_map/ppermute | solution.py:36
  17.6 4.8 %collective-permute-start.4 = (s32[8]{0:T(128)S(1)}, s32[8]{0:T(128)S(1)}, u32[]{:S(2)}, u32[]{:S(2)}) collective-permute-start(s32[8]{0:T(128)S(1)} %pad_add_fusion.2), channel_id=1, source_target_pairs={{0,16},{1,17},{2,18},{3,19},{4,20},{5,21},{6,22},{7,23},{8,56},{9,... | collective-permute-start | bytes 104 | tf_op jit(solution)/shard_map/ppermute | solution.py:36
  25.6 16.3 %collective-permute-start.7 = (bf16[4,1024,128]{2,1,0:T(8,128)(2,1)}, bf16[4,1024,128]{2,1,0:T(8,128)(2,1)}, u32[]{:S(2)}, u32[]{:S(2)}) collective-permute-start(bf16[4,1024,128]{2,1,0:T(8,128)(2,1)} %shard_map.104), channel_id=1, source_target_pairs={{0,16},{1,17},{2,18},{3,19},{4,20},{5,21},{6,22},{7,23},{8,56},{9,... | collective-permute-start | bytes 3145736 | tf_op jit(solution)/shard_map/ppermute | solution.py:36
  27.5 7.9 %collective-permute-start.6 = (bf16[5,64,1152]{2,1,0:T(8,128)(2,1)}, bf16[5,64,1152]{2,1,0:T(8,128)(2,1)}, u32[]{:S(2)}, u32[]{:S(2)}) collective-permute-start(bf16[5,64,1152]{2,1,0:T(8,128)(2,1)} %constant_dynamic-update-slice_fusion.own), channel_id=1, source_target_pairs={{0,8},{1,9},{2,10},{3,11},{4,12},{5,13},{6,14},{7,15},{8,0},{9,1},... | collective-permute-start | bytes 2211848 | tf_op jit(solution)/shard_map/ppermute | solution.py:46
  35.4 9.0 %copy-start.9 = (f32[1024,1024]{1,0:T(8,128)}, f32[1024,1024]{1,0:T(8,128)S(1)}, u32[]{:S(2)}) copy-start(f32[1024,1024]{1,0:T(8,128)S(1)} %get-tuple-element.53.refs_3_) | copy-start | bytes 12582916
  35.4 9.0 %copy-start.17 = (f32[1024,128]{1,0:T(8,128)}, f32[1024,128]{1,0:T(8,128)S(1)}, u32[]{:S(2)}) copy-start(f32[1024,128]{1,0:T(8,128)S(1)} %get-tuple-element.45.refs_4_) | copy-start | bytes 1572868
  37.6 24.2 %collective-permute-start.10 = (bf16[4,1024,128]{2,1,0:T(8,128)(2,1)}, bf16[4,1024,128]{2,1,0:T(8,128)(2,1)}, u32[]{:S(2)}, u32[]{:S(2)}) collective-permute-start(bf16[4,1024,128]{2,1,0:T(8,128)(2,1)} %shard_map.106), channel_id=1, source_target_pairs={{0,48},{1,49},{2,50},{3,51},{4,52},{5,53},{6,54},{7,55},{8,24},{9,... | collective-permute-start | bytes 3145736 | tf_op jit(solution)/shard_map/ppermute | solution.py:36
  44.4 26.8 %collective-permute-start.9 = (bf16[4,1024,128]{2,1,0:T(8,128)(2,1)}, bf16[4,1024,128]{2,1,0:T(8,128)(2,1)}, u32[]{:S(2)}, u32[]{:S(2)}) collective-permute-start(bf16[4,1024,128]{2,1,0:T(8,128)(2,1)} %shard_map.107), channel_id=1, source_target_pairs={{0,16},{1,17},{2,18},{3,19},{4,20},{5,21},{6,22},{7,23},{8,56},{9,... | collective-permute-start | bytes 3145736 | tf_op jit(solution)/shard_map/ppermute | solution.py:36
  50.9 52.8 %collective-permute-start.15 = (bf16[1024,1024]{1,0:T(8,128)(2,1)}, bf16[1024,1024]{1,0:T(8,128)(2,1)}, u32[]{:S(2)}, u32[]{:S(2)}) collective-permute-start(bf16[1024,1024]{1,0:T(8,128)(2,1)} %collective-permute-done.2.refs_0_), channel_id=1, source_target_pairs={{0,1},{1,2},{2,3},{3,0},{4,5},{5,6},{6,7},{7,4},{8,11},{9,8},{10,9... | collective-permute-start | bytes 6291464 | tf_op jit(solution)/shard_map/ppermute | solution.py:30
  57.3 46.4 %collective-permute-start.8 = (bf16[1024,1024]{1,0:T(8,128)(2,1)}, bf16[1024,1024]{1,0:T(8,128)(2,1)}, u32[]{:S(2)}, u32[]{:S(2)}) collective-permute-start(bf16[1024,1024]{1,0:T(8,128)(2,1)} %collective-permute-done.1.refs_1_), channel_id=1, source_target_pairs={{0,3},{1,0},{2,1},{3,2},{4,7},{5,4},{6,5},{7,6},{8,9},{9,10},{10,1... | collective-permute-start | bytes 6291464 | tf_op jit(solution)/shard_map/ppermute | solution.py:30
  61.8 25.8 %collective-permute-start.12 = (bf16[256,1024]{1,0:T(8,128)(2,1)}, bf16[256,1024]{1,0:T(8,128)(2,1)S(1)}, u32[]{:S(2)}, u32[]{:S(2)}) collective-permute-start(bf16[256,1024]{1,0:T(8,128)(2,1)} %slice.23), channel_id=1, source_target_pairs={{0,4},{1,5},{2,6},{3,7},{4,0},{5,1},{6,2},{7,3},{8,12},{9,13},{10,... | collective-permute-start | bytes 1572872 | tf_op jit(solution)/shard_map/ppermute | solution.py:42
  63.6 7.6 %copy-start.5 = (bf16[5,1024,128]{2,1,0:T(8,128)(2,1)S(1)}, bf16[5,1024,128]{2,1,0:T(8,128)(2,1)}, u32[]{:S(2)}) copy-start(bf16[5,1024,128]{2,1,0:T(8,128)(2,1)} %copy-done.3) | copy-start | bytes 3932164
  73.8 16.8 %collective-permute-start.13 = (bf16[2,1024,128]{2,1,0:T(8,128)(2,1)}, bf16[2,1024,128]{2,1,0:T(8,128)(2,1)}, u32[]{:S(2)}, u32[]{:S(2)}) collective-permute-start(bf16[2,1024,128]{2,1,0:T(8,128)(2,1)} %shard_map.111), channel_id=1, source_target_pairs={{0,64},{1,65},{2,66},{3,67},{4,68},{5,69},{6,70},{7,71},{8,72},{9,... | collective-permute-start | bytes 1572872 | tf_op jit(solution)/shard_map/ppermute | solution.py:50
  77.0 12.3 %copy-start.23 = (s32[1,8]{1,0:T(1,128)S(1)}, s32[1,8]{1,0:T(1,128)}, u32[]{:S(2)}) copy-start(s32[1,8]{1,0:T(1,128)} %param.17) | copy-start | bytes 100
  88.4 10.6 %collective-permute-start.19 = (bf16[256,1024]{1,0:T(8,128)(2,1)}, bf16[256,1024]{1,0:T(8,128)(2,1)}, u32[]{:S(2)}, u32[]{:S(2)}) collective-permute-start(bf16[256,1024]{1,0:T(8,128)(2,1)} %get-tuple-element.61), channel_id=1, source_target_pairs={{0,4},{1,5},{2,6},{3,7},{4,0},{5,1},{6,2},{7,3},{8,12},{9,13},{10,... | collective-permute-start | bytes 1572872 | tf_op jit(solution)/shard_map/ppermute | solution.py:42
  89.2 12.0 %collective-permute-start.14 = (bf16[4,64,1152]{2,1,0:T(8,128)(2,1)}, bf16[4,64,1152]{2,1,0:T(8,128)(2,1)}, u32[]{:S(2)}, u32[]{:S(2)}) collective-permute-start(bf16[4,64,1152]{2,1,0:T(8,128)(2,1)} %shard_map.108), channel_id=1, source_target_pairs={{0,16},{1,17},{2,18},{3,19},{4,20},{5,21},{6,22},{7,23},{8,56},{9,... | collective-permute-start | bytes 1769480 | tf_op jit(solution)/shard_map/ppermute | solution.py:36
  96.5 13.8 %collective-permute-start.17 = (bf16[1024,128]{1,0:T(8,128)(2,1)}, bf16[1024,128]{1,0:T(8,128)(2,1)}, u32[]{:S(2)}, u32[]{:S(2)}) collective-permute-start(bf16[1024,128]{1,0:T(8,128)(2,1)} %get-tuple-element.63), channel_id=1, source_target_pairs={{0,4},{1,5},{2,6},{3,7},{4,0},{5,1},{6,2},{7,3},{8,12},{9,13},{10,... | collective-permute-start | bytes 786440 | tf_op jit(solution)/shard_map/ppermute | solution.py:42
  99.0 27.3 %collective-permute-start.20 = (bf16[512,1024]{1,0:T(8,128)(2,1)}, bf16[512,1024]{1,0:T(8,128)(2,1)}, u32[]{:S(2)}, u32[]{:S(2)}) collective-permute-start(bf16[512,1024]{1,0:T(8,128)(2,1)} %get-tuple-element.69), channel_id=1, source_target_pairs={{0,4},{1,5},{2,6},{3,7},{4,0},{5,1},{6,2},{7,3},{8,12},{9,13},{10,... | collective-permute-start | bytes 3145736 | tf_op jit(solution)/shard_map/ppermute | solution.py:42
  99.0 11.3 %copy-start.13 = (f32[1024,128]{1,0:T(8,128)S(1)}, f32[1024,128]{1,0:T(8,128)}, u32[]{:S(2)}) copy-start(f32[1024,128]{1,0:T(8,128)} %copy-done.12) | copy-start | bytes 1572868
  103.6 37.0 %collective-permute-start.16 = (bf16[1024,1024]{1,0:T(8,128)(2,1)}, bf16[1024,1024]{1,0:T(8,128)(2,1)}, u32[]{:S(2)}, u32[]{:S(2)}) collective-permute-start(bf16[1024,1024]{1,0:T(8,128)(2,1)} %collective-permute-done.8.refs_3_), channel_id=1, source_target_pairs={{0,3},{1,0},{2,1},{3,2},{4,7},{5,4},{6,5},{7,6},{8,9},{9,10},{10,1... | collective-permute-start | bytes 6291464 | tf_op jit(solution)/shard_map/ppermute | solution.py:30
  105.0 21.2 %collective-permute-start.23 = (bf16[4,64,1152]{2,1,0:T(8,128)(2,1)}, bf16[4,64,1152]{2,1,0:T(8,128)(2,1)S(1)}, u32[]{:S(2)}, u32[]{:S(2)}) collective-permute-start(bf16[4,64,1152]{2,1,0:T(8,128)(2,1)} %shard_map.109), channel_id=1, source_target_pairs={{0,48},{1,49},{2,50},{3,51},{4,52},{5,53},{6,54},{7,55},{8,24},{9,... | collective-permute-start | bytes 1769480 | tf_op jit(solution)/shard_map/ppermute | solution.py:36
  110.3 16.0 %collective-permute-start.22 = (bf16[4,64,1152]{2,1,0:T(8,128)(2,1)}, bf16[4,64,1152]{2,1,0:T(8,128)(2,1)S(1)}, u32[]{:S(2)}, u32[]{:S(2)}) collective-permute-start(bf16[4,64,1152]{2,1,0:T(8,128)(2,1)} %shard_map.115), channel_id=1, source_target_pairs={{0,16},{1,17},{2,18},{3,19},{4,20},{5,21},{6,22},{7,23},{8,56},{9,... | collective-permute-start | bytes 1769480 | tf_op jit(solution)/shard_map/ppermute | solution.py:36
  112.0 10.7 %collective-permute-start.18 = (bf16[1024,128]{1,0:T(8,128)(2,1)}, bf16[1024,128]{1,0:T(8,128)(2,1)S(1)}, u32[]{:S(2)}, u32[]{:S(2)}) collective-permute-start(bf16[1024,128]{1,0:T(8,128)(2,1)} %fusion), channel_id=1, source_target_pairs={{0,1},{1,2},{2,3},{3,0},{4,5},{5,6},{6,7},{7,4},{8,11},{9,8},{10,9... | collective-permute-start | bytes 786440 | tf_op jit(solution)/shard_map/ppermute | solution.py:30
  113.1 9.5 %copy-start.14 = (f32[1024,128]{1,0:T(8,128)S(1)}, f32[1024,128]{1,0:T(8,128)}, u32[]{:S(2)}) copy-start(f32[1024,128]{1,0:T(8,128)} %copy-done.12) | copy-start | bytes 1572868
  120.5 8.5 %copy-start.16 = (bf16[256,1024]{1,0:T(8,128)(2,1)S(1)}, bf16[256,1024]{1,0:T(8,128)(2,1)}, u32[]{:S(2)}) copy-start(bf16[256,1024]{1,0:T(8,128)(2,1)} %copy-done.15) | copy-start | bytes 1572868
  123.7 16.9 %collective-permute-start.21 = (bf16[1024,128]{1,0:T(8,128)(2,1)S(1)}, bf16[1024,128]{1,0:T(8,128)(2,1)S(1)}, u32[]{:S(2)}, u32[]{:S(2)}) collective-permute-start(bf16[1024,128]{1,0:T(8,128)(2,1)S(1)} %get-tuple-element.73), channel_id=1, source_target_pairs={{0,2},{1,3},{2,0},{3,1},{4,6},{5,7},{6,4},{7,5},{8,10},{9,11},{10,... | collective-permute-start | bytes 786440 | tf_op jit(solution)/shard_map/ppermute | solution.py:30
  127.7 11.2 %collective-permute-start.24 = (bf16[2,64,1152]{2,1,0:T(8,128)(2,1)S(1)}, bf16[2,64,1152]{2,1,0:T(8,128)(2,1)S(1)}, u32[]{:S(2)}, u32[]{:S(2)}) collective-permute-start(bf16[2,64,1152]{2,1,0:T(8,128)(2,1)S(1)} %shard_map.118), channel_id=1, source_target_pairs={{0,64},{1,65},{2,66},{3,67},{4,68},{5,69},{6,70},{7,71},{8,72},{9,... | collective-permute-start | bytes 884744 | tf_op jit(solution)/shard_map/ppermute | solution.py:50
  (17 other events, 46.7 us)
